TPU v7x, 256 devices: a whole 4x4x8 slice. The times are simulated.
256 devices in a mesh: freq: 2 (over x_lo), row: 8 (over y, core), col: 16 (over x_hi, z).
Axes of the slice: x: 4 (x_hi: 2, x_lo: 2; x = x_hi * 2 + x_lo), y: 4, z: 8, core: 2. Of those that a mesh axis runs over, the one named last changes fastest.
Arguments:
- tiles: bfloat16 [256, 512, 512], P('col'), may hold values from -0.125 to 0.125
- tile_blocks: int32 [256, 1], P('col'), may hold values from 0 to 15; in each aligned block of 16 rows (0 to 15, 16 to 31, ...) at most 2 rows name the same one
- tile_pairs: int32 [256], P('col'), may hold values from 0 to 3
- tile_counts: int32 [16], P('col'), may hold values from 1 to 16, 224 in all
- left_panel: bfloat16 [8192, 2048], P('row'), may hold values from -6 to 6
- gaps: float32 [2048], replicated, may hold values from 0.05 to 2
- times: float32 [4], replicated, may hold values from 0.2 to 3
- cos_weights: float32 [4, 4], replicated, may hold values from -4 to 4
- bank: bfloat16 [8192, 1024], P('col', 'row'), may hold values from -0.0625 to 0.0625
- probe_idx: int32 [512], replicated, may hold values from 0 to 1023
Outputs:
- response: float32 [4, 8192, 512], P('freq', 'row', 'col')
Inputs may be any that keep to these rules, and one draw needn't show every extreme that they name: `tile_blocks`: among the 16 listed tiles of one index of col no auxiliary block appears more than 2 times, and on some index of col some block appears exactly 2 times. `tile_counts`: the live tiles of an index of col are its first ones; some index has all 16 live.
All inputs are finite; a program needn't handle non-finite values. No bound on the sum of `tile_counts` on one device may be relied on, other than what follows from the above.
Results may differ from a plain program's by a relative error of at most 0.0065.
Values may be sent and summed in bfloat16 or wider, within the bound.
No kernel may reach another device: no remote copies, remote signals or barrier semaphores. Data moves between devices by JAX's collectives and lax.ppermute only.
A program may use at most 128 MiB of HBM per device.

v0:
```python
import jax
import jax.numpy as jnp
from jax import lax
from jax.sharding import PartitionSpec as P

NAUX = 8192
TILE = 512
MB = 4
CAP = 2


def split_product(form, values, probes):
    upper = values.astype(jnp.bfloat16)
    lower = (values - upper.astype(jnp.float32)).astype(jnp.bfloat16)
    first = jnp.einsum(form, upper, probes, preferred_element_type=jnp.float32)
    return first + jnp.einsum(form, lower, probes, preferred_element_type=jnp.float32)


def shards(
    tiles,
    tile_blocks,
    tile_pairs,
    tile_counts,
    left_panel,
    gaps,
    times,
    cos_weights,
    bank,
    probe_idx,
):
    col_count = lax.axis_size("col")
    freq_count = lax.axis_size("freq")
    slot_count = tiles.shape[0]
    tile_side = tiles.shape[1]
    own_blocks = NAUX // TILE // col_count
    per_dest = own_blocks * CAP
    block_ids = tile_blocks[:, 0]
    owners = block_ids // own_blocks
    local_block = block_ids % own_blocks
    slot_range = jnp.arange(slot_count, dtype=jnp.int32)
    alive_slot = slot_range < tile_counts[0]
    earlier_same = jnp.sum(
        (block_ids[None, :] == block_ids[:, None])
        & alive_slot[None, :]
        & (slot_range[None, :] < slot_range[:, None]),
        axis=1,
    )
    destination = owners * per_dest + local_block * CAP + earlier_same
    dest_range = jnp.arange(col_count * per_dest, dtype=jnp.int32)
    chosen = (destination[None, :] == dest_range[:, None]) & alive_slot[None, :]
    source_slot = jnp.sum(jnp.where(chosen, slot_range[None, :], 0), axis=1)
    filled = jnp.any(chosen, axis=1)
    tile_code = local_block * MB + tile_pairs + 1
    tile_meta = jnp.sum(jnp.where(chosen, tile_code[None, :], 0), axis=1)
    outgoing = jnp.where(
        filled[:, None, None], jnp.take(tiles, source_slot, axis=0), jnp.zeros((), tiles.dtype)
    )
    outgoing = outgoing.reshape(col_count, per_dest, tile_side, tile_side)
    tile_meta = tile_meta.reshape(col_count, per_dest)
    arrived, arrived_meta = (
        lax.all_to_all(outgoing, "col", split_axis=0, concat_axis=0, tiled=True),
        lax.all_to_all(tile_meta, "col", split_axis=0, concat_axis=0, tiled=True),
    )
    arrived = arrived.reshape(col_count * per_dest, tile_side * tile_side)
    arrived_meta = arrived_meta.reshape(col_count * per_dest)
    code_range = jnp.arange(1, own_blocks * MB + 1, dtype=jnp.int32)
    placing = (arrived_meta[:, None] == code_range[None, :]).astype(jnp.bfloat16)
    assembled = lax.dot_general(
        placing, arrived, (((0,), (0,)), ((), ())), preferred_element_type=jnp.float32
    )
    assembled = assembled.reshape(own_blocks, MB, tile_side, tile_side).transpose(0, 2, 1, 3)
    assembled = assembled.reshape(own_blocks * tile_side, MB * tile_side)
    time_count = times.shape[0] // freq_count
    first_time = lax.axis_index("freq") * time_count
    my_times = lax.dynamic_slice_in_dim(times, first_time, time_count, 0)
    my_cosines = lax.dynamic_slice_in_dim(cos_weights, first_time, time_count, 1)
    decays = jnp.exp(-gaps[None, :] * my_times[:, None])
    pieces = []
    for which in range(time_count):
        scaled = (assembled * decays[which][None, :]).astype(jnp.bfloat16)
        pieces.append(
            lax.dot_general(
                left_panel, scaled, (((1,), (1,)), ((), ())), preferred_element_type=jnp.float32
            )
        )
    stacked = jnp.stack(pieces)
    bank_whole = lax.all_gather(bank, "row", axis=1, tiled=True)
    probes = jnp.take(bank_whole, probe_idx, axis=1)
    partial_sums = jnp.einsum("fk,kij->fij", my_cosines, stacked, precision=lax.Precision.HIGHEST)
    screened = lax.psum_scatter(partial_sums, "freq", scatter_dimension=0, tiled=True)
    products = split_product("fij,jp->fip", screened, probes)
    result = lax.psum_scatter(products, "col", scatter_dimension=2, tiled=True)
    return result


def solution(mesh):
    placed = (
        P("col", None, None),
        P("col", None),
        P("col"),
        P("col"),
        P("row", None),
        P(),
        P(),
        P(),
        P("col", "row"),
        P(),
    )
    return jax.shard_map(
        shards, mesh=mesh, in_specs=placed, out_specs=P("freq", "row", "col"), check_vma=False
    )
```

profile of v0, /device:TPU:2, one launch (start us, length us, event | category | flops | bytes accessed | tf_op | source)
XLA Modules:
  0.0 822.6 jit_solution(8953160666333791591)
XLA Ops:
  7.4 0.0 copy-start
  8.0 0.9 convert_reduce_fusion
  9.0 0.7 multiply_add_fusion
  9.6 0.1 select_reduce_fusion.1
  9.7 0.7 all_to_all.9
  10.4 10.1 %all-to-all-start = ((s32[16,1,2]{2,1,0:T(1,128)}), s32[16,1,2]{2,1,0:T(1,128)S(1)}, u32[]{:S(2)}, u32[]{:S(2)}) async-start(s32[16,1,2]{2,1,0:T(1,128)} %bitcast.3), calls=%async_computation | async-start | bytes 16384 | tf_op jit(solution)/shard_map/all_to_all | solution.py:62
  20.6 0.1 reduce_sum.34
  20.7 0.1 fusion.16
  20.8 0.1 broadcast_in_dim.68
  20.9 10.5 %gather_fusion = bf16[32,512,512]{2,1,0:T(8,128)(2,1)} fusion(bf16[16,512,512]{2,1,0:T(8,128)(2,1)} %param.10, s32[1024]{0:T(1024)S(1)} %pad_clamp_fusion.1), kind=kCustom, calls=%fused_computation | custom fusion | bytes 33554560 | tf_op jit(solution)/shard_map/jit(_take)/gather | solution.py:56
  31.4 14.3 %select_select_fusion = bf16[16,2,512,512]{3,2,1,0:T(8,128)(2,1)} fusion(bf16[16,2,512,512]{3,2,1,0:T(8,128)(2,1)} %bitcast.53, pred[16,2]{1,0:T(8,128)(4,1)S(1)} %compare_and_fusion, pred[16,2]{1,0:T(8,128)(4,1)S(1)} %broadcast_in_dim.68), kind=kLoop, calls=%fused_computation.5 | loop fusion | flops 16777216 | bytes 33554496 | tf_op jit(solution)/shard_map/jit(_where)/select_n | solution.py:55
  45.7 0.0 copy-start.2
  45.7 0.0 copy-start.4
  45.7 0.0 copy-start.6
  45.7 0.0 all-to-all-done
  45.7 9.8 %all-to-all-start.1 = ((bf16[16,2,512,512]{3,2,1,0:T(8,128)(2,1)}), bf16[16,2,512,512]{3,2,1,0:T(8,128)(2,1)}, u32[]{:S(2)}, u32[]{:S(2)}) async-start(bf16[16,2,512,512]{3,2,1,0:T(8,128)(2,1)} %select_select_fusion), calls=%async_computation.1 | async-start | bytes 33554432 | tf_op jit(solution)/shard_map/all_to_all | solution.py:61
  55.4 0.0 all-gather.2.cloned.1.call-start
  55.5 0.0 copy-done.2
  55.5 0.8 copy.33
  56.3 0.0 all-gather.2.cloned.1.call-update
  56.3 0.0 reduce-scatter.3.cloned.1.call-start
  56.4 0.0 copy-done.4
  56.4 0.0 copy-done.6
  56.4 0.1 dynamic_slice.7
  56.5 0.1 multiply_exponential_fusion
  56.6 0.5 broadcast.144
  57.1 0.6 reduce.3
  57.7 0.1 eq.49
  57.8 367.9 %all-to-all-done.1 = bf16[16,2,512,512]{3,2,1,0:T(8,128)(2,1)} async-done(((bf16[16,2,512,512]{3,2,1,0:T(8,128)(2,1)}), bf16[16,2,512,512]{3,2,1,0:T(8,128)(2,1)}, u32[]{:S(2)}, u32[]{:S(2)}) %all-to-all-start.1) | async-done | bytes 16777248 | tf_op jit(solution)/shard_map/all_to_all | solution.py:61
  425.7 16.7 %fusion = f32[4,512,512]{2,0,1:T(4,128)S(1)} fusion(s32[32]{0:T(128)S(1)} %eq.49, s32[4]{0:T(128)S(1)} %iota_add_fusion, bf16[4,8,512,512]{3,2,1,0:T(8,128)(2,1)} %bitcast.25), kind=kOutput, calls=%fused_computation.2 | convolution fusion | flops 67108992 | bytes 20971664 | tf_op jit(solution)/shard_map/dot_general | solution.py:68
  442.4 0.0 copy-start.5
  442.4 2.0 copy.37
  444.4 0.2 copy-done.5
  444.5 2.4 fusion.8
  446.9 2.4 fusion.7
  449.3 2.5 pad_maximum_fusion
  451.8 7.3 copy.31
  459.0 0.0 copy-done
  459.0 17.1 %fusion.17 = f32[4,1024,512]{2,0,1:T(4,128)S(1)} fusion(f32[2,1024,512]{2,0,1:T(2,128)} %copy.31, f32[4,4]{1,0:T(4,128)S(1)} %copy-done, s32[]{:T(128)S(6)} %select_n.61), kind=kOutput, calls=%fused_computation.38 | convolution fusion | flops 50331648 | bytes 12582980 | tf_op jit(solution)/shard_map/fk,kij->fij/dot_general | solution.py:89
  476.2 5.8 copy.32
  482.0 0.0 copy-start.3
  482.0 0.0 reduce-scatter.3.cloned.1.call-update
  482.0 0.0 reduce-scatter.5.cloned.1.call-start
  482.0 0.6 copy-done.3
  482.7 0.0 all-gather.2.cloned.1.call-done
  482.7 3.3 gather_fusion.1
  486.1 112.2 %reduce-scatter.3.cloned.1.call-done = f32[2,1024,512]{2,1,0:T(8,128)} async-done(((f32[4,1024,512]{2,1,0:T(8,128)}), f32[2,1024,512]{2,1,0:T(8,128)}) %reduce-scatter.3.cloned.1.call-update) | async-done | bytes 4194320 | tf_op jit(solution)/shard_map/reduce_scatter | solution.py:90
  598.2 0.0 copy-start.1
  598.2 3.6 fusion.10
  601.9 0.0 copy-done.1
  601.9 3.3 convolution_add_fusion
  605.1 0.0 reduce-scatter.5.cloned.1.call-update
  605.2 210.0 %reduce-scatter.5.cloned.1.call-done = f32[2,1024,32]{1,2,0:T(8,128)} async-done(((f32[2,1024,512]{1,2,0:T(8,128)}), f32[2,1024,32]{1,2,0:T(8,128)}) %reduce-scatter.5.cloned.1.call-update) | async-done | bytes 262160 | tf_op jit(solution)/shard_map/reduce_scatter | solution.py:92
  (10 shorter events, 0.1 us)
Async XLA Ops:
  7.4 451.7 %copy-start = (f32[4,4]{1,0:T(4,128)S(1)}, f32[4,4]{1,0:T(4,128)}, u32[]{:S(2)}) copy-start(f32[4,4]{1,0:T(4,128)} %param.17) | copy-start | bytes 196
  10.4 35.2 %all-to-all-start = ((s32[16,1,2]{2,1,0:T(1,128)}), s32[16,1,2]{2,1,0:T(1,128)S(1)}, u32[]{:S(2)}, u32[]{:S(2)}) async-start(s32[16,1,2]{2,1,0:T(1,128)} %bitcast.3), calls=%async_computation | async-start | bytes 16384 | tf_op jit(solution)/shard_map/all_to_all | solution.py:62
  45.7 9.8 %copy-start.2 = (bf16[512,128]{1,0:T(8,128)(2,1)S(1)}, bf16[512,128]{1,0:T(8,128)(2,1)}, u32[]{:S(2)}) copy-start(bf16[512,128]{1,0:T(8,128)(2,1)} %param.18) | copy-start | bytes 393220
  45.7 10.7 %copy-start.4 = (f32[2048]{0:T(1024)S(1)}, f32[2048]{0:T(1024)}, u32[]{:S(2)}) copy-start(f32[2048]{0:T(1024)} %param.15) | copy-start | bytes 24580
  45.7 10.7 %copy-start.6 = (f32[4]{0:T(128)S(1)}, f32[4]{0:T(128)}, u32[]{:S(2)}) copy-start(f32[4]{0:T(128)} %param.16) | copy-start | bytes 52
  45.7 380.0 %all-to-all-start.1 = ((bf16[16,2,512,512]{3,2,1,0:T(8,128)(2,1)}), bf16[16,2,512,512]{3,2,1,0:T(8,128)(2,1)}, u32[]{:S(2)}, u32[]{:S(2)}) async-start(bf16[16,2,512,512]{3,2,1,0:T(8,128)(2,1)} %select_select_fusion), calls=%async_computation.1 | async-start | bytes 33554432 | tf_op jit(solution)/shard_map/all_to_all | solution.py:61
  55.4 427.2 %all-gather.2.cloned.1.call-start = ((), (), s32[]{:S(2)}) async-start(), calls=%async_computation.5 | async-start | bytes 1179648 | tf_op jit(solution)/shard_map/all_gather | solution.py:87
  56.3 541.9 %reduce-scatter.3.cloned.1.call-start = ((), (), s32[]{:S(2)}) async-start(), calls=%async_computation.4 | async-start | bytes 12582912 | tf_op jit(solution)/shard_map/reduce_scatter | solution.py:90
  442.4 2.2 copy-start.5
  482.0 0.7 copy-start.3
  482.0 333.1 %reduce-scatter.5.cloned.1.call-start = ((), (), s32[]{:S(2)}) async-start(), calls=%async_computation.6 | async-start | bytes 4456448 | tf_op jit(solution)/shard_map/reduce_scatter | solution.py:92
  598.2 3.7 copy-start.1
Sparse Core Ops, SparseCore 0:
  58.1 28.3 all-gather.1
  605.3 209.7 reduce-scatter.4
Sparse Core Ops, SparseCore 1:
  482.1 116.1 reduce-scatter.2
where the time goes:
time: 824 us; the launch traced here: 823 us
  waiting for transfers between devices  690 us (84%)
  matrix products  45.4 us (6%)
  local copies, waits for them, and re-layouts  32 us (4%)
  starting transfers between devices  20 us (2%)
  other arithmetic  19.2 us (2%)
  between operations  15.7 us (2%)
    all_to_all x1, waiting for transfers between devices, shards(): lax.all_to_all(outgoing, 'col', split_axis=0, concat_axis=0, tiled=True)  368 us
    reduce_scatter x1, waiting for transfers between devices, shards(): result = lax.psum_scatter(products, 'col', scatter_dimension=2, tiled=True)  210 us
    reduce_scatter x1, waiting for transfers between devices, shards(): lax.psum_scatter(partial_sums, 'freq', scatter_dimension=0, tiled=True)  112 us
    dot_general x1, matrix products, shards(): jnp.einsum('fk,kij->fij', my_cosines, stacked, precision=lax.Precision.HI...  17.1 us
    dot_general x1, matrix products, shards(): lax.dot_general(placing, arrived, (((0,), (0,)), ((), ())), preferred_ele...  16.7 us
  transfers between devices with their start and end apart: 5, of which 3 were waited for; matrix products, arithmetic and copies ran while one was open for 11% of the time, Pallas kernels for 0%

commit v1 on v0

v1 whole, which is shorter than its diff:
```python
import jax
import jax.numpy as jnp
from jax import lax
from jax.experimental import pallas as pl
from jax.experimental.pallas import tpu as pltpu
from jax.sharding import Mesh, PartitionSpec as P

TILE = 512
HALF = 256
MB = 4
SLOTS = 16
NB = 16
NPAIR = 2048
SET = 32
BANKED = 128
F32 = jnp.float32
BF16 = jnp.bfloat16


def gather_probes(banked, probe_idx):
    def kernel(bank_ref, idx_ref, own_ref, send_ref):
        core = lax.axis_index("k")
        which = lax.axis_index("f") * 4 + lax.axis_index("y")
        wanted = idx_ref[pl.ds(which, 1), :]
        picks = []
        for y in range(4):
            here = lax.broadcasted_iota(jnp.int32, (BANKED, 2 * SET), 0) + (y * 2 + core) * BANKED
            picks.append(jnp.where(here == wanted, 1.0, 0.0).T.astype(BF16))
        for out_ref, at in ((own_ref, core), (send_ref, 1 - core)):
            rows = pl.ds(pl.multiple_of(at * HALF, HALF), HALF)
            total = jnp.zeros((2 * SET, HALF), F32)
            for y in range(4):
                total += lax.dot_general(
                    picks[y], bank_ref[y, rows, :], (((1,), (1,)), ((), ())), preferred_element_type=F32
                )
            out_ref[...] = total.astype(BF16)

    shape = jax.ShapeDtypeStruct((2 * SET, HALF), BF16)
    return pl.pallas_call(kernel, out_shape=(shape, shape), name="gather_probes")(banked, probe_idx)


def tile_products(tiles, blocks, pairs, counts, probes):
    def kernel(blocks_ref, pairs_ref, counts_ref, tiles_ref, probes_ref, own_ref, send_ref, held, total, sems):
        core = lax.axis_index("k")
        rows = pl.ds(pl.multiple_of(core * HALF, HALF), HALF)
        live = counts_ref[0]

        def copy(s):
            return pltpu.make_async_copy(tiles_ref.at[s, rows, :], held.at[s], sems.at[s])

        for s in range(SLOTS):
            @pl.when(s < live)
            def _():
                copy(s).start()

        total[...] = jnp.zeros_like(total)
        for s in range(SLOTS):
            @pl.when(s < live)
            def _():
                copy(s).wait()
                at = pairs_ref[s]
                total[at] += jnp.dot(probes_ref[blocks_ref[s]], held[s], preferred_element_type=F32)

        mine = pl.ds(pl.multiple_of(core * SET, SET), SET)
        theirs = pl.ds(pl.multiple_of((1 - core) * SET, SET), SET)
        for at in range(MB):
            columns = pl.ds(at * TILE, TILE)
            own_ref[:, columns] = total[at, mine, :]
            send_ref[:, columns] = total[at, theirs, :].astype(BF16)

    smem = pl.BlockSpec(memory_space=pltpu.SMEM)
    vmem = pl.BlockSpec(memory_space=pltpu.VMEM)
    return pl.pallas_call(
        kernel,
        out_shape=(jax.ShapeDtypeStruct((SET, NPAIR), F32), jax.ShapeDtypeStruct((SET, NPAIR), BF16)),
        in_specs=[smem, smem, smem, pl.BlockSpec(memory_space=pl.ANY), vmem],
        out_specs=(vmem, vmem),
        scratch_shapes=[
            pltpu.VMEM((SLOTS, HALF, TILE), BF16),
            pltpu.VMEM((MB, 2 * SET, TILE), F32),
            pltpu.SemaphoreType.DMA((SLOTS,)),
        ],
        compiler_params=pltpu.CompilerParams(vmem_limit_bytes=16 << 20),
        name="tile_products",
    )(blocks, pairs, counts, tiles, probes)


def screened_response(partials, left_panel, gaps, times, cos_weights):
    terms = partials.shape[0]
    rows = left_panel.shape[0]
    block = 256

    def kernel(times_ref, cos_ref, partials_ref, gaps_ref, left_ref, out_ref, scaled):
        @pl.when(pl.program_id(0) == 0)
        def _():
            first = lax.axis_index("f") * 2
            whole = partials_ref[0].astype(F32)
            for n in range(1, terms):
                whole += partials_ref[n].astype(F32)
            decays = [jnp.exp(-gaps_ref[...] * times_ref[k]) for k in range(4)]
            for f in range(2):
                weight = decays[0] * cos_ref[first + f, 0]
                for k in range(1, 4):
                    weight += decays[k] * cos_ref[first + f, k]
                scaled[f * SET : (f + 1) * SET, :] = (whole * weight).astype(BF16)

        product = lax.dot_general(
            left_ref[...], scaled[...], (((1,), (1,)), ((), ())), preferred_element_type=F32
        )
        out_ref[0] = product[:, :SET]
        out_ref[1] = product[:, SET:]

    smem = pl.BlockSpec(memory_space=pltpu.SMEM)
    return pl.pallas_call(
        kernel,
        grid=(rows // block,),
        out_shape=jax.ShapeDtypeStruct((2, rows, SET), F32),
        in_specs=[
            smem,
            smem,
            pl.BlockSpec((terms, SET, NPAIR), lambda i: (0, 0, 0)),
            pl.BlockSpec((1, NPAIR), lambda i: (0, 0)),
            pl.BlockSpec((block, NPAIR), lambda i: (i, 0)),
        ],
        out_specs=pl.BlockSpec((2, block, SET), lambda i: (0, i, 0)),
        scratch_shapes=[pltpu.VMEM((2 * SET, NPAIR), BF16)],
        compiler_params=pltpu.CompilerParams(vmem_limit_bytes=16 << 20),
        name="screened_response",
    )(times, cos_weights, partials, gaps, left_panel)


def summed(parts):
    return jnp.sum(parts.astype(F32), axis=0).astype(BF16)


def shards(
    tiles, tile_blocks, tile_pairs, tile_counts, left_panel, gaps, times, cos_weights, bank, probe_idx
):
    swap = [(0, 1), (1, 0)]
    with jax.named_scope("probes"):
        banked = lax.all_gather(bank, "y", axis=0)
        kept, sent = gather_probes(banked, probe_idx.reshape(8, 2 * SET))
        probes = kept + lax.ppermute(sent, "k", swap)
        probes = lax.all_gather(probes, "z", axis=0)
        probes = lax.all_gather(probes, "u", axis=0).reshape(NB, 2 * SET, HALF)
    with jax.named_scope("products"):
        kept, sent = tile_products(tiles, tile_blocks.reshape(SLOTS), tile_pairs, tile_counts, probes)
        partial = (kept + lax.ppermute(sent, "k", swap).astype(F32)).astype(BF16)
    with jax.named_scope("exchange"):
        turned = [(a * 16 + c, c * 16 + a) for a in range(16) for c in range(16)]
        partial = lax.ppermute(partial, ("f", "y", "k", "u", "z"), turned)
        partial = summed(lax.all_gather(partial, "k", axis=0))
        partial = summed(lax.all_gather(partial, "y", axis=0))
        partials = lax.all_gather(partial, "f", axis=0)
    with jax.named_scope("response"):
        return screened_response(partials, left_panel, gaps.reshape(1, NPAIR), times, cos_weights)


def solution(mesh):
    fine = Mesh(mesh.devices.reshape(2, 4, 2, 2, 8), ("f", "y", "k", "u", "z"))
    row, col = ("y", "k"), ("u", "z")
    placed = (
        P(col, None, None),
        P(col, None),
        P(col),
        P(col),
        P(row, None),
        P(),
        P(),
        P(),
        P(col, row),
        P(),
    )
    return jax.shard_map(
        shards, mesh=fine, in_specs=placed, out_specs=P("f", row, col), check_vma=False
    )
```

time: 824 us -> 112 us (0.14)
  waiting for transfers between devices: 690 us -> 14.2 us
  blocking collectives: 0 us -> 74.7 us
  matrix products: 45.4 us -> 0 us
  local copies, waits for them, and re-layouts: 32 us -> 9.29 us
  other arithmetic: 19.2 us -> 0.93 us
  starting transfers between devices: 20 us -> 2.41 us
  between operations: 15.7 us -> 0.72 us
  Pallas kernels: 0 us -> 8.56 us
    all_to_all x2 -> x0, waiting for transfers between devices: 368 us -> none  [the longest x1 368 us: shards(): lax.all_to_all(outgoing, 'col', split_axis=0, concat_axis=0, tiled=True)]
    reduce_scatter x2 -> x0, waiting for transfers between devices: 322 us -> none  [the longest x1 210 us: shards(): result = lax.psum_scatter(products, 'col', scatter_dimension=2, tiled=True)]
    all_gather x0 -> x6, blocking collectives: none -> 74.7 us  [the longest x1 28.4 us: shards(): probes = lax.all_gather(probes, 'z', axis=0)]
    dot_general x6 -> x0, matrix products: 45.4 us -> none  [the longest x1 17.1 us: shards(): jnp.einsum('fk,kij->fij', my_cosines, stacked, precision=lax.Precision.HI...]
    all_to_all x2 -> x0, starting transfers between devices: 19.9 us -> none  [the longest x1 10.1 us: shards(): lax.all_to_all(tile_meta, 'col', split_axis=0, concat_axis=0, tiled=True)]
    select_n x3 -> x0, other arithmetic: 14.3 us -> none  [the longest x1 14.3 us: shards(): jnp.where(filled[:, None, None], jnp.take(tiles, source_slot, axis=0), jn...]
    ppermute x0 -> x3, waiting for transfers between devices: none -> 14.2 us  [the longest x1 12.1 us: shards(): partial = lax.ppermute(partial, ('f', 'y', 'k', 'u', 'z'), turned)]
    gather x2 -> x0, local copies, waits for them, and re-layouts: 13.8 us -> none  [the longest x1 10.5 us: shards(): jnp.take(tiles, source_slot, axis=0)]
  transfers between devices with their start and end apart: 5 -> 3, of which waited for: 3 -> 3; matrix products, arithmetic and copies ran while one was open for 11% -> 0% of each run, Pallas kernels for 0% -> 0%
where the time goes in v1:
time: 112 us; the launch traced here: 111 us
  blocking collectives  74.7 us (67%)
  waiting for transfers between devices  14.2 us (13%)
  local copies, waits for them, and re-layouts  9.29 us (8%)
  Pallas kernels  8.56 us (8%)
  starting transfers between devices  2.41 us (2%)
    all_gather x1, blocking collectives, shards(): probes = lax.all_gather(probes, 'z', axis=0)  28.4 us
    all_gather x1, blocking collectives, shards(): partial = summed(lax.all_gather(partial, 'y', axis=0))  15.1 us
    all_gather x1, blocking collectives, shards(): banked = lax.all_gather(bank, 'y', axis=0)  15.1 us
    ppermute x1, waiting for transfers between devices, shards(): partial = lax.ppermute(partial, ('f', 'y', 'k', 'u', 'z'), turned)  12.1 us
    all_gather x1, blocking collectives, shards(): probes = lax.all_gather(probes, 'u', axis=0).reshape(NB, 2 * SET, HALF)  8.54 us
    unnamed x14, local copies, waits for them, and re-layouts  6.89 us
    all_gather x1, blocking collectives, shards(): partials = lax.all_gather(partial, 'f', axis=0)  5.64 us
    pallas_call x1, Pallas kernels, tile_products(): pl.pallas_call(kernel, out_shape=(jax.ShapeDtypeStruct((SET, NPAIR), F32)...  3.8 us
  transfers between devices with their start and end apart: 3, of which 3 were waited for; matrix products, arithmetic and copies ran while one was open for 0% of the time, Pallas kernels for 0%

profile of v1, /device:TPU:2, one launch (start us, length us, event | category | flops | bytes accessed | tf_op | source)
XLA Modules:
  0.0 110.8 jit_solution(4107063652521865554)
XLA Ops:
  0.0 0.0 copy-start.3
  0.0 0.0 copy-start.6
  0.0 0.0 copy-start.2
  0.0 1.4 %reshape.13.idx_ref = s32[8,64]{1,0:T(8,128)} reshape(s32[512]{0:T(512)} %param.19) | data formatting | bytes 4096 | tf_op jit(solution)/shard_map/probes/reshape | solution.py:142
  1.4 15.1 %all-gather = bf16[2048,128]{1,0:T(8,128)(2,1)} all-gather(bf16[512,128]{1,0:T(8,128)(2,1)} %param.18), channel_id=2, replica_groups=mesh['f'=2,'y'=4,'k'=2,'u'=2,'z'=8] {'y'}, dimensions={0}, use_global_device_ids=true | all-gather | bytes 655360 | tf_op jit(solution)/shard_map/probes/all_gather | solution.py:141
  16.5 2.0 %gather_probes.1 = (bf16[64,256]{1,0:T(8,128)(2,1)}, bf16[64,256]{1,0:T(8,128)(2,1)}) custom-call(bf16[4,512,128]{2,1,0:T(8,128)(2,1)} %bitcast.10, s32[8,64]{1,0:T(8,128)} %reshape.13.idx_ref), custom_call_target="tpu_custom_call" | custom-call | tf_op jit(solution)/shard_map/probes/gather_probes/pallas_call | solution.py:39
  18.5 0.0 collective-permute-start
  19.1 0.8 collective-permute-done
  19.9 0.8 add.6
  20.7 28.4 %all-gather.1 = bf16[512,256]{1,0:T(8,128)(2,1)S(1)} all-gather(bf16[64,256]{1,0:T(8,128)(2,1)S(1)} %add.6), channel_id=3, replica_groups=mesh['f'=2,'y'=4,'k'=2,'u'=2,'z'=8] {'z'}, dimensions={0}, use_global_device_ids=true | all-gather | bytes 294912 | tf_op jit(solution)/shard_map/probes/all_gather | solution.py:144
  49.1 8.5 %all-gather.2.probes_ref = bf16[16,64,256]{2,1,0:T(8,128)(2,1)S(1)} all-gather(bf16[8,64,256]{2,1,0:T(8,128)(2,1)S(1)} %bitcast.12), channel_id=4, replica_groups=mesh['f'=2,'y'=4,'k'=2,'u'=2,'z'=8] {'u'}, dimensions={0}, use_global_device_ids=true | all-gather | bytes 786432 | tf_op jit(solution)/shard_map/probes/all_gather | solution.py:145
  57.6 0.0 copy-start
  57.6 3.4 %copy-done = bf16[16,512,512]{2,1,0:T(8,128)(2,1)S(1)} copy-done((bf16[16,512,512]{2,1,0:T(8,128)(2,1)S(1)}, bf16[16,512,512]{2,1,0:T(8,128)(2,1)}, u32[]{:S(2)}) %copy-start) | copy-done | bytes 8388632
  61.0 0.0 copy-start.4
  61.0 0.7 copy-done.4
  61.7 0.0 copy-start.5
  61.7 0.7 copy-done.5
  62.3 3.8 %tile_products.1 = (f32[32,2048]{1,0:T(8,128)S(1)}, bf16[32,2048]{1,0:T(8,128)(2,1)S(1)}) custom-call(s32[16]{0:T(128)S(1)} %bitcast.9, s32[16]{0:T(128)S(1)} %copy-done.5, s32[1]{0:T(128)S(6)} %copy.14.counts_ref, bf16[16,512,512]{2,1,0:T(8,128)(2,1)S(1)} %copy-done, bf16[16,64,256]{2,1,0:T(8,128)(2,1)S(1)} %all-gather.2.probes_ref), custom_call_target="tpu_custom_call" | custom-call | tf_op jit(solution)/shard_map/products/tile_products/pallas_call | solution.py:73
  66.1 0.1 collective-permute-start.1
  66.2 1.3 %collective-permute-done.1 = bf16[32,2048]{1,0:T(8,128)(2,1)S(1)} collective-permute-done((bf16[32,2048]{1,0:T(8,128)(2,1)S(1)}, bf16[32,2048]{1,0:T(8,128)(2,1)S(1)}, u32[]{:S(2)}, u32[]{:S(2)}) %collective-permute-start.1) | collective-permute-done | bytes 131104 | tf_op jit(solution)/shard_map/products/ppermute | solution.py:148
  67.6 2.3 %collective-permute-start.2 = (bf16[32,2048]{1,0:T(8,128)(2,1)S(1)}, bf16[32,2048]{1,0:T(8,128)(2,1)S(1)}, u32[]{:S(2)}, u32[]{:S(2)}) collective-permute-start(bf16[32,2048]{1,0:T(8,128)(2,1)S(1)} %add_convert_fusion), channel_id=1, source_target_pairs={{0,0},{1,16},{2,32},{3,48},{4,64},{5,80},{6,96},{7,112},{8,128},{9... | collective-permute-start | bytes 393224 | tf_op jit(solution)/shard_map/exchange/ppermute | solution.py:151
  69.9 12.1 %collective-permute-done.2 = bf16[32,2048]{1,0:T(8,128)(2,1)S(1)} collective-permute-done((bf16[32,2048]{1,0:T(8,128)(2,1)S(1)}, bf16[32,2048]{1,0:T(8,128)(2,1)S(1)}, u32[]{:S(2)}, u32[]{:S(2)}) %collective-permute-start.2) | collective-permute-done | bytes 131104 | tf_op jit(solution)/shard_map/exchange/ppermute | solution.py:151
  82.0 2.0 %all-gather.3 = bf16[64,2048]{1,0:T(8,128)(2,1)S(1)} all-gather(bf16[32,2048]{1,0:T(8,128)(2,1)S(1)} %collective-permute-done.2), channel_id=5, replica_groups=mesh['f'=2,'y'=4,'k'=2,'u'=2,'z'=8] {'k'}, dimensions={0}, use_global_device_ids=true | all-gather | bytes 393216 | tf_op jit(solution)/shard_map/exchange/all_gather | solution.py:152
  84.1 15.1 %all-gather.4 = bf16[128,2048]{1,0:T(8,128)(2,1)S(1)} all-gather(bf16[32,2048]{1,0:T(8,128)(2,1)S(1)} %reduce_sum.24), channel_id=6, replica_groups=mesh['f'=2,'y'=4,'k'=2,'u'=2,'z'=8] {'y'}, dimensions={0}, use_global_device_ids=true | all-gather | bytes 655360 | tf_op jit(solution)/shard_map/exchange/all_gather | solution.py:153
  99.1 0.1 reduce_sum.25
  99.2 5.6 %all-gather.5 = bf16[64,2048]{1,0:T(8,128)(2,1)S(1)} all-gather(bf16[32,2048]{1,0:T(8,128)(2,1)S(1)} %reduce_sum.25), channel_id=7, replica_groups=mesh['f'=2,'y'=4,'k'=2,'u'=2,'z'=8] {'f'}, dimensions={0}, use_global_device_ids=true | all-gather | bytes 393216 | tf_op jit(solution)/shard_map/exchange/all_gather | solution.py:154
  104.9 0.0 copy-done.3
  104.9 0.0 copy-done.6
  104.9 0.0 copy-done.2
  104.9 0.0 copy-start.1
  104.9 2.2 %copy-done.1 = bf16[1024,2048]{1,0:T(8,128)(2,1)S(1)} copy-done((bf16[1024,2048]{1,0:T(8,128)(2,1)S(1)}, bf16[1024,2048]{1,0:T(8,128)(2,1)}, u32[]{:S(2)}) %copy-start.1) | copy-done | bytes 4194328
  107.1 2.7 %screened_response.1 = f32[2,1024,32]{2,1,0:T(8,128)S(1)} custom-call(f32[4]{0:T(128)S(1)} %copy-done.6, f32[4,4]{1,0:T(4,128)S(1)} %copy-done.3, bf16[2,32,2048]{2,1,0:T(8,128)(2,1)S(1)} %bitcast.7, f32[1,2048]{1,0:T(1,128)S(1)} %bitcast.8, bf16[1024,2048]{1,0:T(8,128)(2,1)S(1)} %copy-done.1), custom_call_target="tpu_custom_call" | custom-call | tf_op jit(solution)/shard_map/response/screened_response/pallas_call | solution.py:114
  109.8 1.0 copy.13
  (2 shorter events, 0.1 us)
Async XLA Ops:
  0.0 104.9 %copy-start.3 = (f32[4,4]{1,0:T(4,128)S(1)}, f32[4,4]{1,0:T(4,128)}, u32[]{:S(2)}) copy-start(f32[4,4]{1,0:T(4,128)} %cos_ref.1) | copy-start | bytes 196
  0.0 104.9 %copy-start.6 = (f32[4]{0:T(128)S(1)}, f32[4]{0:T(128)}, u32[]{:S(2)}) copy-start(f32[4]{0:T(128)} %times_ref.1) | copy-start | bytes 52
  0.0 104.9 %copy-start.2 = (f32[2048]{0:T(1024)S(1)}, f32[2048]{0:T(1024)}, u32[]{:S(2)}) copy-start(f32[2048]{0:T(1024)} %param.15) | copy-start | bytes 24580
  18.5 1.4 %collective-permute-start = (bf16[64,256]{1,0:T(8,128)(2,1)}, bf16[64,256]{1,0:T(8,128)(2,1)S(1)}, u32[]{:S(2)}, u32[]{:S(2)}) collective-permute-start(bf16[64,256]{1,0:T(8,128)(2,1)} %get-tuple-element.10), channel_id=1, source_target_pairs={{0,16},{16,0},{1,17},{17,1},{2,18},{18,2},{3,19},{19,3},{4,20},{20... | collective-permute-start | bytes 98312 | tf_op jit(solution)/shard_map/probes/ppermute | solution.py:143
  57.6 3.4 %copy-start = (bf16[16,512,512]{2,1,0:T(8,128)(2,1)S(1)}, bf16[16,512,512]{2,1,0:T(8,128)(2,1)}, u32[]{:S(2)}) copy-start(bf16[16,512,512]{2,1,0:T(8,128)(2,1)} %tiles_ref.1) | copy-start | bytes 25165828
  61.0 0.7 copy-start.4
  61.7 0.7 copy-start.5
  66.1 1.4 %collective-permute-start.1 = (bf16[32,2048]{1,0:T(8,128)(2,1)S(1)}, bf16[32,2048]{1,0:T(8,128)(2,1)S(1)}, u32[]{:S(2)}, u32[]{:S(2)}) collective-permute-start(bf16[32,2048]{1,0:T(8,128)(2,1)S(1)} %get-tuple-element.12), channel_id=1, source_target_pairs={{0,16},{16,0},{1,17},{17,1},{2,18},{18,2},{3,19},{19,3},{4,20},{20... | collective-permute-start | bytes 393224 | tf_op jit(solution)/shard_map/products/ppermute | solution.py:148
  67.6 14.4 %collective-permute-start.2 = (bf16[32,2048]{1,0:T(8,128)(2,1)S(1)}, bf16[32,2048]{1,0:T(8,128)(2,1)S(1)}, u32[]{:S(2)}, u32[]{:S(2)}) collective-permute-start(bf16[32,2048]{1,0:T(8,128)(2,1)S(1)} %add_convert_fusion), channel_id=1, source_target_pairs={{0,0},{1,16},{2,32},{3,48},{4,64},{5,80},{6,96},{7,112},{8,128},{9... | collective-permute-start | bytes 393224 | tf_op jit(solution)/shard_map/exchange/ppermute | solution.py:151
  104.9 2.2 %copy-start.1 = (bf16[1024,2048]{1,0:T(8,128)(2,1)S(1)}, bf16[1024,2048]{1,0:T(8,128)(2,1)}, u32[]{:S(2)}) copy-start(bf16[1024,2048]{1,0:T(8,128)(2,1)} %left_ref.1) | copy-start | bytes 12582916

commit v2 on v1

v2 whole, which is shorter than its diff:
```python
import jax
import jax.numpy as jnp
from jax import lax
from jax.experimental import pallas as pl
from jax.experimental.pallas import tpu as pltpu
from jax.sharding import Mesh, PartitionSpec as P

TILE = 512
MB = 4
CAP = 2
SLOTS = 16
NB = 16
NPAIR = 2048
NPROBE = 512
SET = 32
PART = 32
CODE = 16
ROWS = CAP * PART + CODE
LANES = 128
F32 = jnp.float32
BF16 = jnp.bfloat16
SMEM = pl.BlockSpec(memory_space=pltpu.SMEM)
VMEM = pl.BlockSpec(memory_space=pltpu.VMEM)


def place():
    return lax.axis_index("f") * 8 + lax.axis_index("y") * 2 + lax.axis_index("k")


def outgoing_parts(tiles, blocks, pairs, counts):
    def kernel(blocks_ref, pairs_ref, counts_ref, tiles_ref, out_ref, held, sems):
        me = place()
        lanes = pl.ds(pl.multiple_of(me // 4 * LANES, LANES), LANES)
        live = counts_ref[0]

        def copy(s):
            return pltpu.make_async_copy(tiles_ref.at[s, :, lanes], held.at[s], sems.at[s])

        for s in range(SLOTS):
            @pl.when(s < live)
            def _():
                copy(s).start()

        out_ref[...] = jnp.zeros_like(out_ref)
        wanted = lax.broadcasted_iota(jnp.int32, (PART, LANES), 0) + me % 4 * PART
        pick = jnp.where(wanted == lax.broadcasted_iota(jnp.int32, (PART, LANES), 1), 1.0, 0.0).astype(BF16)
        second = lax.broadcasted_iota(jnp.int32, (CODE, TILE), 0) // (CODE // CAP)
        for s in range(SLOTS):
            @pl.when(s < live)
            def _():
                owner = blocks_ref[s]
                earlier = jnp.int32(0)
                for t in range(s):
                    earlier += jnp.where(blocks_ref[t] == owner, 1, 0)
                copy(s).wait()
                part = lax.dot_general(pick, held[s], (((1,), (1,)), ((), ())), preferred_element_type=F32)
                out_ref[owner, pl.ds(pl.multiple_of(earlier * PART, PART), PART), :] = part.astype(BF16)
                codes = out_ref[owner, CAP * PART :, :].astype(F32)
                codes = jnp.where(second == earlier, pairs_ref[s].astype(F32), codes)
                out_ref[owner, CAP * PART :, :] = codes.astype(BF16)

    return pl.pallas_call(
        kernel,
        out_shape=jax.ShapeDtypeStruct((NB, ROWS, TILE), BF16),
        in_specs=[SMEM, SMEM, SMEM, pl.BlockSpec(memory_space=pl.ANY)],
        out_specs=VMEM,
        scratch_shapes=[pltpu.VMEM((SLOTS, TILE, LANES), BF16), pltpu.SemaphoreType.DMA((SLOTS,))],
        compiler_params=pltpu.CompilerParams(vmem_limit_bytes=56 << 20),
        name="outgoing_parts",
    )(blocks, pairs, counts, tiles)


def picked_probes(own, other, probe_idx):
    def kernel(own_ref, other_ref, idx_ref, out_ref):
        core = lax.axis_index("k")
        total = jnp.zeros((TILE, NPROBE), F32)
        for bank_ref, at in ((own_ref, core), (other_ref, 1 - core)):
            for y in range(4):
                here = lax.broadcasted_iota(jnp.int32, (LANES, NPROBE), 0) + (y * 2 + at) * LANES
                pick = jnp.where(here == idx_ref[...], 1.0, 0.0).astype(BF16)
                total += jnp.dot(bank_ref[y], pick, preferred_element_type=F32)
        out_ref[...] = total.astype(BF16)

    return pl.pallas_call(
        kernel,
        out_shape=jax.ShapeDtypeStruct((TILE, NPROBE), BF16),
        compiler_params=pltpu.CompilerParams(vmem_limit_bytes=16 << 20),
        name="picked_probes",
    )(own, other, probe_idx)


def owner_products(parts, probes):
    def kernel(parts_ref, probes_ref, out_ref, product):
        rows = parts_ref[:, : CAP * PART, :].reshape(NB * CAP * PART, TILE)
        product[...] = jnp.dot(rows, probes_ref[...], preferred_element_type=F32)
        for m in range(MB):
            total = jnp.zeros((PART, NPROBE), F32)
            for c in range(NB):
                for j in range(CAP):
                    code = parts_ref[c, CAP * PART :, :].astype(F32)[j * (CODE // CAP) : j * (CODE // CAP) + 1, :]
                    start = (c * CAP + j) * PART
                    total += jnp.where(code == m, product[start : start + PART, :], 0.0)
            turned = total.T.astype(BF16)
            for c in range(NB):
                out_ref[c, :, m * PART : (m + 1) * PART] = turned[c * SET : (c + 1) * SET, :]

    return pl.pallas_call(
        kernel,
        out_shape=jax.ShapeDtypeStruct((NB, SET, MB * PART), BF16),
        scratch_shapes=[pltpu.VMEM((NB * CAP * PART, NPROBE), F32)],
        compiler_params=pltpu.CompilerParams(vmem_limit_bytes=16 << 20),
        name="owner_products",
    )(parts, probes)


def screened_response(parts, left_panel, gaps, times, cos_weights):
    rows = left_panel.shape[0]
    block = 256

    def kernel(times_ref, cos_ref, parts_ref, gaps_ref, left_ref, out_ref, scaled):
        @pl.when(pl.program_id(0) == 0)
        def _():
            first = lax.axis_index("f") * 2
            lane = lax.broadcasted_iota(jnp.int32, (SET, LANES), 1) // PART
            decays = [jnp.exp(-gaps_ref[...] * times_ref[k]) for k in range(4)]
            weights = []
            for f in range(2):
                weight = decays[0] * cos_ref[first + f, 0]
                for k in range(1, 4):
                    weight += decays[k] * cos_ref[first + f, k]
                weights.append(weight)
            for g in range(4):
                held = [parts_ref[(4 * g + sub) // 2, sub % 2].astype(F32) for sub in range(4)]
                for m in range(MB):
                    whole = held[m]
                    for sub in range(4):
                        if sub != m:
                            whole = jnp.where(lane == sub, pltpu.roll(held[sub], (sub - m) % 4 * PART, 1), whole)
                    at = (m * 4 + g) * LANES
                    for f in range(2):
                        scaled[f * SET : (f + 1) * SET, at : at + LANES] = (
                            whole * weights[f][:, at : at + LANES]
                        ).astype(BF16)

        product = lax.dot_general(
            scaled[...], left_ref[...], (((1,), (1,)), ((), ())), preferred_element_type=F32
        )
        out_ref[0] = product[:SET]
        out_ref[1] = product[SET:]

    return pl.pallas_call(
        kernel,
        grid=(rows // block,),
        out_shape=jax.ShapeDtypeStruct((2, SET, rows), F32),
        in_specs=[
            SMEM,
            SMEM,
            pl.BlockSpec((8, 2, SET, LANES), lambda i: (0, 0, 0, 0)),
            pl.BlockSpec((1, NPAIR), lambda i: (0, 0)),
            pl.BlockSpec((block, NPAIR), lambda i: (i, 0)),
        ],
        out_specs=pl.BlockSpec((2, SET, block), lambda i: (0, 0, i)),
        scratch_shapes=[pltpu.VMEM((2 * SET, NPAIR), BF16)],
        compiler_params=pltpu.CompilerParams(vmem_limit_bytes=56 << 20),
        name="screened_response",
    )(times, cos_weights, parts, gaps, left_panel)


def shards(
    tiles, tile_blocks, tile_pairs, tile_counts, left_panel, gaps, times, cos_weights, bank, probe_idx
):
    with jax.named_scope("parts"):
        parts = outgoing_parts(tiles, tile_blocks.reshape(SLOTS), tile_pairs, tile_counts)
        parts = lax.all_to_all(parts, ("u", "z"), 0, 0, tiled=True)
    with jax.named_scope("probes"):
        banked = lax.all_gather(bank, "y", axis=0)
        probes = picked_probes(banked, lax.ppermute(banked, "k", [(0, 1), (1, 0)]), probe_idx.reshape(1, NPROBE))
    with jax.named_scope("products"):
        products = owner_products(parts, probes)
        products = lax.all_to_all(products, ("u", "z"), 0, 0, tiled=True)
        product = jnp.sum(products.astype(F32), axis=0).astype(BF16)
    with jax.named_scope("spread"):
        both = lax.all_gather(product, "k", axis=0)
        both = lax.all_to_all(jnp.broadcast_to(both, (8,) + both.shape), ("f", "y"), 0, 0, tiled=True)
    with jax.named_scope("response"):
        turned = screened_response(both, left_panel, gaps.reshape(1, NPAIR), times, cos_weights)
        return jnp.swapaxes(turned, 1, 2)


def solution(mesh):
    fine = Mesh(mesh.devices.reshape(2, 4, 2, 2, 8), ("f", "y", "k", "u", "z"))
    row, col = ("y", "k"), ("u", "z")
    placed = (
        P(col, None, None),
        P(col, None),
        P(col),
        P(col),
        P(row, None),
        P(),
        P(),
        P(),
        P(col, row),
        P(),
    )
    return jax.shard_map(
        shards, mesh=fine, in_specs=placed, out_specs=P("f", row, col), check_vma=False
    )
```

time: 112 us -> 85.6 us (0.76)
  blocking collectives: 74.7 us -> 40.8 us
  local copies, waits for them, and re-layouts: 9.29 us -> 0.03 us
  starting transfers between devices: 2.41 us -> 10.1 us
  waiting for transfers between devices: 14.2 us -> 19.5 us
  Pallas kernels: 8.56 us -> 13.6 us
    all_gather x5 -> x1, blocking collectives: 59.7 us -> 1.81 us  [shards(): both = lax.all_gather(product, 'k', axis=0)]
    all_to_all x0 -> x2, blocking collectives: none -> 25.7 us  [the longest x1 14.6 us: shards(): products = lax.all_to_all(products, ('u', 'z'), 0, 0, tiled=True)]
    all_to_all x0 -> x1, waiting for transfers between devices: none -> 17.6 us  [shards(): parts = lax.all_to_all(parts, ('u', 'z'), 0, 0, tiled=True)]
    ppermute x3 -> x1, waiting for transfers between devices: 14.2 us -> 1.91 us  [shards(): lax.ppermute(banked, 'k', [(0, 1), (1, 0)])]
    all_to_all x0 -> x1, starting transfers between devices: none -> 10.1 us  [shards(): parts = lax.all_to_all(parts, ('u', 'z'), 0, 0, tiled=True)]
    unnamed x14 -> x4, local copies, waits for them, and re-layouts: 6.89 us -> 0.01 us
    pallas_call x2 -> x3, Pallas kernels: 5.81 us -> 8.7 us  [the longest x1 5.64 us: outgoing_parts(): pl.pallas_call(kernel, out_shape=jax.ShapeDtypeStruct((NB, ROWS, TILE), B...]
    ppermute x3 -> x1, starting transfers between devices: 2.41 us -> 0.01 us  [shards(): lax.ppermute(banked, 'k', [(0, 1), (1, 0)])]
  transfers between devices with their start and end apart: 3 -> 2, of which waited for: 3 -> 2; matrix products, arithmetic and copies ran while one was open for 0% -> 0% of each run, Pallas kernels for 0% -> 1%
where the time goes in v2:
time: 85.6 us; the launch traced here: 84.8 us
  blocking collectives  40.8 us (48%)
  waiting for transfers between devices  19.5 us (23%)
  Pallas kernels  13.6 us (16%)
  starting transfers between devices  10.1 us (12%)
    all_to_all x1, waiting for transfers between devices, shards(): parts = lax.all_to_all(parts, ('u', 'z'), 0, 0, tiled=True)  17.6 us
    all_to_all x1, blocking collectives, shards(): products = lax.all_to_all(products, ('u', 'z'), 0, 0, tiled=True)  14.6 us
    all_gather x1, blocking collectives, shards(): banked = lax.all_gather(bank, 'y', axis=0)  13.3 us
    all_to_all x1, blocking collectives, shards(): lax.all_to_all(jnp.broadcast_to(both, (8,) + both.shape), ('f', 'y'), 0,...  11.1 us
    all_to_all x1, starting transfers between devices, shards(): parts = lax.all_to_all(parts, ('u', 'z'), 0, 0, tiled=True)  10.1 us
    pallas_call x1, Pallas kernels, outgoing_parts(): pl.pallas_call(kernel, out_shape=jax.ShapeDtypeStruct((NB, ROWS, TILE), B...  5.64 us
    pallas_call x1, Pallas kernels, screened_response(): pl.pallas_call(kernel, grid=(rows // block,), out_shape=jax.ShapeDtypeStr...  4.88 us
    ppermute x1, waiting for transfers between devices, shards(): lax.ppermute(banked, 'k', [(0, 1), (1, 0)])  1.91 us
  transfers between devices with their start and end apart: 2, of which 2 were waited for; matrix products, arithmetic and copies ran while one was open for 0% of the time, Pallas kernels for 1%

profile of v2, /device:TPU:2, one launch (start us, length us, event | category | flops | bytes accessed | tf_op | source)
XLA Modules:
  0.0 84.8 jit_solution(10719599044282085600)
XLA Ops:
  0.7 0.0 copy-start.1
  0.7 0.0 copy-start
  0.7 5.6 %outgoing_parts.1 = bf16[16,80,512]{2,1,0:T(8,128)(2,1)} custom-call(s32[16]{0:T(128)} %bitcast.11, s32[16]{0:T(128)} %pairs_ref.1, s32[1]{0:T(128)S(6)} %copy.11.counts_ref, bf16[16,512,512]{2,1,0:T(8,128)(2,1)} %tiles_ref.1), custom_call_target="tpu_custom_call" | custom-call | tf_op jit(solution)/shard_map/parts/outgoing_parts/pallas_call | solution.py:62
  6.3 10.1 %all-to-all-start = ((bf16[16,80,512]{2,1,0:T(8,128)(2,1)}), bf16[16,80,512]{2,1,0:T(8,128)(2,1)S(1)}, u32[]{:S(2)}, u32[]{:S(2)}) async-start(bf16[16,80,512]{2,1,0:T(8,128)(2,1)} %outgoing_parts.1), calls=%async_computation | async-start | bytes 2621440 | tf_op jit(solution)/shard_map/parts/all_to_all | solution.py:174
  16.5 0.0 copy-done.1
  16.5 13.3 %all-gather = bf16[2048,128]{1,0:T(8,128)(2,1)S(1)} all-gather(bf16[512,128]{1,0:T(8,128)(2,1)S(1)} %copy-done.1), channel_id=2, replica_groups=mesh['f'=2,'y'=4,'k'=2,'u'=2,'z'=8] {'y'}, dimensions={0}, use_global_device_ids=true | all-gather | bytes 655360 | tf_op jit(solution)/shard_map/probes/all_gather | solution.py:176
  29.8 0.0 collective-permute-start
  29.8 1.9 %collective-permute-done.other_ref = bf16[4,512,128]{2,1,0:T(8,128)(2,1)S(1)} collective-permute-done((bf16[4,512,128]{2,1,0:T(8,128)(2,1)S(1)}, bf16[4,512,128]{2,1,0:T(8,128)(2,1)S(1)}, u32[]{:S(2)}, u32[]{:S(2)}) %collective-permute-start) | collective-permute-done | bytes 524320 | tf_op jit(solution)/shard_map/probes/ppermute | solution.py:177
  31.7 0.0 copy-done
  31.7 1.2 %picked_probes.1.probes_ref = bf16[512,512]{1,0:T(8,128)(2,1)S(1)} custom-call(bf16[4,512,128]{2,1,0:T(8,128)(2,1)S(1)} %bitcast.7, bf16[4,512,128]{2,1,0:T(8,128)(2,1)S(1)} %collective-permute-done.other_ref, s32[1,512]{1,0:T(1,128)S(1)} %bitcast.8), custom_call_target="tpu_custom_call" | custom-call | tf_op jit(solution)/shard_map/probes/picked_probes/pallas_call | solution.py:84
  32.9 17.6 %all-to-all-done.parts_ref = bf16[16,80,512]{2,1,0:T(8,128)(2,1)S(1)} async-done(((bf16[16,80,512]{2,1,0:T(8,128)(2,1)}), bf16[16,80,512]{2,1,0:T(8,128)(2,1)S(1)}, u32[]{:S(2)}, u32[]{:S(2)}) %all-to-all-start) | async-done | bytes 1310752 | tf_op jit(solution)/shard_map/parts/all_to_all | solution.py:174
  50.5 1.8 %owner_products.1 = bf16[16,32,128]{2,1,0:T(8,128)(2,1)S(1)} custom-call(bf16[16,80,512]{2,1,0:T(8,128)(2,1)S(1)} %all-to-all-done.parts_ref, bf16[512,512]{1,0:T(8,128)(2,1)S(1)} %picked_probes.1.probes_ref), custom_call_target="tpu_custom_call" | custom-call | tf_op jit(solution)/shard_map/products/owner_products/pallas_call | solution.py:107
  52.4 14.6 %all_to_all.15 = bf16[16,32,128]{2,1,0:T(8,128)(2,1)S(1)} all-to-all(bf16[16,32,128]{2,1,0:T(8,128)(2,1)S(1)} %owner_products.1), channel_id=1, replica_groups=mesh['f'=2,'y'=4,'k'=2,'u'=2,'z'=8] {'u','z'}, dimensions={0} | all-to-all | bytes 262144 | tf_op jit(solution)/shard_map/products/all_to_all | solution.py:180
  67.0 1.8 %all-gather.1 = bf16[64,128]{1,0:T(8,128)(2,1)S(1)} all-gather(bf16[32,128]{1,0:T(8,128)(2,1)S(1)} %reduce_sum.12), channel_id=3, replica_groups=mesh['f'=2,'y'=4,'k'=2,'u'=2,'z'=8] {'k'}, dimensions={0}, use_global_device_ids=true | all-gather | bytes 24576 | tf_op jit(solution)/shard_map/spread/all_gather | solution.py:183
  68.8 11.1 %all_to_all.16.parts_ref = bf16[8,2,32,128]{3,2,1,0:T(8,128)(2,1)} all-to-all(bf16[8,2,32,128]{3,2,1,0:T(8,128)(2,1)S(1)} %broadcast_in_dim.3), channel_id=1, replica_groups=mesh['f'=2,'y'=4,'k'=2,'u'=2,'z'=8] {'f','y'}, dimensions={0} | all-to-all | bytes 262144 | tf_op jit(solution)/shard_map/spread/all_to_all | solution.py:184
  79.9 4.9 %screened_response.1 = f32[2,32,1024]{2,1,0:T(8,128)} custom-call(f32[4]{0:T(128)} %times_ref.1, f32[4,4]{1,0:T(4,128)} %cos_ref.1, bf16[8,2,32,128]{3,2,1,0:T(8,128)(2,1)} %all_to_all.16.parts_ref, f32[1,2048]{1,0:T(1,128)} %bitcast.10, bf16[1024,2048]{1,0:T(8,128)(2,1)} %left_ref.1), custom_call_target="tpu_custom_call" | custom-call | tf_op jit(solution)/shard_map/response/screened_response/pallas_call | solution.py:151
  (2 shorter events, 0.0 us)
Async XLA Ops:
  0.7 15.8 %copy-start.1 = (bf16[512,128]{1,0:T(8,128)(2,1)S(1)}, bf16[512,128]{1,0:T(8,128)(2,1)}, u32[]{:S(2)}) copy-start(bf16[512,128]{1,0:T(8,128)(2,1)} %param.18) | copy-start | bytes 393220
  0.7 31.0 %copy-start = (s32[512]{0:T(512)S(1)}, s32[512]{0:T(512)}, u32[]{:S(2)}) copy-start(s32[512]{0:T(512)} %param.19) | copy-start | bytes 6148
  6.3 44.2 %all-to-all-start = ((bf16[16,80,512]{2,1,0:T(8,128)(2,1)}), bf16[16,80,512]{2,1,0:T(8,128)(2,1)S(1)}, u32[]{:S(2)}, u32[]{:S(2)}) async-start(bf16[16,80,512]{2,1,0:T(8,128)(2,1)} %outgoing_parts.1), calls=%async_computation | async-start | bytes 2621440 | tf_op jit(solution)/shard_map/parts/all_to_all | solution.py:174
  29.8 1.9 %collective-permute-start = (bf16[4,512,128]{2,1,0:T(8,128)(2,1)S(1)}, bf16[4,512,128]{2,1,0:T(8,128)(2,1)S(1)}, u32[]{:S(2)}, u32[]{:S(2)}) collective-permute-start(bf16[4,512,128]{2,1,0:T(8,128)(2,1)S(1)} %bitcast.6), channel_id=1, source_target_pairs={{0,16},{16,0},{1,17},{17,1},{2,18},{18,2},{3,19},{19,3},{4,20},{20... | collective-permute-start | bytes 1572872 | tf_op jit(solution)/shard_map/probes/ppermute | solution.py:177

commit v3 on v2

v3 whole, which is shorter than its diff:
```python
import jax
import jax.numpy as jnp
from jax import lax
from jax.experimental import pallas as pl
from jax.experimental.pallas import tpu as pltpu
from jax.sharding import Mesh, PartitionSpec as P

TILE = 512
MB = 4
CAP = 2
SLOTS = 16
NB = 16
NPAIR = 2048
NPROBE = 512
SET = 32
PART = 32
CODE = 16
LANES = 128
CHUNKS = 4
UNIT = PART * TILE // LANES
ROWS = CAP * UNIT + CODE
F32 = jnp.float32
BF16 = jnp.bfloat16
SMEM = pl.BlockSpec(memory_space=pltpu.SMEM)
VMEM = pl.BlockSpec(memory_space=pltpu.VMEM)


def place():
    return lax.axis_index("f") * 8 + lax.axis_index("y") * 2 + lax.axis_index("k")


def outgoing_parts(tiles, blocks, pairs, counts):
    def kernel(blocks_ref, pairs_ref, counts_ref, tiles_ref, out_ref, held, parts, source, sems):
        me = place()
        lanes = pl.ds(pl.multiple_of(me // 4 * LANES, LANES), LANES)

        def copy(s):
            return pltpu.make_async_copy(tiles_ref.at[s, :, lanes], held.at[s], sems.at[s])

        for s in range(SLOTS):
            copy(s).start()
        live = counts_ref[0]
        for d in range(NB * CAP):
            source[d] = -1
        for s in range(SLOTS):
            at = blocks_ref[s] * CAP
            at = jnp.where(source[at] >= 0, at + 1, at)
            source[at] = jnp.where(s < live, s, source[at])

        wanted = lax.broadcasted_iota(jnp.int32, (PART, LANES), 0) + me % 4 * PART
        pick = jnp.where(wanted == lax.broadcasted_iota(jnp.int32, (PART, LANES), 1), 1.0, 0.0).astype(BF16)
        for s in range(SLOTS):
            copy(s).wait()
            part = lax.dot_general(pick, held[s], (((1,), (1,)), ((), ())), preferred_element_type=F32)
            for n in range(TILE // LANES):
                parts[s, n * PART : (n + 1) * PART, :] = part[:, n * LANES : (n + 1) * LANES].astype(BF16)

        second = lax.broadcasted_iota(jnp.int32, (CODE, LANES), 0) >= CODE // CAP
        for d in range(NB):
            codes = []
            for j in range(CAP):
                s = source[d * CAP + j]
                there = jnp.maximum(s, 0)
                full = jnp.where(s >= 0, 1.0, 0.0).astype(BF16)
                out_ref[d, j * UNIT : (j + 1) * UNIT, :] = parts[there] * full
                codes.append(pairs_ref[there].astype(F32))
            out_ref[d, CAP * UNIT :, :] = jnp.where(second, codes[1], codes[0]).astype(BF16)

    return pl.pallas_call(
        kernel,
        out_shape=jax.ShapeDtypeStruct((NB, ROWS, LANES), BF16),
        in_specs=[SMEM, SMEM, SMEM, pl.BlockSpec(memory_space=pl.ANY)],
        out_specs=VMEM,
        scratch_shapes=[
            pltpu.VMEM((SLOTS, TILE, LANES), BF16),
            pltpu.VMEM((SLOTS, UNIT, LANES), BF16),
            pltpu.SMEM((NB * CAP,), jnp.int32),
            pltpu.SemaphoreType.DMA((SLOTS,)),
        ],
        compiler_params=pltpu.CompilerParams(vmem_limit_bytes=56 << 20),
        name="outgoing_parts",
    )(blocks, pairs, counts, tiles)


def picked_probes(own, other, probe_idx, gaps, times, cos_weights):
    def kernel(times_ref, cos_ref, own_ref, other_ref, idx_ref, gaps_ref, out_ref, weights_ref):
        core = lax.axis_index("k")
        total = jnp.zeros((TILE, NPROBE), F32)
        for bank_ref, at in ((own_ref, core), (other_ref, 1 - core)):
            for y in range(4):
                here = lax.broadcasted_iota(jnp.int32, (LANES, NPROBE), 0) + (y * 2 + at) * LANES
                pick = jnp.where(here == idx_ref[...], 1.0, 0.0).astype(BF16)
                total += jnp.dot(bank_ref[y], pick, preferred_element_type=F32)
        out_ref[...] = total.astype(BF16)
        first = lax.axis_index("f") * 2
        decays = [jnp.exp(-gaps_ref[...] * times_ref[k]) for k in range(4)]
        for f in range(2):
            weight = decays[0] * cos_ref[first + f, 0]
            for k in range(1, 4):
                weight += decays[k] * cos_ref[first + f, k]
            weights_ref[f : f + 1, :] = weight

    return pl.pallas_call(
        kernel,
        out_shape=(jax.ShapeDtypeStruct((TILE, NPROBE), BF16), jax.ShapeDtypeStruct((2, NPAIR), F32)),
        in_specs=[SMEM, SMEM, VMEM, VMEM, VMEM, VMEM],
        out_specs=(VMEM, VMEM),
        compiler_params=pltpu.CompilerParams(vmem_limit_bytes=24 << 20),
        name="picked_probes",
    )(times, cos_weights, own, other, probe_idx, gaps)


def owner_products(parts, probes):
    def kernel(parts_ref, probes_ref, out_ref, product):
        units = parts_ref[:, : CAP * UNIT, :].reshape(NB * CAP, TILE // LANES, PART, LANES)
        rows = jnp.concatenate([units[:, n] for n in range(TILE // LANES)], axis=-1).reshape(NB * CAP * PART, TILE)
        product[...] = jnp.dot(rows, probes_ref[...], preferred_element_type=F32)
        codes = [
            parts_ref[c, CAP * UNIT :, :].astype(F32)[j * (CODE // CAP) : j * (CODE // CAP) + 1, :1]
            for c in range(NB)
            for j in range(CAP)
        ]
        for m in range(MB):
            total = jnp.zeros((PART, NPROBE), F32)
            for n, code in enumerate(codes):
                total += jnp.where(code == m, product[n * PART : (n + 1) * PART, :], 0.0)
            turned = total.T.astype(BF16)
            for c in range(NB):
                out_ref[c, :, m * PART : (m + 1) * PART] = turned[c * SET : (c + 1) * SET, :]

    return pl.pallas_call(
        kernel,
        out_shape=jax.ShapeDtypeStruct((NB, SET, MB * PART), BF16),
        scratch_shapes=[pltpu.VMEM((NB * CAP * PART, NPROBE), F32)],
        compiler_params=pltpu.CompilerParams(vmem_limit_bytes=16 << 20),
        name="owner_products",
    )(parts, probes)


def screened_response(parts, left_panel, weights):
    rows = left_panel.shape[0]
    step = rows // CHUNKS

    def kernel(parts_ref, left_ref, weights_ref, out_ref, scaled, left, sems):
        def copy(n):
            chunk = pl.ds(n * step, step)
            return pltpu.make_async_copy(left_ref.at[chunk, :], left.at[chunk, :], sems.at[n])

        for n in range(CHUNKS):
            copy(n).start()
        lane = lax.broadcasted_iota(jnp.int32, (SET, LANES), 1) // PART
        for g in range(4):
            held = [parts_ref[(4 * g + sub) // 2, sub % 2].astype(F32) for sub in range(4)]
            for m in range(MB):
                whole = held[m]
                for sub in range(4):
                    if sub != m:
                        whole = jnp.where(lane == sub, pltpu.roll(held[sub], (sub - m) % 4 * PART, 1), whole)
                at = (m * 4 + g) * LANES
                for f in range(2):
                    scaled[f * SET : (f + 1) * SET, at : at + LANES] = (
                        whole * weights_ref[f : f + 1, at : at + LANES]
                    ).astype(BF16)
        for n in range(CHUNKS):
            copy(n).wait()
            product = lax.dot_general(
                scaled[...], left[n * step : (n + 1) * step, :], (((1,), (1,)), ((), ())), preferred_element_type=F32
            )
            out_ref[0, :, n * step : (n + 1) * step] = product[:SET]
            out_ref[1, :, n * step : (n + 1) * step] = product[SET:]

    return pl.pallas_call(
        kernel,
        out_shape=jax.ShapeDtypeStruct((2, SET, rows), F32),
        in_specs=[VMEM, pl.BlockSpec(memory_space=pl.ANY), VMEM],
        out_specs=VMEM,
        scratch_shapes=[
            pltpu.VMEM((2 * SET, NPAIR), BF16),
            pltpu.VMEM((rows, NPAIR), BF16),
            pltpu.SemaphoreType.DMA((CHUNKS,)),
        ],
        compiler_params=pltpu.CompilerParams(vmem_limit_bytes=56 << 20),
        name="screened_response",
    )(parts, left_panel, weights)


def shards(
    tiles, tile_blocks, tile_pairs, tile_counts, left_panel, gaps, times, cos_weights, bank, probe_idx
):
    with jax.named_scope("parts"):
        parts = outgoing_parts(tiles, tile_blocks.reshape(SLOTS), tile_pairs, tile_counts)
        parts = lax.all_to_all(parts, ("u", "z"), 0, 0, tiled=True)
    with jax.named_scope("probes"):
        banked = lax.all_gather(bank, "y", axis=0)
        other = lax.ppermute(banked, "k", [(0, 1), (1, 0)])
        probes, weights = picked_probes(
            banked, other, probe_idx.reshape(1, NPROBE), gaps.reshape(1, NPAIR), times, cos_weights
        )
    with jax.named_scope("products"):
        products = owner_products(parts, probes)
        products = lax.all_to_all(products, ("u", "z"), 0, 0, tiled=True)
        product = jnp.sum(products.astype(F32), axis=0).astype(BF16)
    with jax.named_scope("spread"):
        both = lax.all_gather(product, "k", axis=0)
        both = lax.all_to_all(jnp.broadcast_to(both, (8,) + both.shape), ("f", "y"), 0, 0, tiled=True)
    with jax.named_scope("response"):
        turned = screened_response(both, left_panel, weights)
        return jnp.swapaxes(turned, 1, 2)


def solution(mesh):
    fine = Mesh(mesh.devices.reshape(2, 4, 2, 2, 8), ("f", "y", "k", "u", "z"))
    row, col = ("y", "k"), ("u", "z")
    placed = (
        P(col, None, None),
        P(col, None),
        P(col),
        P(col),
        P(row, None),
        P(),
        P(),
        P(),
        P(col, row),
        P(),
    )
    return jax.shard_map(
        shards, mesh=fine, in_specs=placed, out_specs=P("f", row, col), check_vma=False
    )
```

time: 85.6 us -> 81.9 us (0.957)
  waiting for transfers between devices: 19.5 us -> 14.2 us
    all_to_all x1, waiting for transfers between devices: 17.6 us -> 12.3 us  [shards(): parts = lax.all_to_all(parts, ('u', 'z'), 0, 0, tiled=True)]
    pallas_call x3, Pallas kernels: 11.8 us -> 12.9 us  [the longest x1 5.56 us: screened_response(): pl.pallas_call(kernel, out_shape=jax.ShapeDtypeStruct((2, SET, rows), F32...]
  transfers between devices with their start and end apart: 2 -> 2, of which waited for: 2 -> 2; matrix products, arithmetic and copies ran while one was open for 0% -> 0% of each run, Pallas kernels for 1% -> 2%
where the time goes in v3:
time: 81.9 us; the launch traced here: 80.9 us
  blocking collectives  40.7 us (50%)
  Pallas kernels  14.4 us (18%)
  waiting for transfers between devices  14.2 us (17%)
  starting transfers between devices  10.1 us (12%)
    all_to_all x1, blocking collectives, shards(): products = lax.all_to_all(products, ('u', 'z'), 0, 0, tiled=True)  14.5 us
    all_gather x1, blocking collectives, shards(): banked = lax.all_gather(bank, 'y', axis=0)  13.3 us
    all_to_all x1, waiting for transfers between devices, shards(): parts = lax.all_to_all(parts, ('u', 'z'), 0, 0, tiled=True)  12.3 us
    all_to_all x1, blocking collectives, shards(): lax.all_to_all(jnp.broadcast_to(both, (8,) + both.shape), ('f', 'y'), 0,...  11.1 us
    all_to_all x1, starting transfers between devices, shards(): parts = lax.all_to_all(parts, ('u', 'z'), 0, 0, tiled=True)  10.1 us
    pallas_call x1, Pallas kernels, screened_response(): pl.pallas_call(kernel, out_shape=jax.ShapeDtypeStruct((2, SET, rows), F32...  5.56 us
    pallas_call x1, Pallas kernels, outgoing_parts(): pl.pallas_call(kernel, out_shape=jax.ShapeDtypeStruct((NB, ROWS, LANES),...  5.54 us
    ppermute x1, waiting for transfers between devices, shards(): other = lax.ppermute(banked, 'k', [(0, 1), (1, 0)])  1.91 us
  transfers between devices with their start and end apart: 2, of which 2 were waited for; matrix products, arithmetic and copies ran while one was open for 0% of the time, Pallas kernels for 2%

profile of v3, /device:TPU:2, one launch (start us, length us, event | category | flops | bytes accessed | tf_op | source)
XLA Modules:
  0.0 80.9 jit_solution(227467256241690768)
XLA Ops:
  0.7 0.0 copy-start.5
  0.7 0.0 copy-start.1
  0.7 0.0 copy-start.2
  0.7 0.0 copy-start.3
  0.7 0.0 copy-start.4
  0.7 5.5 %outgoing_parts.1 = bf16[16,272,128]{2,1,0:T(8,128)(2,1)} custom-call(s32[16]{0:T(128)} %bitcast.11, s32[16]{0:T(128)} %pairs_ref.1, s32[1]{0:T(128)S(6)} %copy.11.counts_ref, bf16[16,512,512]{2,1,0:T(8,128)(2,1)} %tiles_ref.1), custom_call_target="tpu_custom_call" | custom-call | tf_op jit(solution)/shard_map/parts/outgoing_parts/pallas_call | solution.py:69
  6.2 10.1 %all-to-all-start = ((bf16[16,272,128]{2,1,0:T(8,128)(2,1)}), bf16[16,272,128]{2,1,0:T(8,128)(2,1)S(1)}, u32[]{:S(2)}, u32[]{:S(2)}) async-start(bf16[16,272,128]{2,1,0:T(8,128)(2,1)} %outgoing_parts.1), calls=%async_computation | async-start | bytes 2228224 | tf_op jit(solution)/shard_map/parts/all_to_all | solution.py:192
  16.4 0.0 copy-done.5
  16.4 13.3 %all-gather = bf16[2048,128]{1,0:T(8,128)(2,1)S(1)} all-gather(bf16[512,128]{1,0:T(8,128)(2,1)S(1)} %copy-done.5), channel_id=2, replica_groups=mesh['f'=2,'y'=4,'k'=2,'u'=2,'z'=8] {'y'}, dimensions={0}, use_global_device_ids=true | all-gather | bytes 655360 | tf_op jit(solution)/shard_map/probes/all_gather | solution.py:194
  29.7 0.0 collective-permute-start
  29.7 1.9 %collective-permute-done.other_ref = bf16[4,512,128]{2,1,0:T(8,128)(2,1)S(1)} collective-permute-done((bf16[4,512,128]{2,1,0:T(8,128)(2,1)S(1)}, bf16[4,512,128]{2,1,0:T(8,128)(2,1)S(1)}, u32[]{:S(2)}, u32[]{:S(2)}) %collective-permute-start) | collective-permute-done | bytes 524320 | tf_op jit(solution)/shard_map/probes/ppermute | solution.py:195
  31.6 0.0 copy-done.1
  31.6 0.0 copy-done.2
  31.6 0.0 copy-done.3
  31.6 0.0 copy-done.4
  31.6 1.8 %picked_probes.1 = (bf16[512,512]{1,0:T(8,128)(2,1)S(1)}, f32[2,2048]{1,0:T(2,128)S(1)}) custom-call(f32[4]{0:T(128)S(1)} %copy-done.4, f32[4,4]{1,0:T(4,128)S(1)} %copy-done.2, bf16[4,512,128]{2,1,0:T(8,128)(2,1)S(1)} %bitcast.7, bf16[4,512,128]{2,1,0:T(8,128)(2,1)S(1)} %collective-permute-done.other_ref, s32[1,512]{1,0:T(1,128)S(1)} %bitcast.9, ...), custom_call_target="tpu_custom_call" | custom-call | tf_op jit(solution)/shard_map/probes/picked_probes/pallas_call | solution.py:103
  33.5 0.0 copy-start
  33.5 0.6 copy-done
  34.1 12.3 %all-to-all-done.parts_ref = bf16[16,272,128]{2,1,0:T(8,128)(2,1)S(1)} async-done(((bf16[16,272,128]{2,1,0:T(8,128)(2,1)}), bf16[16,272,128]{2,1,0:T(8,128)(2,1)S(1)}, u32[]{:S(2)}, u32[]{:S(2)}) %all-to-all-start) | async-done | bytes 1114144 | tf_op jit(solution)/shard_map/parts/all_to_all | solution.py:192
  46.3 1.5 %owner_products.1 = bf16[16,32,128]{2,1,0:T(8,128)(2,1)S(1)} custom-call(bf16[16,272,128]{2,1,0:T(8,128)(2,1)S(1)} %all-to-all-done.parts_ref, bf16[512,512]{1,0:T(8,128)(2,1)S(1)} %get-tuple-element.7.probes_ref), custom_call_target="tpu_custom_call" | custom-call | tf_op jit(solution)/shard_map/products/owner_products/pallas_call | solution.py:131
  47.9 14.5 %all_to_all.15 = bf16[16,32,128]{2,1,0:T(8,128)(2,1)S(1)} all-to-all(bf16[16,32,128]{2,1,0:T(8,128)(2,1)S(1)} %owner_products.1), channel_id=1, replica_groups=mesh['f'=2,'y'=4,'k'=2,'u'=2,'z'=8] {'u','z'}, dimensions={0} | all-to-all | bytes 262144 | tf_op jit(solution)/shard_map/products/all_to_all | solution.py:201
  62.4 1.8 %all-gather.1 = bf16[64,128]{1,0:T(8,128)(2,1)S(1)} all-gather(bf16[32,128]{1,0:T(8,128)(2,1)S(1)} %reduce_sum.12), channel_id=3, replica_groups=mesh['f'=2,'y'=4,'k'=2,'u'=2,'z'=8] {'k'}, dimensions={0}, use_global_device_ids=true | all-gather | bytes 24576 | tf_op jit(solution)/shard_map/spread/all_gather | solution.py:204
  64.3 11.1 %all_to_all.16.parts_ref = bf16[8,2,32,128]{3,2,1,0:T(8,128)(2,1)} all-to-all(bf16[8,2,32,128]{3,2,1,0:T(8,128)(2,1)S(1)} %broadcast_in_dim.3), channel_id=1, replica_groups=mesh['f'=2,'y'=4,'k'=2,'u'=2,'z'=8] {'f','y'}, dimensions={0} | all-to-all | bytes 262144 | tf_op jit(solution)/shard_map/spread/all_to_all | solution.py:205
  75.3 5.6 %screened_response.1 = f32[2,32,1024]{2,1,0:T(8,128)} custom-call(bf16[8,2,32,128]{3,2,1,0:T(8,128)(2,1)} %all_to_all.16.parts_ref, bf16[1024,2048]{1,0:T(8,128)(2,1)} %left_ref.1, f32[2,2048]{1,0:T(2,128)} %copy-done), custom_call_target="tpu_custom_call" | custom-call | tf_op jit(solution)/shard_map/response/screened_response/pallas_call | solution.py:172
  (2 shorter events, 0.0 us)
Async XLA Ops:
  0.7 15.7 %copy-start.5 = (bf16[512,128]{1,0:T(8,128)(2,1)S(1)}, bf16[512,128]{1,0:T(8,128)(2,1)}, u32[]{:S(2)}) copy-start(bf16[512,128]{1,0:T(8,128)(2,1)} %param.18) | copy-start | bytes 393220
  0.7 31.0 %copy-start.1 = (f32[2048]{0:T(1024)S(1)}, f32[2048]{0:T(1024)}, u32[]{:S(2)}) copy-start(f32[2048]{0:T(1024)} %param.15) | copy-start | bytes 24580
  0.7 31.0 %copy-start.2 = (f32[4,4]{1,0:T(4,128)S(1)}, f32[4,4]{1,0:T(4,128)}, u32[]{:S(2)}) copy-start(f32[4,4]{1,0:T(4,128)} %cos_ref.1) | copy-start | bytes 196
  0.7 31.0 %copy-start.3 = (s32[512]{0:T(512)S(1)}, s32[512]{0:T(512)}, u32[]{:S(2)}) copy-start(s32[512]{0:T(512)} %param.19) | copy-start | bytes 6148
  0.7 30.9 %copy-start.4 = (f32[4]{0:T(128)S(1)}, f32[4]{0:T(128)}, u32[]{:S(2)}) copy-start(f32[4]{0:T(128)} %times_ref.1) | copy-start | bytes 52
  6.2 40.1 %all-to-all-start = ((bf16[16,272,128]{2,1,0:T(8,128)(2,1)}), bf16[16,272,128]{2,1,0:T(8,128)(2,1)S(1)}, u32[]{:S(2)}, u32[]{:S(2)}) async-start(bf16[16,272,128]{2,1,0:T(8,128)(2,1)} %outgoing_parts.1), calls=%async_computation | async-start | bytes 2228224 | tf_op jit(solution)/shard_map/parts/all_to_all | solution.py:192
  29.7 1.9 %collective-permute-start = (bf16[4,512,128]{2,1,0:T(8,128)(2,1)S(1)}, bf16[4,512,128]{2,1,0:T(8,128)(2,1)S(1)}, u32[]{:S(2)}, u32[]{:S(2)}) collective-permute-start(bf16[4,512,128]{2,1,0:T(8,128)(2,1)S(1)} %bitcast.6), channel_id=1, source_target_pairs={{0,16},{16,0},{1,17},{17,1},{2,18},{18,2},{3,19},{19,3},{4,20},{20... | collective-permute-start | bytes 1572872 | tf_op jit(solution)/shard_map/probes/ppermute | solution.py:195
  33.5 0.6 copy-start

commit v4 on v3

--- a/solution.py
+++ b/solution.py
@@ -16,13 +16,13 @@
 PART = 32
 CODE = 16
 LANES = 128
-CHUNKS = 4
 UNIT = PART * TILE // LANES
 ROWS = CAP * UNIT + CODE
 F32 = jnp.float32
 BF16 = jnp.bfloat16
 SMEM = pl.BlockSpec(memory_space=pltpu.SMEM)
 VMEM = pl.BlockSpec(memory_space=pltpu.VMEM)
+HBM = pl.BlockSpec(memory_space=pltpu.HBM)
 
 
 def place():
@@ -51,6 +51,7 @@
         pick = jnp.where(wanted == lax.broadcasted_iota(jnp.int32, (PART, LANES), 1), 1.0, 0.0).astype(BF16)
         for s in range(SLOTS):
             copy(s).wait()
+        for s in range(SLOTS):
             part = lax.dot_general(pick, held[s], (((1,), (1,)), ((), ())), preferred_element_type=F32)
             for n in range(TILE // LANES):
                 parts[s, n * PART : (n + 1) * PART, :] = part[:, n * LANES : (n + 1) * LANES].astype(BF16)
@@ -69,7 +70,7 @@
     return pl.pallas_call(
         kernel,
         out_shape=jax.ShapeDtypeStruct((NB, ROWS, LANES), BF16),
-        in_specs=[SMEM, SMEM, SMEM, pl.BlockSpec(memory_space=pl.ANY)],
+        in_specs=[SMEM, SMEM, SMEM, HBM],
         out_specs=VMEM,
         scratch_shapes=[
             pltpu.VMEM((SLOTS, TILE, LANES), BF16),
@@ -77,7 +78,7 @@
             pltpu.SMEM((NB * CAP,), jnp.int32),
             pltpu.SemaphoreType.DMA((SLOTS,)),
         ],
-        compiler_params=pltpu.CompilerParams(vmem_limit_bytes=56 << 20),
+        compiler_params=pltpu.CompilerParams(vmem_limit_bytes=8 << 20),
         name="outgoing_parts",
     )(blocks, pairs, counts, tiles)
 
@@ -110,11 +111,18 @@
     )(times, cos_weights, own, other, probe_idx, gaps)
 
 
-def owner_products(parts, probes):
-    def kernel(parts_ref, probes_ref, out_ref, product):
+def owner_products(parts, probes, left_panel):
+    half = left_panel.shape[0] // 2
+
+    def kernel(parts_ref, probes_ref, left_ref, out_ref, left_out_ref, held, product, sems):
+        first = pltpu.make_async_copy(probes_ref, held, sems.at[0])
+        first.start()
+        fetch = pltpu.make_async_copy(left_ref.at[pl.ds(0, half), :], left_out_ref, sems.at[1])
         units = parts_ref[:, : CAP * UNIT, :].reshape(NB * CAP, TILE // LANES, PART, LANES)
         rows = jnp.concatenate([units[:, n] for n in range(TILE // LANES)], axis=-1).reshape(NB * CAP * PART, TILE)
-        product[...] = jnp.dot(rows, probes_ref[...], preferred_element_type=F32)
+        first.wait()
+        fetch.start()
+        product[...] = jnp.dot(rows, held[...], preferred_element_type=F32)
         codes = [
             parts_ref[c, CAP * UNIT :, :].astype(F32)[j * (CODE // CAP) : j * (CODE // CAP) + 1, :1]
             for c in range(NB)
@@ -127,27 +135,32 @@
             turned = total.T.astype(BF16)
             for c in range(NB):
                 out_ref[c, :, m * PART : (m + 1) * PART] = turned[c * SET : (c + 1) * SET, :]
-
-    return pl.pallas_call(
-        kernel,
-        out_shape=jax.ShapeDtypeStruct((NB, SET, MB * PART), BF16),
-        scratch_shapes=[pltpu.VMEM((NB * CAP * PART, NPROBE), F32)],
+        fetch.wait()
+
+    return pl.pallas_call(
+        kernel,
+        out_shape=(
+            jax.ShapeDtypeStruct((NB, SET, MB * PART), BF16),
+            jax.ShapeDtypeStruct((half, NPAIR), BF16),
+        ),
+        in_specs=[VMEM, HBM, HBM],
+        out_specs=(VMEM, VMEM),
+        scratch_shapes=[
+            pltpu.VMEM((TILE, NPROBE), BF16),
+            pltpu.VMEM((NB * CAP * PART, NPROBE), F32),
+            pltpu.SemaphoreType.DMA((2,)),
+        ],
         compiler_params=pltpu.CompilerParams(vmem_limit_bytes=16 << 20),
         name="owner_products",
-    )(parts, probes)
-
-
-def screened_response(parts, left_panel, weights):
-    rows = left_panel.shape[0]
-    step = rows // CHUNKS
-
-    def kernel(parts_ref, left_ref, weights_ref, out_ref, scaled, left, sems):
-        def copy(n):
-            chunk = pl.ds(n * step, step)
-            return pltpu.make_async_copy(left_ref.at[chunk, :], left.at[chunk, :], sems.at[n])
-
-        for n in range(CHUNKS):
-            copy(n).start()
+    )(parts, probes, left_panel)
+
+
+def screened_response(parts, first_half, left_panel, weights):
+    half = first_half.shape[0]
+
+    def kernel(parts_ref, first_ref, left_ref, weights_ref, out_ref, scaled, second, sem):
+        fetch = pltpu.make_async_copy(left_ref.at[pl.ds(half, half), :], second, sem)
+        fetch.start()
         lane = lax.broadcasted_iota(jnp.int32, (SET, LANES), 1) // PART
         for g in range(4):
             held = [parts_ref[(4 * g + sub) // 2, sub % 2].astype(F32) for sub in range(4)]
@@ -161,34 +174,37 @@
                     scaled[f * SET : (f + 1) * SET, at : at + LANES] = (
                         whole * weights_ref[f : f + 1, at : at + LANES]
                     ).astype(BF16)
-        for n in range(CHUNKS):
-            copy(n).wait()
+        for n, left in enumerate((first_ref, second)):
+            if n == 1:
+                fetch.wait()
             product = lax.dot_general(
-                scaled[...], left[n * step : (n + 1) * step, :], (((1,), (1,)), ((), ())), preferred_element_type=F32
+                scaled[...], left[...], (((1,), (1,)), ((), ())), preferred_element_type=F32
             )
-            out_ref[0, :, n * step : (n + 1) * step] = product[:SET]
-            out_ref[1, :, n * step : (n + 1) * step] = product[SET:]
-
-    return pl.pallas_call(
-        kernel,
-        out_shape=jax.ShapeDtypeStruct((2, SET, rows), F32),
-        in_specs=[VMEM, pl.BlockSpec(memory_space=pl.ANY), VMEM],
+            out_ref[0, :, n * half : (n + 1) * half] = product[:SET]
+            out_ref[1, :, n * half : (n + 1) * half] = product[SET:]
+
+    return pl.pallas_call(
+        kernel,
+        out_shape=jax.ShapeDtypeStruct((2, SET, 2 * half), F32),
+        in_specs=[VMEM, VMEM, HBM, VMEM],
         out_specs=VMEM,
         scratch_shapes=[
             pltpu.VMEM((2 * SET, NPAIR), BF16),
-            pltpu.VMEM((rows, NPAIR), BF16),
-            pltpu.SemaphoreType.DMA((CHUNKS,)),
+            pltpu.VMEM((half, NPAIR), BF16),
+            pltpu.SemaphoreType.DMA,
         ],
-        compiler_params=pltpu.CompilerParams(vmem_limit_bytes=56 << 20),
+        compiler_params=pltpu.CompilerParams(vmem_limit_bytes=12 << 20),
         name="screened_response",
-    )(parts, left_panel, weights)
+    )(parts, first_half, left_panel, weights)
 
 
 def shards(
     tiles, tile_blocks, tile_pairs, tile_counts, left_panel, gaps, times, cos_weights, bank, probe_idx
 ):
+    stay = lambda array: pltpu.with_memory_space_constraint(array, pltpu.HBM)
+    tiles, tile_blocks, tile_pairs, left_panel = map(stay, (tiles, tile_blocks.reshape(SLOTS), tile_pairs, left_panel))
     with jax.named_scope("parts"):
-        parts = outgoing_parts(tiles, tile_blocks.reshape(SLOTS), tile_pairs, tile_counts)
+        parts = outgoing_parts(tiles, tile_blocks, tile_pairs, tile_counts)
         parts = lax.all_to_all(parts, ("u", "z"), 0, 0, tiled=True)
     with jax.named_scope("probes"):
         banked = lax.all_gather(bank, "y", axis=0)
@@ -197,14 +213,14 @@
             banked, other, probe_idx.reshape(1, NPROBE), gaps.reshape(1, NPAIR), times, cos_weights
         )
     with jax.named_scope("products"):
-        products = owner_products(parts, probes)
+        products, first_half = owner_products(parts, stay(probes), left_panel)
         products = lax.all_to_all(products, ("u", "z"), 0, 0, tiled=True)
         product = jnp.sum(products.astype(F32), axis=0).astype(BF16)
     with jax.named_scope("spread"):
         both = lax.all_gather(product, "k", axis=0)
         both = lax.all_to_all(jnp.broadcast_to(both, (8,) + both.shape), ("f", "y"), 0, 0, tiled=True)
     with jax.named_scope("response"):
-        turned = screened_response(both, left_panel, weights)
+        turned = screened_response(both, first_half, left_panel, weights)
         return jnp.swapaxes(turned, 1, 2)
 
 

time: 81.9 us -> 81.2 us (level)
    pallas_call x1, Pallas kernels: 5.54 us -> 4.48 us  [outgoing_parts(): pl.pallas_call(kernel, out_shape=jax.ShapeDtypeStruct((NB, ROWS, LANES),...]
where the time goes in v4:
time: 81.2 us; the launch traced here: 80.2 us
  blocking collectives  40.6 us (50%)
  waiting for transfers between devices  14 us (17%)
  Pallas kernels  13.7 us (17%)
  starting transfers between devices  10.3 us (13%)
  local copies, waits for them, and re-layouts  0.86 us (1%)
    all_to_all x1, blocking collectives, shards(): products = lax.all_to_all(products, ('u', 'z'), 0, 0, tiled=True)  14.5 us
    all_gather x1, blocking collectives, shards(): banked = lax.all_gather(bank, 'y', axis=0)  13.3 us
    all_to_all x1, waiting for transfers between devices, shards(): parts = lax.all_to_all(parts, ('u', 'z'), 0, 0, tiled=True)  12.1 us
    all_to_all x1, blocking collectives, shards(): lax.all_to_all(jnp.broadcast_to(both, (8,) + both.shape), ('f', 'y'), 0,...  11 us
    all_to_all x1, starting transfers between devices, shards(): parts = lax.all_to_all(parts, ('u', 'z'), 0, 0, tiled=True)  10.3 us
    pallas_call x1, Pallas kernels, outgoing_parts(): pl.pallas_call(kernel, out_shape=jax.ShapeDtypeStruct((NB, ROWS, LANES),...  4.48 us
    pallas_call x1, Pallas kernels, owner_products(): pl.pallas_call(kernel, out_shape=(jax.ShapeDtypeStruct((NB, SET, MB * PAR...  3.69 us
    pallas_call x1, Pallas kernels, screened_response(): pl.pallas_call(kernel, out_shape=jax.ShapeDtypeStruct((2, SET, 2 * half),...  3.68 us
  transfers between devices with their start and end apart: 2, of which 2 were waited for; matrix products, arithmetic and copies ran while one was open for 0% of the time, Pallas kernels for 2%

profile of v4, /device:TPU:2, one launch (start us, length us, event | category | flops | bytes accessed | tf_op | source)
XLA Modules:
  0.0 80.2 jit_solution(5901601846407067749)
XLA Ops:
  0.7 4.5 %outgoing_parts.1 = bf16[16,272,128]{2,1,0:T(8,128)(2,1)} custom-call(s32[16]{0:T(128)} %bitcast.11, s32[16]{0:T(128)} %pairs_ref.1, s32[1]{0:T(128)S(6)} %copy.11.counts_ref, bf16[16,512,512]{2,1,0:T(8,128)(2,1)} %tiles_ref.1), custom_call_target="tpu_custom_call" | custom-call | tf_op jit(solution)/shard_map/parts/outgoing_parts/pallas_call | solution.py:70
  5.1 0.0 copy-start.5
  5.1 0.0 copy-start.1
  5.2 0.0 copy-start.2
  5.2 0.0 copy-start.3
  5.2 0.0 copy-start.4
  5.2 10.3 %all-to-all-start = ((bf16[16,272,128]{2,1,0:T(8,128)(2,1)}), bf16[16,272,128]{2,1,0:T(8,128)(2,1)S(1)}, u32[]{:S(2)}, u32[]{:S(2)}) async-start(bf16[16,272,128]{2,1,0:T(8,128)(2,1)} %outgoing_parts.1), calls=%async_computation | async-start | bytes 2228224 | tf_op jit(solution)/shard_map/parts/all_to_all | solution.py:208
  15.5 0.0 copy-done.5
  15.5 13.3 %all-gather = bf16[2048,128]{1,0:T(8,128)(2,1)S(1)} all-gather(bf16[512,128]{1,0:T(8,128)(2,1)S(1)} %copy-done.5), channel_id=2, replica_groups=mesh['f'=2,'y'=4,'k'=2,'u'=2,'z'=8] {'y'}, dimensions={0}, use_global_device_ids=true | all-gather | bytes 655360 | tf_op jit(solution)/shard_map/probes/all_gather | solution.py:210
  28.8 0.0 collective-permute-start
  28.8 1.9 %collective-permute-done.other_ref = bf16[4,512,128]{2,1,0:T(8,128)(2,1)S(1)} collective-permute-done((bf16[4,512,128]{2,1,0:T(8,128)(2,1)S(1)}, bf16[4,512,128]{2,1,0:T(8,128)(2,1)S(1)}, u32[]{:S(2)}, u32[]{:S(2)}) %collective-permute-start) | collective-permute-done | bytes 524320 | tf_op jit(solution)/shard_map/probes/ppermute | solution.py:211
  30.7 0.0 copy-done.1
  30.7 0.0 copy-done.2
  30.7 0.0 copy-done.3
  30.7 0.0 copy-done.4
  30.7 1.8 %picked_probes.1 = (bf16[512,512]{1,0:T(8,128)(2,1)S(1)}, f32[2,2048]{1,0:T(2,128)S(1)}) custom-call(f32[4]{0:T(128)S(1)} %copy-done.4, f32[4,4]{1,0:T(4,128)S(1)} %copy-done.2, bf16[4,512,128]{2,1,0:T(8,128)(2,1)S(1)} %bitcast.7, bf16[4,512,128]{2,1,0:T(8,128)(2,1)S(1)} %collective-permute-done.other_ref, s32[1,512]{1,0:T(1,128)S(1)} %bitcast.9, ...), custom_call_target="tpu_custom_call" | custom-call | tf_op jit(solution)/shard_map/probes/picked_probes/pallas_call | solution.py:104
  32.5 0.0 copy-start
  32.6 0.8 %copy-done = bf16[512,512]{1,0:T(8,128)(2,1)} copy-done((bf16[512,512]{1,0:T(8,128)(2,1)}, bf16[512,512]{1,0:T(8,128)(2,1)S(1)}, u32[]{:S(2)}) %copy-start) | copy-done | bytes 524312
  33.4 12.1 %all-to-all-done.parts_ref = bf16[16,272,128]{2,1,0:T(8,128)(2,1)S(1)} async-done(((bf16[16,272,128]{2,1,0:T(8,128)(2,1)}), bf16[16,272,128]{2,1,0:T(8,128)(2,1)S(1)}, u32[]{:S(2)}, u32[]{:S(2)}) %all-to-all-start) | async-done | bytes 1114144 | tf_op jit(solution)/shard_map/parts/all_to_all | solution.py:208
  45.4 3.7 %owner_products.1 = (bf16[16,32,128]{2,1,0:T(8,128)(2,1)S(1)}, bf16[512,2048]{1,0:T(8,128)(2,1)S(1)}) custom-call(bf16[16,272,128]{2,1,0:T(8,128)(2,1)S(1)} %all-to-all-done.parts_ref, bf16[512,512]{1,0:T(8,128)(2,1)} %copy-done, bf16[1024,2048]{1,0:T(8,128)(2,1)} %left_ref.3), custom_call_target="tpu_custom_call" | custom-call | tf_op jit(solution)/shard_map/products/owner_products/pallas_call | solution.py:140
  49.1 14.5 %all_to_all.15 = bf16[16,32,128]{2,1,0:T(8,128)(2,1)S(1)} all-to-all(bf16[16,32,128]{2,1,0:T(8,128)(2,1)S(1)} %get-tuple-element.10), channel_id=1, replica_groups=mesh['f'=2,'y'=4,'k'=2,'u'=2,'z'=8] {'u','z'}, dimensions={0} | all-to-all | bytes 262144 | tf_op jit(solution)/shard_map/products/all_to_all | solution.py:217
  63.7 1.8 %all-gather.1 = bf16[64,128]{1,0:T(8,128)(2,1)S(1)} all-gather(bf16[32,128]{1,0:T(8,128)(2,1)S(1)} %reduce_sum.12), channel_id=3, replica_groups=mesh['f'=2,'y'=4,'k'=2,'u'=2,'z'=8] {'k'}, dimensions={0}, use_global_device_ids=true | all-gather | bytes 24576 | tf_op jit(solution)/shard_map/spread/all_gather | solution.py:220
  65.5 11.0 %all_to_all.16.parts_ref = bf16[8,2,32,128]{3,2,1,0:T(8,128)(2,1)S(1)} all-to-all(bf16[8,2,32,128]{3,2,1,0:T(8,128)(2,1)S(1)} %broadcast_in_dim.3), channel_id=1, replica_groups=mesh['f'=2,'y'=4,'k'=2,'u'=2,'z'=8] {'f','y'}, dimensions={0} | all-to-all | bytes 262144 | tf_op jit(solution)/shard_map/spread/all_to_all | solution.py:221
  76.5 3.7 %screened_response.1 = f32[2,32,1024]{2,1,0:T(8,128)} custom-call(bf16[8,2,32,128]{3,2,1,0:T(8,128)(2,1)S(1)} %all_to_all.16.parts_ref, bf16[512,2048]{1,0:T(8,128)(2,1)S(1)} %get-tuple-element.11.first_ref, bf16[1024,2048]{1,0:T(8,128)(2,1)} %left_ref.3, f32[2,2048]{1,0:T(2,128)S(1)} %get-tuple-element.12.weights_ref), custom_call_target="tpu_custom_call" | custom-call | tf_op jit(solution)/shard_map/response/screened_response/pallas_call | solution.py:186
  (2 shorter events, 0.0 us)
Async XLA Ops:
  5.1 10.3 %copy-start.5 = (bf16[512,128]{1,0:T(8,128)(2,1)S(1)}, bf16[512,128]{1,0:T(8,128)(2,1)}, u32[]{:S(2)}) copy-start(bf16[512,128]{1,0:T(8,128)(2,1)} %param.18) | copy-start | bytes 393220
  5.1 25.6 %copy-start.1 = (f32[2048]{0:T(1024)S(1)}, f32[2048]{0:T(1024)}, u32[]{:S(2)}) copy-start(f32[2048]{0:T(1024)} %param.15) | copy-start | bytes 24580
  5.2 25.6 %copy-start.2 = (f32[4,4]{1,0:T(4,128)S(1)}, f32[4,4]{1,0:T(4,128)}, u32[]{:S(2)}) copy-start(f32[4,4]{1,0:T(4,128)} %cos_ref.1) | copy-start | bytes 196
  5.2 25.5 %copy-start.3 = (s32[512]{0:T(512)S(1)}, s32[512]{0:T(512)}, u32[]{:S(2)}) copy-start(s32[512]{0:T(512)} %param.19) | copy-start | bytes 6148
  5.2 25.5 %copy-start.4 = (f32[4]{0:T(128)S(1)}, f32[4]{0:T(128)}, u32[]{:S(2)}) copy-start(f32[4]{0:T(128)} %times_ref.1) | copy-start | bytes 52
  5.2 40.2 %all-to-all-start = ((bf16[16,272,128]{2,1,0:T(8,128)(2,1)}), bf16[16,272,128]{2,1,0:T(8,128)(2,1)S(1)}, u32[]{:S(2)}, u32[]{:S(2)}) async-start(bf16[16,272,128]{2,1,0:T(8,128)(2,1)} %outgoing_parts.1), calls=%async_computation | async-start | bytes 2228224 | tf_op jit(solution)/shard_map/parts/all_to_all | solution.py:208
  28.8 1.9 %collective-permute-start = (bf16[4,512,128]{2,1,0:T(8,128)(2,1)S(1)}, bf16[4,512,128]{2,1,0:T(8,128)(2,1)S(1)}, u32[]{:S(2)}, u32[]{:S(2)}) collective-permute-start(bf16[4,512,128]{2,1,0:T(8,128)(2,1)S(1)} %bitcast.6), channel_id=1, source_target_pairs={{0,16},{16,0},{1,17},{17,1},{2,18},{18,2},{3,19},{19,3},{4,20},{20... | collective-permute-start | bytes 1572872 | tf_op jit(solution)/shard_map/probes/ppermute | solution.py:211
  32.5 0.8 %copy-start = (bf16[512,512]{1,0:T(8,128)(2,1)}, bf16[512,512]{1,0:T(8,128)(2,1)S(1)}, u32[]{:S(2)}) copy-start(bf16[512,512]{1,0:T(8,128)(2,1)S(1)} %get-tuple-element.9.probes_ref) | copy-start | bytes 1572868

commit v5 on v4

--- a/solution.py
+++ b/solution.py
@@ -83,8 +83,14 @@
     )(blocks, pairs, counts, tiles)
 
 
-def picked_probes(own, other, probe_idx, gaps, times, cos_weights):
-    def kernel(times_ref, cos_ref, own_ref, other_ref, idx_ref, gaps_ref, out_ref, weights_ref):
+def picked_probes(own, other, probe_idx, gaps, times, cos_weights, left_panel):
+    half = left_panel.shape[0] // 2
+
+    def kernel(
+        times_ref, cos_ref, own_ref, other_ref, idx_ref, gaps_ref, left_ref, out_ref, weights_ref, first_ref, sem
+    ):
+        fetch = pltpu.make_async_copy(left_ref.at[pl.ds(0, half), :], first_ref, sem)
+        fetch.start()
         core = lax.axis_index("k")
         total = jnp.zeros((TILE, NPROBE), F32)
         for bank_ref, at in ((own_ref, core), (other_ref, 1 - core)):
@@ -100,28 +106,30 @@
             for k in range(1, 4):
                 weight += decays[k] * cos_ref[first + f, k]
             weights_ref[f : f + 1, :] = weight
-
-    return pl.pallas_call(
-        kernel,
-        out_shape=(jax.ShapeDtypeStruct((TILE, NPROBE), BF16), jax.ShapeDtypeStruct((2, NPAIR), F32)),
-        in_specs=[SMEM, SMEM, VMEM, VMEM, VMEM, VMEM],
-        out_specs=(VMEM, VMEM),
+        fetch.wait()
+
+    return pl.pallas_call(
+        kernel,
+        out_shape=(
+            jax.ShapeDtypeStruct((TILE, NPROBE), BF16),
+            jax.ShapeDtypeStruct((2, NPAIR), F32),
+            jax.ShapeDtypeStruct((half, NPAIR), BF16),
+        ),
+        in_specs=[SMEM, SMEM, VMEM, VMEM, VMEM, VMEM, HBM],
+        out_specs=(VMEM, VMEM, VMEM),
+        scratch_shapes=[pltpu.SemaphoreType.DMA],
         compiler_params=pltpu.CompilerParams(vmem_limit_bytes=24 << 20),
         name="picked_probes",
-    )(times, cos_weights, own, other, probe_idx, gaps)
-
-
-def owner_products(parts, probes, left_panel):
-    half = left_panel.shape[0] // 2
-
-    def kernel(parts_ref, probes_ref, left_ref, out_ref, left_out_ref, held, product, sems):
-        first = pltpu.make_async_copy(probes_ref, held, sems.at[0])
-        first.start()
-        fetch = pltpu.make_async_copy(left_ref.at[pl.ds(0, half), :], left_out_ref, sems.at[1])
+    )(times, cos_weights, own, other, probe_idx, gaps, left_panel)
+
+
+def owner_products(parts, probes):
+    def kernel(parts_ref, probes_ref, out_ref, held, product, sem):
+        fetch = pltpu.make_async_copy(probes_ref, held, sem)
+        fetch.start()
         units = parts_ref[:, : CAP * UNIT, :].reshape(NB * CAP, TILE // LANES, PART, LANES)
         rows = jnp.concatenate([units[:, n] for n in range(TILE // LANES)], axis=-1).reshape(NB * CAP * PART, TILE)
-        first.wait()
-        fetch.start()
+        fetch.wait()
         product[...] = jnp.dot(rows, held[...], preferred_element_type=F32)
         codes = [
             parts_ref[c, CAP * UNIT :, :].astype(F32)[j * (CODE // CAP) : j * (CODE // CAP) + 1, :1]
@@ -135,24 +143,20 @@
             turned = total.T.astype(BF16)
             for c in range(NB):
                 out_ref[c, :, m * PART : (m + 1) * PART] = turned[c * SET : (c + 1) * SET, :]
-        fetch.wait()
-
-    return pl.pallas_call(
-        kernel,
-        out_shape=(
-            jax.ShapeDtypeStruct((NB, SET, MB * PART), BF16),
-            jax.ShapeDtypeStruct((half, NPAIR), BF16),
-        ),
-        in_specs=[VMEM, HBM, HBM],
-        out_specs=(VMEM, VMEM),
+
+    return pl.pallas_call(
+        kernel,
+        out_shape=jax.ShapeDtypeStruct((NB, SET, MB * PART), BF16),
+        in_specs=[VMEM, HBM],
+        out_specs=VMEM,
         scratch_shapes=[
             pltpu.VMEM((TILE, NPROBE), BF16),
             pltpu.VMEM((NB * CAP * PART, NPROBE), F32),
-            pltpu.SemaphoreType.DMA((2,)),
+            pltpu.SemaphoreType.DMA,
         ],
         compiler_params=pltpu.CompilerParams(vmem_limit_bytes=16 << 20),
         name="owner_products",
-    )(parts, probes, left_panel)
+    )(parts, probes)
 
 
 def screened_response(parts, first_half, left_panel, weights):
@@ -209,11 +213,11 @@
     with jax.named_scope("probes"):
         banked = lax.all_gather(bank, "y", axis=0)
         other = lax.ppermute(banked, "k", [(0, 1), (1, 0)])
-        probes, weights = picked_probes(
-            banked, other, probe_idx.reshape(1, NPROBE), gaps.reshape(1, NPAIR), times, cos_weights
+        probes, weights, first_half = picked_probes(
+            banked, other, probe_idx.reshape(1, NPROBE), gaps.reshape(1, NPAIR), times, cos_weights, left_panel
         )
     with jax.named_scope("products"):
-        products, first_half = owner_products(parts, stay(probes), left_panel)
+        products = owner_products(parts, stay(probes))
         products = lax.all_to_all(products, ("u", "z"), 0, 0, tiled=True)
         product = jnp.sum(products.astype(F32), axis=0).astype(BF16)
     with jax.named_scope("spread"):

time: 81.2 us -> 80.1 us (0.986)
    pallas_call x1, Pallas kernels: 3.69 us -> 2.54 us  [owner_products(): pl.pallas_call(kernel, out_shape=jax.ShapeDtypeStruct((NB, SET, MB * PART...]
  transfers between devices with their start and end apart: 2 -> 2, of which waited for: 2 -> 2; matrix products, arithmetic and copies ran while one was open for 0% -> 0% of each run, Pallas kernels for 2% -> 3%
where the time goes in v5:
time: 80.1 us; the launch traced here: 79 us
  blocking collectives  40.6 us (51%)
  waiting for transfers between devices  13.6 us (17%)
  Pallas kernels  12.9 us (16%)
  starting transfers between devices  10.3 us (13%)
  local copies, waits for them, and re-layouts  0.86 us (1%)
    all_to_all x1, blocking collectives, shards(): products = lax.all_to_all(products, ('u', 'z'), 0, 0, tiled=True)  14.5 us
    all_gather x1, blocking collectives, shards(): banked = lax.all_gather(bank, 'y', axis=0)  13.3 us
    all_to_all x1, waiting for transfers between devices, shards(): parts = lax.all_to_all(parts, ('u', 'z'), 0, 0, tiled=True)  11.7 us
    all_to_all x1, blocking collectives, shards(): lax.all_to_all(jnp.broadcast_to(both, (8,) + both.shape), ('f', 'y'), 0,...  11 us
    all_to_all x1, starting transfers between devices, shards(): parts = lax.all_to_all(parts, ('u', 'z'), 0, 0, tiled=True)  10.3 us
    pallas_call x1, Pallas kernels, outgoing_parts(): pl.pallas_call(kernel, out_shape=jax.ShapeDtypeStruct((NB, ROWS, LANES),...  4.47 us
    pallas_call x1, Pallas kernels, screened_response(): pl.pallas_call(kernel, out_shape=jax.ShapeDtypeStruct((2, SET, 2 * half),...  3.67 us
    pallas_call x1, Pallas kernels, owner_products(): pl.pallas_call(kernel, out_shape=jax.ShapeDtypeStruct((NB, SET, MB * PART...  2.54 us
  transfers between devices with their start and end apart: 2, of which 2 were waited for; matrix products, arithmetic and copies ran while one was open for 0% of the time, Pallas kernels for 3%

profile of v5, /device:TPU:2, one launch (start us, length us, event | category | flops | bytes accessed | tf_op | source)
XLA Modules:
  0.0 79.0 jit_solution(4899919805133505084)
XLA Ops:
  0.7 4.5 %outgoing_parts.1 = bf16[16,272,128]{2,1,0:T(8,128)(2,1)} custom-call(s32[16]{0:T(128)} %bitcast.11, s32[16]{0:T(128)} %pairs_ref.1, s32[1]{0:T(128)S(6)} %copy.11.counts_ref, bf16[16,512,512]{2,1,0:T(8,128)(2,1)} %tiles_ref.1), custom_call_target="tpu_custom_call" | custom-call | tf_op jit(solution)/shard_map/parts/outgoing_parts/pallas_call | solution.py:70
  5.1 0.0 copy-start.5
  5.1 0.0 copy-start.1
  5.2 0.0 copy-start.2
  5.2 0.0 copy-start.3
  5.2 0.0 copy-start.4
  5.2 10.3 %all-to-all-start = ((bf16[16,272,128]{2,1,0:T(8,128)(2,1)}), bf16[16,272,128]{2,1,0:T(8,128)(2,1)S(1)}, u32[]{:S(2)}, u32[]{:S(2)}) async-start(bf16[16,272,128]{2,1,0:T(8,128)(2,1)} %outgoing_parts.1), calls=%async_computation | async-start | bytes 2228224 | tf_op jit(solution)/shard_map/parts/all_to_all | solution.py:212
  15.5 0.0 copy-done.5
  15.5 13.3 %all-gather = bf16[2048,128]{1,0:T(8,128)(2,1)S(1)} all-gather(bf16[512,128]{1,0:T(8,128)(2,1)S(1)} %copy-done.5), channel_id=2, replica_groups=mesh['f'=2,'y'=4,'k'=2,'u'=2,'z'=8] {'y'}, dimensions={0}, use_global_device_ids=true | all-gather | bytes 655360 | tf_op jit(solution)/shard_map/probes/all_gather | solution.py:214
  28.8 0.0 collective-permute-start
  28.8 1.9 %collective-permute-done.other_ref = bf16[4,512,128]{2,1,0:T(8,128)(2,1)S(1)} collective-permute-done((bf16[4,512,128]{2,1,0:T(8,128)(2,1)S(1)}, bf16[4,512,128]{2,1,0:T(8,128)(2,1)S(1)}, u32[]{:S(2)}, u32[]{:S(2)}) %collective-permute-start) | collective-permute-done | bytes 524320 | tf_op jit(solution)/shard_map/probes/ppermute | solution.py:215
  30.7 0.0 copy-done.1
  30.7 0.0 copy-done.2
  30.7 0.0 copy-done.3
  30.7 0.0 copy-done.4
  30.7 2.2 %picked_probes.1 = (bf16[512,512]{1,0:T(8,128)(2,1)S(1)}, f32[2,2048]{1,0:T(2,128)S(1)}, bf16[512,2048]{1,0:T(8,128)(2,1)S(1)}) custom-call(f32[4]{0:T(128)S(1)} %copy-done.4, f32[4,4]{1,0:T(4,128)S(1)} %copy-done.2, bf16[4,512,128]{2,1,0:T(8,128)(2,1)S(1)} %bitcast.7, bf16[4,512,128]{2,1,0:T(8,128)(2,1)S(1)} %collective-permute-done.other_ref, ...), custom_call_target="tpu_custom_call" | custom-call | tf_op jit(solution)/shard_map/probes/picked_probes/pallas_call | solution.py:111
  32.9 0.0 copy-start
  32.9 0.8 %copy-done = bf16[512,512]{1,0:T(8,128)(2,1)} copy-done((bf16[512,512]{1,0:T(8,128)(2,1)}, bf16[512,512]{1,0:T(8,128)(2,1)S(1)}, u32[]{:S(2)}) %copy-start) | copy-done | bytes 524312
  33.7 11.7 %all-to-all-done.parts_ref = bf16[16,272,128]{2,1,0:T(8,128)(2,1)S(1)} async-done(((bf16[16,272,128]{2,1,0:T(8,128)(2,1)}), bf16[16,272,128]{2,1,0:T(8,128)(2,1)S(1)}, u32[]{:S(2)}, u32[]{:S(2)}) %all-to-all-start) | async-done | bytes 1114144 | tf_op jit(solution)/shard_map/parts/all_to_all | solution.py:212
  45.4 2.5 %owner_products.1 = bf16[16,32,128]{2,1,0:T(8,128)(2,1)S(1)} custom-call(bf16[16,272,128]{2,1,0:T(8,128)(2,1)S(1)} %all-to-all-done.parts_ref, bf16[512,512]{1,0:T(8,128)(2,1)} %copy-done), custom_call_target="tpu_custom_call" | custom-call | tf_op jit(solution)/shard_map/products/owner_products/pallas_call | solution.py:147
  48.0 14.5 %all_to_all.15 = bf16[16,32,128]{2,1,0:T(8,128)(2,1)S(1)} all-to-all(bf16[16,32,128]{2,1,0:T(8,128)(2,1)S(1)} %owner_products.1), channel_id=1, replica_groups=mesh['f'=2,'y'=4,'k'=2,'u'=2,'z'=8] {'u','z'}, dimensions={0} | all-to-all | bytes 262144 | tf_op jit(solution)/shard_map/products/all_to_all | solution.py:221
  62.5 1.8 %all-gather.1 = bf16[64,128]{1,0:T(8,128)(2,1)S(1)} all-gather(bf16[32,128]{1,0:T(8,128)(2,1)S(1)} %reduce_sum.12), channel_id=3, replica_groups=mesh['f'=2,'y'=4,'k'=2,'u'=2,'z'=8] {'k'}, dimensions={0}, use_global_device_ids=true | all-gather | bytes 24576 | tf_op jit(solution)/shard_map/spread/all_gather | solution.py:224
  64.4 11.0 %all_to_all.16.parts_ref = bf16[8,2,32,128]{3,2,1,0:T(8,128)(2,1)S(1)} all-to-all(bf16[8,2,32,128]{3,2,1,0:T(8,128)(2,1)S(1)} %broadcast_in_dim.3), channel_id=1, replica_groups=mesh['f'=2,'y'=4,'k'=2,'u'=2,'z'=8] {'f','y'}, dimensions={0} | all-to-all | bytes 262144 | tf_op jit(solution)/shard_map/spread/all_to_all | solution.py:225
  75.3 3.7 %screened_response.1 = f32[2,32,1024]{2,1,0:T(8,128)} custom-call(bf16[8,2,32,128]{3,2,1,0:T(8,128)(2,1)S(1)} %all_to_all.16.parts_ref, bf16[512,2048]{1,0:T(8,128)(2,1)S(1)} %get-tuple-element.9.first_ref, bf16[1024,2048]{1,0:T(8,128)(2,1)} %left_ref.3, f32[2,2048]{1,0:T(2,128)S(1)} %get-tuple-element.10.weights_ref), custom_call_target="tpu_custom_call" | custom-call | tf_op jit(solution)/shard_map/response/screened_response/pallas_call | solution.py:190
  (2 shorter events, 0.0 us)
Async XLA Ops:
  5.1 10.3 %copy-start.5 = (bf16[512,128]{1,0:T(8,128)(2,1)S(1)}, bf16[512,128]{1,0:T(8,128)(2,1)}, u32[]{:S(2)}) copy-start(bf16[512,128]{1,0:T(8,128)(2,1)} %param.18) | copy-start | bytes 393220
  5.1 25.6 %copy-start.1 = (f32[2048]{0:T(1024)S(1)}, f32[2048]{0:T(1024)}, u32[]{:S(2)}) copy-start(f32[2048]{0:T(1024)} %param.15) | copy-start | bytes 24580
  5.2 25.6 %copy-start.2 = (f32[4,4]{1,0:T(4,128)S(1)}, f32[4,4]{1,0:T(4,128)}, u32[]{:S(2)}) copy-start(f32[4,4]{1,0:T(4,128)} %cos_ref.1) | copy-start | bytes 196
  5.2 25.5 %copy-start.3 = (s32[512]{0:T(512)S(1)}, s32[512]{0:T(512)}, u32[]{:S(2)}) copy-start(s32[512]{0:T(512)} %param.19) | copy-start | bytes 6148
  5.2 25.5 %copy-start.4 = (f32[4]{0:T(128)S(1)}, f32[4]{0:T(128)}, u32[]{:S(2)}) copy-start(f32[4]{0:T(128)} %times_ref.1) | copy-start | bytes 52
  5.2 40.2 %all-to-all-start = ((bf16[16,272,128]{2,1,0:T(8,128)(2,1)}), bf16[16,272,128]{2,1,0:T(8,128)(2,1)S(1)}, u32[]{:S(2)}, u32[]{:S(2)}) async-start(bf16[16,272,128]{2,1,0:T(8,128)(2,1)} %outgoing_parts.1), calls=%async_computation | async-start | bytes 2228224 | tf_op jit(solution)/shard_map/parts/all_to_all | solution.py:212
  28.8 1.9 %collective-permute-start = (bf16[4,512,128]{2,1,0:T(8,128)(2,1)S(1)}, bf16[4,512,128]{2,1,0:T(8,128)(2,1)S(1)}, u32[]{:S(2)}, u32[]{:S(2)}) collective-permute-start(bf16[4,512,128]{2,1,0:T(8,128)(2,1)S(1)} %bitcast.6), channel_id=1, source_target_pairs={{0,16},{16,0},{1,17},{17,1},{2,18},{18,2},{3,19},{19,3},{4,20},{20... | collective-permute-start | bytes 1572872 | tf_op jit(solution)/shard_map/probes/ppermute | solution.py:215
  32.9 0.8 %copy-start = (bf16[512,512]{1,0:T(8,128)(2,1)}, bf16[512,512]{1,0:T(8,128)(2,1)S(1)}, u32[]{:S(2)}) copy-start(bf16[512,512]{1,0:T(8,128)(2,1)S(1)} %get-tuple-element.8.probes_ref) | copy-start | bytes 1572868

commit v6 on v5

--- a/solution.py
+++ b/solution.py
@@ -30,12 +30,15 @@
 
 
 def outgoing_parts(tiles, blocks, pairs, counts):
-    def kernel(blocks_ref, pairs_ref, counts_ref, tiles_ref, out_ref, held, parts, source, sems):
+    def kernel(blocks_ref, pairs_ref, counts_ref, tiles_ref, out_ref, held, parts, source, placed, sems, out_sems):
         me = place()
         lanes = pl.ds(pl.multiple_of(me // 4 * LANES, LANES), LANES)
 
         def copy(s):
             return pltpu.make_async_copy(tiles_ref.at[s, :, lanes], held.at[s], sems.at[s])
+
+        def sent(d):
+            return pltpu.make_async_copy(placed.at[d], out_ref.at[d], out_sems.at[d])
 
         for s in range(SLOTS):
             copy(s).start()
@@ -63,20 +66,25 @@
                 s = source[d * CAP + j]
                 there = jnp.maximum(s, 0)
                 full = jnp.where(s >= 0, 1.0, 0.0).astype(BF16)
-                out_ref[d, j * UNIT : (j + 1) * UNIT, :] = parts[there] * full
+                placed[d, j * UNIT : (j + 1) * UNIT, :] = parts[there] * full
                 codes.append(pairs_ref[there].astype(F32))
-            out_ref[d, CAP * UNIT :, :] = jnp.where(second, codes[1], codes[0]).astype(BF16)
+            placed[d, CAP * UNIT :, :] = jnp.where(second, codes[1], codes[0]).astype(BF16)
+            sent(d).start()
+        for d in range(NB):
+            sent(d).wait()
 
     return pl.pallas_call(
         kernel,
         out_shape=jax.ShapeDtypeStruct((NB, ROWS, LANES), BF16),
         in_specs=[SMEM, SMEM, SMEM, HBM],
-        out_specs=VMEM,
+        out_specs=HBM,
         scratch_shapes=[
             pltpu.VMEM((SLOTS, TILE, LANES), BF16),
             pltpu.VMEM((SLOTS, UNIT, LANES), BF16),
             pltpu.SMEM((NB * CAP,), jnp.int32),
+            pltpu.VMEM((NB, ROWS, LANES), BF16),
             pltpu.SemaphoreType.DMA((SLOTS,)),
+            pltpu.SemaphoreType.DMA((NB,)),
         ],
         compiler_params=pltpu.CompilerParams(vmem_limit_bytes=8 << 20),
         name="outgoing_parts",
@@ -84,12 +92,12 @@
 
 
 def picked_probes(own, other, probe_idx, gaps, times, cos_weights, left_panel):
-    half = left_panel.shape[0] // 2
+    cut = left_panel.shape[0] // 2
 
     def kernel(
         times_ref, cos_ref, own_ref, other_ref, idx_ref, gaps_ref, left_ref, out_ref, weights_ref, first_ref, sem
     ):
-        fetch = pltpu.make_async_copy(left_ref.at[pl.ds(0, half), :], first_ref, sem)
+        fetch = pltpu.make_async_copy(left_ref.at[pl.ds(0, cut), :], first_ref, sem)
         fetch.start()
         core = lax.axis_index("k")
         total = jnp.zeros((TILE, NPROBE), F32)
@@ -113,7 +121,7 @@
         out_shape=(
             jax.ShapeDtypeStruct((TILE, NPROBE), BF16),
             jax.ShapeDtypeStruct((2, NPAIR), F32),
-            jax.ShapeDtypeStruct((half, NPAIR), BF16),
+            jax.ShapeDtypeStruct((cut, NPAIR), BF16),
         ),
         in_specs=[SMEM, SMEM, VMEM, VMEM, VMEM, VMEM, HBM],
         out_specs=(VMEM, VMEM, VMEM),
@@ -159,15 +167,16 @@
     )(parts, probes)
 
 
-def screened_response(parts, first_half, left_panel, weights):
-    half = first_half.shape[0]
+def screened_response(parts, first, left_panel, weights):
+    cut, rows = first.shape[0], left_panel.shape[0]
 
     def kernel(parts_ref, first_ref, left_ref, weights_ref, out_ref, scaled, second, sem):
-        fetch = pltpu.make_async_copy(left_ref.at[pl.ds(half, half), :], second, sem)
+        fetch = pltpu.make_async_copy(left_ref.at[pl.ds(cut, rows - cut), :], second, sem)
         fetch.start()
+        core = lax.axis_index("k")
         lane = lax.broadcasted_iota(jnp.int32, (SET, LANES), 1) // PART
         for g in range(4):
-            held = [parts_ref[(4 * g + sub) // 2, sub % 2].astype(F32) for sub in range(4)]
+            held = [parts_ref[2 * g + sub // 2, jnp.abs(core - sub % 2)].astype(F32) for sub in range(4)]
             for m in range(MB):
                 whole = held[m]
                 for sub in range(4):
@@ -178,28 +187,28 @@
                     scaled[f * SET : (f + 1) * SET, at : at + LANES] = (
                         whole * weights_ref[f : f + 1, at : at + LANES]
                     ).astype(BF16)
-        for n, left in enumerate((first_ref, second)):
-            if n == 1:
+        for left, start, stop in ((first_ref, 0, cut), (second, cut, rows)):
+            if start == cut:
                 fetch.wait()
             product = lax.dot_general(
                 scaled[...], left[...], (((1,), (1,)), ((), ())), preferred_element_type=F32
             )
-            out_ref[0, :, n * half : (n + 1) * half] = product[:SET]
-            out_ref[1, :, n * half : (n + 1) * half] = product[SET:]
-
-    return pl.pallas_call(
-        kernel,
-        out_shape=jax.ShapeDtypeStruct((2, SET, 2 * half), F32),
+            out_ref[0, :, start:stop] = product[:SET]
+            out_ref[1, :, start:stop] = product[SET:]
+
+    return pl.pallas_call(
+        kernel,
+        out_shape=jax.ShapeDtypeStruct((2, SET, rows), F32),
         in_specs=[VMEM, VMEM, HBM, VMEM],
         out_specs=VMEM,
         scratch_shapes=[
             pltpu.VMEM((2 * SET, NPAIR), BF16),
-            pltpu.VMEM((half, NPAIR), BF16),
+            pltpu.VMEM((rows - cut, NPAIR), BF16),
             pltpu.SemaphoreType.DMA,
         ],
         compiler_params=pltpu.CompilerParams(vmem_limit_bytes=12 << 20),
         name="screened_response",
-    )(parts, first_half, left_panel, weights)
+    )(parts, first, left_panel, weights)
 
 
 def shards(
@@ -213,7 +222,7 @@
     with jax.named_scope("probes"):
         banked = lax.all_gather(bank, "y", axis=0)
         other = lax.ppermute(banked, "k", [(0, 1), (1, 0)])
-        probes, weights, first_half = picked_probes(
+        probes, weights, first = picked_probes(
             banked, other, probe_idx.reshape(1, NPROBE), gaps.reshape(1, NPAIR), times, cos_weights, left_panel
         )
     with jax.named_scope("products"):
@@ -221,10 +230,10 @@
         products = lax.all_to_all(products, ("u", "z"), 0, 0, tiled=True)
         product = jnp.sum(products.astype(F32), axis=0).astype(BF16)
     with jax.named_scope("spread"):
-        both = lax.all_gather(product, "k", axis=0)
+        both = jnp.stack([product, lax.ppermute(product, "k", [(0, 1), (1, 0)])])
         both = lax.all_to_all(jnp.broadcast_to(both, (8,) + both.shape), ("f", "y"), 0, 0, tiled=True)
     with jax.named_scope("response"):
-        turned = screened_response(both, first_half, left_panel, weights)
+        turned = screened_response(both, first, left_panel, weights)
         return jnp.swapaxes(turned, 1, 2)
 
 

time: 80.1 us -> 79.6 us (level)
  blocking collectives: 40.6 us -> 38.8 us
  waiting for transfers between devices: 13.6 us -> 14.7 us
    all_gather x1 -> x0, blocking collectives: 1.81 us -> none  [shards(): both = lax.all_gather(product, 'k', axis=0)]
    ppermute x0 -> x1, waiting for transfers between devices: none -> 1.16 us  [shards(): both = jnp.stack([product, lax.ppermute(product, 'k', [(0, 1), (1, 0)])])]
  transfers between devices with their start and end apart: 2 -> 3, of which waited for: 2 -> 3; matrix products, arithmetic and copies ran while one was open for 0% -> 0% of each run, Pallas kernels for 3% -> 3%
where the time goes in v6:
time: 79.6 us; the launch traced here: 78.6 us
  blocking collectives  38.8 us (49%)
  waiting for transfers between devices  14.7 us (18%)
  Pallas kernels  13.1 us (16%)
  starting transfers between devices  10.4 us (13%)
  local copies, waits for them, and re-layouts  0.86 us (1%)
    all_to_all x1, blocking collectives, shards(): products = lax.all_to_all(products, ('u', 'z'), 0, 0, tiled=True)  14.5 us
    all_gather x1, blocking collectives, shards(): banked = lax.all_gather(bank, 'y', axis=0)  13.3 us
    all_to_all x1, waiting for transfers between devices, shards(): parts = lax.all_to_all(parts, ('u', 'z'), 0, 0, tiled=True)  11.7 us
    all_to_all x1, blocking collectives, shards(): lax.all_to_all(jnp.broadcast_to(both, (8,) + both.shape), ('f', 'y'), 0,...  11 us
    all_to_all x1, starting transfers between devices, shards(): parts = lax.all_to_all(parts, ('u', 'z'), 0, 0, tiled=True)  10.3 us
    pallas_call x1, Pallas kernels, outgoing_parts(): pl.pallas_call(kernel, out_shape=jax.ShapeDtypeStruct((NB, ROWS, LANES),...  4.64 us
    pallas_call x1, Pallas kernels, screened_response(): pl.pallas_call(kernel, out_shape=jax.ShapeDtypeStruct((2, SET, rows), F32...  3.68 us
    pallas_call x1, Pallas kernels, owner_products(): pl.pallas_call(kernel, out_shape=jax.ShapeDtypeStruct((NB, SET, MB * PART...  2.54 us
  transfers between devices with their start and end apart: 3, of which 3 were waited for; matrix products, arithmetic and copies ran while one was open for 0% of the time, Pallas kernels for 3%

profile of v6, /device:TPU:2, one launch (start us, length us, event | category | flops | bytes accessed | tf_op | source)
XLA Modules:
  0.0 78.6 jit_solution(9070298185336239575)
XLA Ops:
  0.7 4.6 %outgoing_parts.1 = bf16[16,272,128]{2,1,0:T(8,128)(2,1)} custom-call(s32[16]{0:T(128)} %bitcast.13, s32[16]{0:T(128)} %pairs_ref.1, s32[1]{0:T(128)S(6)} %copy.11.counts_ref, bf16[16,512,512]{2,1,0:T(8,128)(2,1)} %tiles_ref.1), custom_call_target="tpu_custom_call" | custom-call | tf_op jit(solution)/shard_map/parts/outgoing_parts/pallas_call | solution.py:76
  5.3 0.0 copy-start.5
  5.3 0.0 copy-start.1
  5.3 0.0 copy-start.2
  5.3 0.0 copy-start.3
  5.3 0.0 copy-start.4
  5.4 10.3 %all-to-all-start = ((bf16[16,272,128]{2,1,0:T(8,128)(2,1)}), bf16[16,272,128]{2,1,0:T(8,128)(2,1)S(1)}, u32[]{:S(2)}, u32[]{:S(2)}) async-start(bf16[16,272,128]{2,1,0:T(8,128)(2,1)} %outgoing_parts.1), calls=%async_computation | async-start | bytes 2228224 | tf_op jit(solution)/shard_map/parts/all_to_all | solution.py:221
  15.6 0.0 copy-done.5
  15.7 13.3 %all-gather = bf16[2048,128]{1,0:T(8,128)(2,1)S(1)} all-gather(bf16[512,128]{1,0:T(8,128)(2,1)S(1)} %copy-done.5), channel_id=2, replica_groups=mesh['f'=2,'y'=4,'k'=2,'u'=2,'z'=8] {'y'}, dimensions={0}, use_global_device_ids=true | all-gather | bytes 655360 | tf_op jit(solution)/shard_map/probes/all_gather | solution.py:223
  29.0 0.0 collective-permute-start
  29.0 1.9 %collective-permute-done.other_ref = bf16[4,512,128]{2,1,0:T(8,128)(2,1)S(1)} collective-permute-done((bf16[4,512,128]{2,1,0:T(8,128)(2,1)S(1)}, bf16[4,512,128]{2,1,0:T(8,128)(2,1)S(1)}, u32[]{:S(2)}, u32[]{:S(2)}) %collective-permute-start) | collective-permute-done | bytes 524320 | tf_op jit(solution)/shard_map/probes/ppermute | solution.py:224
  30.9 0.0 copy-done.1
  30.9 0.0 copy-done.2
  30.9 0.0 copy-done.3
  30.9 0.0 copy-done.4
  30.9 2.2 %picked_probes.1 = (bf16[512,512]{1,0:T(8,128)(2,1)S(1)}, f32[2,2048]{1,0:T(2,128)S(1)}, bf16[512,2048]{1,0:T(8,128)(2,1)S(1)}) custom-call(f32[4]{0:T(128)S(1)} %copy-done.4, f32[4,4]{1,0:T(4,128)S(1)} %copy-done.2, bf16[4,512,128]{2,1,0:T(8,128)(2,1)S(1)} %bitcast.8, bf16[4,512,128]{2,1,0:T(8,128)(2,1)S(1)} %collective-permute-done.other_ref, ...), custom_call_target="tpu_custom_call" | custom-call | tf_op jit(solution)/shard_map/probes/picked_probes/pallas_call | solution.py:119
  33.1 0.0 copy-start
  33.1 0.8 %copy-done = bf16[512,512]{1,0:T(8,128)(2,1)} copy-done((bf16[512,512]{1,0:T(8,128)(2,1)}, bf16[512,512]{1,0:T(8,128)(2,1)S(1)}, u32[]{:S(2)}) %copy-start) | copy-done | bytes 524312
  33.9 11.7 %all-to-all-done.parts_ref = bf16[16,272,128]{2,1,0:T(8,128)(2,1)S(1)} async-done(((bf16[16,272,128]{2,1,0:T(8,128)(2,1)}), bf16[16,272,128]{2,1,0:T(8,128)(2,1)S(1)}, u32[]{:S(2)}, u32[]{:S(2)}) %all-to-all-start) | async-done | bytes 1114144 | tf_op jit(solution)/shard_map/parts/all_to_all | solution.py:221
  45.6 2.5 %owner_products.1 = bf16[16,32,128]{2,1,0:T(8,128)(2,1)S(1)} custom-call(bf16[16,272,128]{2,1,0:T(8,128)(2,1)S(1)} %all-to-all-done.parts_ref, bf16[512,512]{1,0:T(8,128)(2,1)} %copy-done), custom_call_target="tpu_custom_call" | custom-call | tf_op jit(solution)/shard_map/products/owner_products/pallas_call | solution.py:155
  48.1 14.5 %all_to_all.15 = bf16[16,32,128]{2,1,0:T(8,128)(2,1)S(1)} all-to-all(bf16[16,32,128]{2,1,0:T(8,128)(2,1)S(1)} %owner_products.1), channel_id=1, replica_groups=mesh['f'=2,'y'=4,'k'=2,'u'=2,'z'=8] {'u','z'}, dimensions={0} | all-to-all | bytes 262144 | tf_op jit(solution)/shard_map/products/all_to_all | solution.py:230
  62.7 0.1 collective-permute-start.1
  62.8 1.2 %collective-permute-done.1 = bf16[32,128]{1,0:T(8,128)(2,1)S(1)} collective-permute-done((bf16[32,128]{1,0:T(8,128)(2,1)S(1)}, bf16[32,128]{1,0:T(8,128)(2,1)S(1)}, u32[]{:S(2)}, u32[]{:S(2)}) %collective-permute-start.1) | collective-permute-done | bytes 8224 | tf_op jit(solution)/shard_map/spread/ppermute | solution.py:233
  64.0 11.0 %all_to_all.16.parts_ref = bf16[8,2,32,128]{3,2,1,0:T(8,128)(2,1)S(1)} all-to-all(bf16[8,2,32,128]{3,2,1,0:T(8,128)(2,1)S(1)} %broadcast_in_dim.3), channel_id=1, replica_groups=mesh['f'=2,'y'=4,'k'=2,'u'=2,'z'=8] {'f','y'}, dimensions={0} | all-to-all | bytes 262144 | tf_op jit(solution)/shard_map/spread/all_to_all | solution.py:234
  75.0 3.7 %screened_response.1 = f32[2,32,1024]{2,1,0:T(8,128)} custom-call(bf16[8,2,32,128]{3,2,1,0:T(8,128)(2,1)S(1)} %all_to_all.16.parts_ref, bf16[512,2048]{1,0:T(8,128)(2,1)S(1)} %get-tuple-element.9.first_ref, bf16[1024,2048]{1,0:T(8,128)(2,1)} %left_ref.3, f32[2,2048]{1,0:T(2,128)S(1)} %get-tuple-element.10.weights_ref), custom_call_target="tpu_custom_call" | custom-call | tf_op jit(solution)/shard_map/response/screened_response/pallas_call | solution.py:199
  (3 shorter events, 0.1 us)
Async XLA Ops:
  5.3 10.3 %copy-start.5 = (bf16[512,128]{1,0:T(8,128)(2,1)S(1)}, bf16[512,128]{1,0:T(8,128)(2,1)}, u32[]{:S(2)}) copy-start(bf16[512,128]{1,0:T(8,128)(2,1)} %param.18) | copy-start | bytes 393220
  5.3 25.6 %copy-start.1 = (f32[2048]{0:T(1024)S(1)}, f32[2048]{0:T(1024)}, u32[]{:S(2)}) copy-start(f32[2048]{0:T(1024)} %param.15) | copy-start | bytes 24580
  5.3 25.6 %copy-start.2 = (f32[4,4]{1,0:T(4,128)S(1)}, f32[4,4]{1,0:T(4,128)}, u32[]{:S(2)}) copy-start(f32[4,4]{1,0:T(4,128)} %cos_ref.1) | copy-start | bytes 196
  5.3 25.5 %copy-start.3 = (s32[512]{0:T(512)S(1)}, s32[512]{0:T(512)}, u32[]{:S(2)}) copy-start(s32[512]{0:T(512)} %param.19) | copy-start | bytes 6148
  5.3 25.5 %copy-start.4 = (f32[4]{0:T(128)S(1)}, f32[4]{0:T(128)}, u32[]{:S(2)}) copy-start(f32[4]{0:T(128)} %times_ref.1) | copy-start | bytes 52
  5.4 40.2 %all-to-all-start = ((bf16[16,272,128]{2,1,0:T(8,128)(2,1)}), bf16[16,272,128]{2,1,0:T(8,128)(2,1)S(1)}, u32[]{:S(2)}, u32[]{:S(2)}) async-start(bf16[16,272,128]{2,1,0:T(8,128)(2,1)} %outgoing_parts.1), calls=%async_computation | async-start | bytes 2228224 | tf_op jit(solution)/shard_map/parts/all_to_all | solution.py:221
  29.0 1.9 %collective-permute-start = (bf16[4,512,128]{2,1,0:T(8,128)(2,1)S(1)}, bf16[4,512,128]{2,1,0:T(8,128)(2,1)S(1)}, u32[]{:S(2)}, u32[]{:S(2)}) collective-permute-start(bf16[4,512,128]{2,1,0:T(8,128)(2,1)S(1)} %bitcast.7), channel_id=1, source_target_pairs={{0,16},{16,0},{1,17},{17,1},{2,18},{18,2},{3,19},{19,3},{4,20},{20... | collective-permute-start | bytes 1572872 | tf_op jit(solution)/shard_map/probes/ppermute | solution.py:224
  33.1 0.8 %copy-start = (bf16[512,512]{1,0:T(8,128)(2,1)}, bf16[512,512]{1,0:T(8,128)(2,1)S(1)}, u32[]{:S(2)}) copy-start(bf16[512,512]{1,0:T(8,128)(2,1)S(1)} %get-tuple-element.8.probes_ref) | copy-start | bytes 1572868
  62.7 1.3 %collective-permute-start.1 = (bf16[32,128]{1,0:T(8,128)(2,1)S(1)}, bf16[32,128]{1,0:T(8,128)(2,1)S(1)}, u32[]{:S(2)}, u32[]{:S(2)}) collective-permute-start(bf16[32,128]{1,0:T(8,128)(2,1)S(1)} %reduce_sum.12), channel_id=1, source_target_pairs={{0,16},{16,0},{1,17},{17,1},{2,18},{18,2},{3,19},{19,3},{4,20},{20... | collective-permute-start | bytes 24584 | tf_op jit(solution)/shard_map/spread/ppermute | solution.py:233

commit v7 on v5

--- a/solution.py
+++ b/solution.py
@@ -13,7 +13,8 @@
 NPAIR = 2048
 NPROBE = 512
 SET = 32
-PART = 32
+PART = 64
+GROUP = 8
 CODE = 16
 LANES = 128
 UNIT = PART * TILE // LANES
@@ -25,14 +26,14 @@
 HBM = pl.BlockSpec(memory_space=pltpu.HBM)
 
 
-def place():
-    return lax.axis_index("f") * 8 + lax.axis_index("y") * 2 + lax.axis_index("k")
+def runs():
+    return [[k * 16 + u * 8 + (2 * k + 4 * h + p) % 8 for u in range(2) for p in range(4)] for k in range(2) for h in range(2)]
 
 
 def outgoing_parts(tiles, blocks, pairs, counts):
     def kernel(blocks_ref, pairs_ref, counts_ref, tiles_ref, out_ref, held, parts, source, sems):
-        me = place()
-        lanes = pl.ds(pl.multiple_of(me // 4 * LANES, LANES), LANES)
+        core = lax.axis_index("k")
+        lanes = pl.ds(pl.multiple_of(lax.axis_index("y") * LANES, LANES), LANES)
 
         def copy(s):
             return pltpu.make_async_copy(tiles_ref.at[s, :, lanes], held.at[s], sems.at[s])
@@ -40,14 +41,19 @@
         for s in range(SLOTS):
             copy(s).start()
         live = counts_ref[0]
-        for d in range(NB * CAP):
+        far = lax.axis_index("f")
+        run = (lax.axis_index("z") + 8 - 2 * core) % 8 // 4
+        for d in range(GROUP * CAP):
             source[d] = -1
         for s in range(SLOTS):
-            at = blocks_ref[s] * CAP
+            block = blocks_ref[s]
+            along = (block % 8 + 8 - 2 * core) % 8
+            mine = jnp.where(along // 4 == run, 0, 1) == far
+            at = (block // 8 * 4 + along % 4) * CAP
             at = jnp.where(source[at] >= 0, at + 1, at)
-            source[at] = jnp.where(s < live, s, source[at])
-
-        wanted = lax.broadcasted_iota(jnp.int32, (PART, LANES), 0) + me % 4 * PART
+            source[at] = jnp.where(jnp.logical_and(s < live, mine), s, source[at])
+
+        wanted = lax.broadcasted_iota(jnp.int32, (PART, LANES), 0) + core * PART
         pick = jnp.where(wanted == lax.broadcasted_iota(jnp.int32, (PART, LANES), 1), 1.0, 0.0).astype(BF16)
         for s in range(SLOTS):
             copy(s).wait()
@@ -57,7 +63,7 @@
                 parts[s, n * PART : (n + 1) * PART, :] = part[:, n * LANES : (n + 1) * LANES].astype(BF16)
 
         second = lax.broadcasted_iota(jnp.int32, (CODE, LANES), 0) >= CODE // CAP
-        for d in range(NB):
+        for d in range(GROUP):
             codes = []
             for j in range(CAP):
                 s = source[d * CAP + j]
@@ -69,13 +75,13 @@
 
     return pl.pallas_call(
         kernel,
-        out_shape=jax.ShapeDtypeStruct((NB, ROWS, LANES), BF16),
+        out_shape=jax.ShapeDtypeStruct((GROUP, ROWS, LANES), BF16),
         in_specs=[SMEM, SMEM, SMEM, HBM],
         out_specs=VMEM,
         scratch_shapes=[
             pltpu.VMEM((SLOTS, TILE, LANES), BF16),
             pltpu.VMEM((SLOTS, UNIT, LANES), BF16),
-            pltpu.SMEM((NB * CAP,), jnp.int32),
+            pltpu.SMEM((GROUP * CAP,), jnp.int32),
             pltpu.SemaphoreType.DMA((SLOTS,)),
         ],
         compiler_params=pltpu.CompilerParams(vmem_limit_bytes=8 << 20),
@@ -86,18 +92,17 @@
 def picked_probes(own, other, probe_idx, gaps, times, cos_weights, left_panel):
     half = left_panel.shape[0] // 2
 
-    def kernel(
-        times_ref, cos_ref, own_ref, other_ref, idx_ref, gaps_ref, left_ref, out_ref, weights_ref, first_ref, sem
-    ):
+    def kernel(times_ref, cos_ref, *refs):
+        bank_refs, (idx_ref, gaps_ref, left_ref, out_ref, weights_ref, first_ref, sem) = refs[:8], refs[8:]
         fetch = pltpu.make_async_copy(left_ref.at[pl.ds(0, half), :], first_ref, sem)
         fetch.start()
-        core = lax.axis_index("k")
+        core, y = lax.axis_index("k"), lax.axis_index("y")
         total = jnp.zeros((TILE, NPROBE), F32)
-        for bank_ref, at in ((own_ref, core), (other_ref, 1 - core)):
-            for y in range(4):
-                here = lax.broadcasted_iota(jnp.int32, (LANES, NPROBE), 0) + (y * 2 + at) * LANES
-                pick = jnp.where(here == idx_ref[...], 1.0, 0.0).astype(BF16)
-                total += jnp.dot(bank_ref[y], pick, preferred_element_type=F32)
+        for n, bank_ref in enumerate(bank_refs):
+            row = (y + 4 - n % 4) % 4 * 2 + (core if n < 4 else 1 - core)
+            here = lax.broadcasted_iota(jnp.int32, (LANES, NPROBE), 0) + row * LANES
+            pick = jnp.where(here == idx_ref[...], 1.0, 0.0).astype(BF16)
+            total += jnp.dot(bank_ref[...], pick, preferred_element_type=F32)
         out_ref[...] = total.astype(BF16)
         first = lax.axis_index("f") * 2
         decays = [jnp.exp(-gaps_ref[...] * times_ref[k]) for k in range(4)]
@@ -115,25 +120,25 @@
             jax.ShapeDtypeStruct((2, NPAIR), F32),
             jax.ShapeDtypeStruct((half, NPAIR), BF16),
         ),
-        in_specs=[SMEM, SMEM, VMEM, VMEM, VMEM, VMEM, HBM],
+        in_specs=[SMEM, SMEM] + [VMEM] * 10 + [HBM],
         out_specs=(VMEM, VMEM, VMEM),
         scratch_shapes=[pltpu.SemaphoreType.DMA],
         compiler_params=pltpu.CompilerParams(vmem_limit_bytes=24 << 20),
         name="picked_probes",
-    )(times, cos_weights, own, other, probe_idx, gaps, left_panel)
+    )(times, cos_weights, *own, *other, probe_idx, gaps, left_panel)
 
 
 def owner_products(parts, probes):
     def kernel(parts_ref, probes_ref, out_ref, held, product, sem):
         fetch = pltpu.make_async_copy(probes_ref, held, sem)
         fetch.start()
-        units = parts_ref[:, : CAP * UNIT, :].reshape(NB * CAP, TILE // LANES, PART, LANES)
-        rows = jnp.concatenate([units[:, n] for n in range(TILE // LANES)], axis=-1).reshape(NB * CAP * PART, TILE)
+        units = parts_ref[:, : CAP * UNIT, :].reshape(GROUP * CAP, TILE // LANES, PART, LANES)
+        rows = jnp.concatenate([units[:, n] for n in range(TILE // LANES)], axis=-1).reshape(GROUP * CAP * PART, TILE)
         fetch.wait()
         product[...] = jnp.dot(rows, held[...], preferred_element_type=F32)
         codes = [
             parts_ref[c, CAP * UNIT :, :].astype(F32)[j * (CODE // CAP) : j * (CODE // CAP) + 1, :1]
-            for c in range(NB)
+            for c in range(GROUP)
             for j in range(CAP)
         ]
         for m in range(MB):
@@ -151,7 +156,7 @@
         out_specs=VMEM,
         scratch_shapes=[
             pltpu.VMEM((TILE, NPROBE), BF16),
-            pltpu.VMEM((NB * CAP * PART, NPROBE), F32),
+            pltpu.VMEM((GROUP * CAP * PART, NPROBE), F32),
             pltpu.SemaphoreType.DMA,
         ],
         compiler_params=pltpu.CompilerParams(vmem_limit_bytes=16 << 20),
@@ -165,15 +170,20 @@
     def kernel(parts_ref, first_ref, left_ref, weights_ref, out_ref, scaled, second, sem):
         fetch = pltpu.make_async_copy(left_ref.at[pl.ds(half, half), :], second, sem)
         fetch.start()
-        lane = lax.broadcasted_iota(jnp.int32, (SET, LANES), 1) // PART
-        for g in range(4):
-            held = [parts_ref[(4 * g + sub) // 2, sub % 2].astype(F32) for sub in range(4)]
+        core = lax.axis_index("k")
+        low = lax.broadcasted_iota(jnp.int32, (SET, LANES), 1) < PART
+        for y in range(4):
+            held = [
+                parts_ref[y, jnp.abs(core - k)].astype(F32) + parts_ref[4 + y, jnp.abs(core - k)].astype(F32)
+                for k in range(2)
+            ]
             for m in range(MB):
-                whole = held[m]
-                for sub in range(4):
-                    if sub != m:
-                        whole = jnp.where(lane == sub, pltpu.roll(held[sub], (sub - m) % 4 * PART, 1), whole)
-                at = (m * 4 + g) * LANES
+                start = m // 2 * LANES
+                both = [held[k][:, start : start + LANES] for k in range(2)]
+                turned = 1 - m % 2
+                both[turned] = pltpu.roll(both[turned], PART, 1)
+                whole = jnp.where(low, both[0], both[1])
+                at = (m * 4 + y) * LANES
                 for f in range(2):
                     scaled[f * SET : (f + 1) * SET, at : at + LANES] = (
                         whole * weights_ref[f : f + 1, at : at + LANES]
@@ -207,21 +217,25 @@
 ):
     stay = lambda array: pltpu.with_memory_space_constraint(array, pltpu.HBM)
     tiles, tile_blocks, tile_pairs, left_panel = map(stay, (tiles, tile_blocks.reshape(SLOTS), tile_pairs, left_panel))
+    swap = [(0, 1), (1, 0)]
     with jax.named_scope("parts"):
         parts = outgoing_parts(tiles, tile_blocks, tile_pairs, tile_counts)
-        parts = lax.all_to_all(parts, ("u", "z"), 0, 0, tiled=True)
+        parts, bank = lax.optimization_barrier((parts, bank))
+        parts = lax.all_to_all(parts, ("k", "u", "z"), 0, 0, tiled=True, axis_index_groups=runs())
     with jax.named_scope("probes"):
-        banked = lax.all_gather(bank, "y", axis=0)
-        other = lax.ppermute(banked, "k", [(0, 1), (1, 0)])
+        owned = [(z, z) for z in range(8)] + [(8 + z, 8 + (z ^ 4)) for z in range(8)]
+        bank = lax.ppermute(bank, ("f", "z"), owned)
+        own = [bank] + [lax.ppermute(bank, "y", [(y, (y + n) % 4) for y in range(4)]) for n in (1, 2, 3)]
+        other = [lax.ppermute(columns, "k", swap) for columns in own]
         probes, weights, first_half = picked_probes(
-            banked, other, probe_idx.reshape(1, NPROBE), gaps.reshape(1, NPAIR), times, cos_weights, left_panel
+            own, other, probe_idx.reshape(1, NPROBE), gaps.reshape(1, NPAIR), times, cos_weights, left_panel
         )
     with jax.named_scope("products"):
         products = owner_products(parts, stay(probes))
         products = lax.all_to_all(products, ("u", "z"), 0, 0, tiled=True)
         product = jnp.sum(products.astype(F32), axis=0).astype(BF16)
     with jax.named_scope("spread"):
-        both = lax.all_gather(product, "k", axis=0)
+        both = jnp.stack([product, lax.ppermute(product, "k", swap)])
         both = lax.all_to_all(jnp.broadcast_to(both, (8,) + both.shape), ("f", "y"), 0, 0, tiled=True)
     with jax.named_scope("response"):
         turned = screened_response(both, first_half, left_panel, weights)

time: 80.1 us -> 93.3 us (1.16)
  waiting for transfers between devices: 13.6 us -> 30.4 us
  blocking collectives: 40.6 us -> 27.5 us
  starting transfers between devices: 10.3 us -> 18.7 us
    ppermute x1 -> x9, waiting for transfers between devices: 1.91 us -> 30.4 us  [the longest x1 21.6 us: shards(): bank = lax.ppermute(bank, ('f', 'z'), owned)]
    all_gather x2 -> x0, blocking collectives: 15.1 us -> none  [the longest x1 13.3 us: shards(): banked = lax.all_gather(bank, 'y', axis=0)]
    all_to_all x1, waiting for transfers between devices: 11.7 us -> 0.01 us  [shards(): lax.all_to_all(parts, ('k', 'u', 'z'), 0, 0, tiled=True, axis_index_group...]
    ppermute x1 -> x9, starting transfers between devices: 0.01 us -> 11.1 us  [the longest x1 6.41 us: shards(): bank = lax.ppermute(bank, ('f', 'z'), owned)]
    all_to_all x1, blocking collectives: 14.5 us -> 18.2 us  [shards(): products = lax.all_to_all(products, ('u', 'z'), 0, 0, tiled=True)]
    all_to_all x1, starting transfers between devices: 10.3 us -> 7.59 us  [shards(): lax.all_to_all(parts, ('k', 'u', 'z'), 0, 0, tiled=True, axis_index_group...]
    all_to_all x1, blocking collectives: 11 us -> 9.31 us  [shards(): lax.all_to_all(jnp.broadcast_to(both, (8,) + both.shape), ('f', 'y'), 0,...]
  transfers between devices with their start and end apart: 2 -> 10, of which waited for: 2 -> 6; matrix products, arithmetic and copies ran while one was open for 0% -> 0% of each run, Pallas kernels for 3% -> 3%
where the time goes in v7:
time: 93.3 us; the launch traced here: 92 us
  waiting for transfers between devices  30.4 us (33%)
  blocking collectives  27.5 us (29%)
  starting transfers between devices  18.7 us (20%)
  Pallas kernels  13.7 us (15%)
    ppermute x1, waiting for transfers between devices, shards(): bank = lax.ppermute(bank, ('f', 'z'), owned)  21.6 us
    all_to_all x1, blocking collectives, shards(): products = lax.all_to_all(products, ('u', 'z'), 0, 0, tiled=True)  18.2 us
    all_to_all x1, blocking collectives, shards(): lax.all_to_all(jnp.broadcast_to(both, (8,) + both.shape), ('f', 'y'), 0,...  9.31 us
    all_to_all x1, starting transfers between devices, shards(): lax.all_to_all(parts, ('k', 'u', 'z'), 0, 0, tiled=True, axis_index_group...  7.59 us
    ppermute x1, starting transfers between devices, shards(): bank = lax.ppermute(bank, ('f', 'z'), owned)  6.41 us
    ppermute x3, waiting for transfers between devices, shards(): lax.ppermute(bank, 'y', [(y, (y + n) % 4) for y in range(4)])  6.26 us
    pallas_call x1, Pallas kernels, outgoing_parts(): pl.pallas_call(kernel, out_shape=jax.ShapeDtypeStruct((GROUP, ROWS, LANES...  4.7 us
    ppermute x3, starting transfers between devices, shards(): lax.ppermute(bank, 'y', [(y, (y + n) % 4) for y in range(4)])  4.61 us
  transfers between devices with their start and end apart: 10, of which 6 were waited for; matrix products, arithmetic and copies ran while one was open for 0% of the time, Pallas kernels for 3%

profile of v7, /device:TPU:2, one launch (start us, length us, event | category | flops | bytes accessed | tf_op | source)
XLA Modules:
  0.0 92.0 jit_solution(7305143328005917063)
XLA Ops:
  0.7 4.7 %outgoing_parts.1 = bf16[8,528,128]{2,1,0:T(8,128)(2,1)} custom-call(s32[16]{0:T(128)} %bitcast.10, s32[16]{0:T(128)} %pairs_ref.1, s32[1]{0:T(128)S(6)} %copy.11.counts_ref, bf16[16,512,512]{2,1,0:T(8,128)(2,1)} %tiles_ref.1), custom_call_target="tpu_custom_call" | custom-call | tf_op jit(solution)/shard_map/parts/outgoing_parts/pallas_call | solution.py:76
  5.4 0.0 copy-start.5
  5.4 0.0 copy-start.1
  5.4 0.0 copy-start.2
  5.4 0.0 copy-start.3
  5.4 0.0 copy-start.4
  5.4 7.6 %all-to-all-start = ((bf16[8,528,128]{2,1,0:T(8,128)(2,1)}), bf16[8,528,128]{2,1,0:T(8,128)(2,1)S(1)}, u32[]{:S(2)}, u32[]{:S(2)}) async-start(bf16[8,528,128]{2,1,0:T(8,128)(2,1)} %outgoing_parts.1), calls=%async_computation | async-start | bytes 2162688 | tf_op jit(solution)/shard_map/parts/all_to_all | solution.py:224
  13.0 0.0 copy-done.5
  13.0 6.4 %collective-permute-start = (bf16[512,128]{1,0:T(8,128)(2,1)S(1)}, bf16[512,128]{1,0:T(8,128)(2,1)S(1)}, u32[]{:S(2)}, u32[]{:S(2)}) collective-permute-start(bf16[512,128]{1,0:T(8,128)(2,1)S(1)} %copy-done.5), channel_id=1, source_target_pairs={{0,0},{1,1},{2,2},{3,3},{4,4},{5,5},{6,6},{7,7},{128,132},{129,133... | collective-permute-start | bytes 393224 | tf_op jit(solution)/shard_map/probes/ppermute | solution.py:227
  19.4 21.6 %collective-permute-done.refs_0_ = bf16[512,128]{1,0:T(8,128)(2,1)S(1)} collective-permute-done((bf16[512,128]{1,0:T(8,128)(2,1)S(1)}, bf16[512,128]{1,0:T(8,128)(2,1)S(1)}, u32[]{:S(2)}, u32[]{:S(2)}) %collective-permute-start) | collective-permute-done | bytes 131104 | tf_op jit(solution)/shard_map/probes/ppermute | solution.py:227
  41.0 3.0 %collective-permute-start.3 = (bf16[512,128]{1,0:T(8,128)(2,1)S(1)}, bf16[512,128]{1,0:T(8,128)(2,1)S(1)}, u32[]{:S(2)}, u32[]{:S(2)}) collective-permute-start(bf16[512,128]{1,0:T(8,128)(2,1)S(1)} %collective-permute-done.refs_0_), channel_id=1, source_target_pairs={{0,96},{32,0},{64,32},{96,64},{1,97},{33,1},{65,33},{97,65},{2,98}... | collective-permute-start | bytes 393224 | tf_op jit(solution)/shard_map/probes/ppermute | solution.py:228
  44.0 0.6 collective-permute-start.2
  44.7 1.0 %collective-permute-start.1 = (bf16[512,128]{1,0:T(8,128)(2,1)S(1)}, bf16[512,128]{1,0:T(8,128)(2,1)S(1)}, u32[]{:S(2)}, u32[]{:S(2)}) collective-permute-start(bf16[512,128]{1,0:T(8,128)(2,1)S(1)} %collective-permute-done.refs_0_), channel_id=1, source_target_pairs={{0,32},{32,64},{64,96},{96,0},{1,33},{33,65},{65,97},{97,1},{2,34}... | collective-permute-start | bytes 393224 | tf_op jit(solution)/shard_map/probes/ppermute | solution.py:228
  45.6 0.0 collective-permute-start.4
  45.6 2.3 %collective-permute-done.3.refs_3_ = bf16[512,128]{1,0:T(8,128)(2,1)S(1)} collective-permute-done((bf16[512,128]{1,0:T(8,128)(2,1)S(1)}, bf16[512,128]{1,0:T(8,128)(2,1)S(1)}, u32[]{:S(2)}, u32[]{:S(2)}) %collective-permute-start.3) | collective-permute-done | bytes 131104 | tf_op jit(solution)/shard_map/probes/ppermute | solution.py:228
  48.0 0.0 collective-permute-start.7
  48.0 2.6 %collective-permute-done.2.refs_2_ = bf16[512,128]{1,0:T(8,128)(2,1)S(1)} collective-permute-done((bf16[512,128]{1,0:T(8,128)(2,1)S(1)}, bf16[512,128]{1,0:T(8,128)(2,1)S(1)}, u32[]{:S(2)}, u32[]{:S(2)}) %collective-permute-start.2) | collective-permute-done | bytes 131104 | tf_op jit(solution)/shard_map/probes/ppermute | solution.py:228
  50.6 0.0 collective-permute-start.6
  50.6 1.3 %collective-permute-done.1.refs_1_ = bf16[512,128]{1,0:T(8,128)(2,1)S(1)} collective-permute-done((bf16[512,128]{1,0:T(8,128)(2,1)S(1)}, bf16[512,128]{1,0:T(8,128)(2,1)S(1)}, u32[]{:S(2)}, u32[]{:S(2)}) %collective-permute-start.1) | collective-permute-done | bytes 131104 | tf_op jit(solution)/shard_map/probes/ppermute | solution.py:228
  51.9 0.0 collective-permute-start.5
  51.9 0.0 collective-permute-done.4.refs_4_
  51.9 0.0 collective-permute-done.7.refs_7_
  51.9 0.0 collective-permute-done.6.refs_6_
  52.0 1.3 %collective-permute-done.5.refs_5_ = bf16[512,128]{1,0:T(8,128)(2,1)S(1)} collective-permute-done((bf16[512,128]{1,0:T(8,128)(2,1)S(1)}, bf16[512,128]{1,0:T(8,128)(2,1)S(1)}, u32[]{:S(2)}, u32[]{:S(2)}) %collective-permute-start.5) | collective-permute-done | bytes 131104 | tf_op jit(solution)/shard_map/probes/ppermute | solution.py:229
  53.3 0.0 copy-done.1
  53.3 0.0 copy-done.2
  53.3 0.0 copy-done.3
  53.3 0.0 copy-done.4
  53.3 2.8 %picked_probes.1 = (bf16[512,512]{1,0:T(8,128)(2,1)S(1)}, f32[2,2048]{1,0:T(2,128)S(1)}, bf16[512,2048]{1,0:T(8,128)(2,1)S(1)}) custom-call(f32[4]{0:T(128)S(1)} %copy-done.4, f32[4,4]{1,0:T(4,128)S(1)} %copy-done.2, bf16[512,128]{1,0:T(8,128)(2,1)S(1)} %collective-permute-done.refs_0_, bf16[512,128]{1,0:T(8,128)(2,1)S(1)} %collective-permute-done.1.refs_1_, ...), custom_call_target="tpu_custom_call" | custom-call | tf_op jit(solution)/shard_map/probes/picked_probes/pallas_call | solution.py:116
  56.1 0.0 copy-start
  56.1 0.8 copy-done
  56.9 0.0 all-to-all-done.parts_ref
  56.9 2.5 %owner_products.1 = bf16[16,32,256]{2,1,0:T(8,128)(2,1)S(1)} custom-call(bf16[8,528,128]{2,1,0:T(8,128)(2,1)S(1)} %all-to-all-done.parts_ref, bf16[512,512]{1,0:T(8,128)(2,1)} %copy-done), custom_call_target="tpu_custom_call" | custom-call | tf_op jit(solution)/shard_map/products/owner_products/pallas_call | solution.py:152
  59.4 18.2 %all_to_all.15 = bf16[16,32,256]{2,1,0:T(8,128)(2,1)S(1)} all-to-all(bf16[16,32,256]{2,1,0:T(8,128)(2,1)S(1)} %owner_products.1), channel_id=1, replica_groups=mesh['f'=2,'y'=4,'k'=2,'u'=2,'z'=8] {'u','z'}, dimensions={0} | all-to-all | bytes 524288 | tf_op jit(solution)/shard_map/products/all_to_all | solution.py:235
  77.7 0.1 collective-permute-start.8
  77.8 1.2 %collective-permute-done.8 = bf16[32,256]{1,0:T(8,128)(2,1)S(1)} collective-permute-done((bf16[32,256]{1,0:T(8,128)(2,1)S(1)}, bf16[32,256]{1,0:T(8,128)(2,1)S(1)}, u32[]{:S(2)}, u32[]{:S(2)}) %collective-permute-start.8) | collective-permute-done | bytes 16416 | tf_op jit(solution)/shard_map/spread/ppermute | solution.py:238
  79.0 9.3 %all_to_all.16.parts_ref = bf16[8,2,32,256]{3,2,1,0:T(8,128)(2,1)S(1)} all-to-all(bf16[8,2,32,256]{3,2,1,0:T(8,128)(2,1)S(1)} %broadcast_in_dim.3), channel_id=1, replica_groups=mesh['f'=2,'y'=4,'k'=2,'u'=2,'z'=8] {'f','y'}, dimensions={0} | all-to-all | bytes 524288 | tf_op jit(solution)/shard_map/spread/all_to_all | solution.py:239
  88.3 3.7 %screened_response.1 = f32[2,32,1024]{2,1,0:T(8,128)} custom-call(bf16[8,2,32,256]{3,2,1,0:T(8,128)(2,1)S(1)} %all_to_all.16.parts_ref, bf16[512,2048]{1,0:T(8,128)(2,1)S(1)} %get-tuple-element.13.first_ref, bf16[1024,2048]{1,0:T(8,128)(2,1)} %left_ref.1, f32[2,2048]{1,0:T(2,128)S(1)} %get-tuple-element.14.weights_ref), custom_call_target="tpu_custom_call" | custom-call | tf_op jit(solution)/shard_map/response/screened_response/pallas_call | solution.py:200
  (3 shorter events, 0.1 us)
Async XLA Ops:
  5.4 7.7 %copy-start.5 = (bf16[512,128]{1,0:T(8,128)(2,1)S(1)}, bf16[512,128]{1,0:T(8,128)(2,1)}, u32[]{:S(2)}) copy-start(bf16[512,128]{1,0:T(8,128)(2,1)} %param.18) | copy-start | bytes 393220
  5.4 47.9 %copy-start.1 = (f32[2048]{0:T(1024)S(1)}, f32[2048]{0:T(1024)}, u32[]{:S(2)}) copy-start(f32[2048]{0:T(1024)} %param.15) | copy-start | bytes 24580
  5.4 47.9 %copy-start.2 = (f32[4,4]{1,0:T(4,128)S(1)}, f32[4,4]{1,0:T(4,128)}, u32[]{:S(2)}) copy-start(f32[4,4]{1,0:T(4,128)} %cos_ref.1) | copy-start | bytes 196
  5.4 47.9 %copy-start.3 = (s32[512]{0:T(512)S(1)}, s32[512]{0:T(512)}, u32[]{:S(2)}) copy-start(s32[512]{0:T(512)} %param.19) | copy-start | bytes 6148
  5.4 47.9 %copy-start.4 = (f32[4]{0:T(128)S(1)}, f32[4]{0:T(128)}, u32[]{:S(2)}) copy-start(f32[4]{0:T(128)} %times_ref.1) | copy-start | bytes 52
  5.4 51.5 %all-to-all-start = ((bf16[8,528,128]{2,1,0:T(8,128)(2,1)}), bf16[8,528,128]{2,1,0:T(8,128)(2,1)S(1)}, u32[]{:S(2)}, u32[]{:S(2)}) async-start(bf16[8,528,128]{2,1,0:T(8,128)(2,1)} %outgoing_parts.1), calls=%async_computation | async-start | bytes 2162688 | tf_op jit(solution)/shard_map/parts/all_to_all | solution.py:224
  13.0 28.0 %collective-permute-start = (bf16[512,128]{1,0:T(8,128)(2,1)S(1)}, bf16[512,128]{1,0:T(8,128)(2,1)S(1)}, u32[]{:S(2)}, u32[]{:S(2)}) collective-permute-start(bf16[512,128]{1,0:T(8,128)(2,1)S(1)} %copy-done.5), channel_id=1, source_target_pairs={{0,0},{1,1},{2,2},{3,3},{4,4},{5,5},{6,6},{7,7},{128,132},{129,133... | collective-permute-start | bytes 393224 | tf_op jit(solution)/shard_map/probes/ppermute | solution.py:227
  41.0 6.9 %collective-permute-start.3 = (bf16[512,128]{1,0:T(8,128)(2,1)S(1)}, bf16[512,128]{1,0:T(8,128)(2,1)S(1)}, u32[]{:S(2)}, u32[]{:S(2)}) collective-permute-start(bf16[512,128]{1,0:T(8,128)(2,1)S(1)} %collective-permute-done.refs_0_), channel_id=1, source_target_pairs={{0,96},{32,0},{64,32},{96,64},{1,97},{33,1},{65,33},{97,65},{2,98}... | collective-permute-start | bytes 393224 | tf_op jit(solution)/shard_map/probes/ppermute | solution.py:228
  44.0 6.6 %collective-permute-start.2 = (bf16[512,128]{1,0:T(8,128)(2,1)S(1)}, bf16[512,128]{1,0:T(8,128)(2,1)S(1)}, u32[]{:S(2)}, u32[]{:S(2)}) collective-permute-start(bf16[512,128]{1,0:T(8,128)(2,1)S(1)} %collective-permute-done.refs_0_), channel_id=1, source_target_pairs={{0,64},{32,96},{64,0},{96,32},{1,65},{33,97},{65,1},{97,33},{2,66}... | collective-permute-start | bytes 393224 | tf_op jit(solution)/shard_map/probes/ppermute | solution.py:228
  44.7 7.2 %collective-permute-start.1 = (bf16[512,128]{1,0:T(8,128)(2,1)S(1)}, bf16[512,128]{1,0:T(8,128)(2,1)S(1)}, u32[]{:S(2)}, u32[]{:S(2)}) collective-permute-start(bf16[512,128]{1,0:T(8,128)(2,1)S(1)} %collective-permute-done.refs_0_), channel_id=1, source_target_pairs={{0,32},{32,64},{64,96},{96,0},{1,33},{33,65},{65,97},{97,1},{2,34}... | collective-permute-start | bytes 393224 | tf_op jit(solution)/shard_map/probes/ppermute | solution.py:228
  45.6 6.3 %collective-permute-start.4 = (bf16[512,128]{1,0:T(8,128)(2,1)S(1)}, bf16[512,128]{1,0:T(8,128)(2,1)S(1)}, u32[]{:S(2)}, u32[]{:S(2)}) collective-permute-start(bf16[512,128]{1,0:T(8,128)(2,1)S(1)} %collective-permute-done.refs_0_), channel_id=1, source_target_pairs={{0,16},{16,0},{1,17},{17,1},{2,18},{18,2},{3,19},{19,3},{4,20},{20... | collective-permute-start | bytes 393224 | tf_op jit(solution)/shard_map/probes/ppermute | solution.py:229
  48.0 4.0 %collective-permute-start.7 = (bf16[512,128]{1,0:T(8,128)(2,1)S(1)}, bf16[512,128]{1,0:T(8,128)(2,1)S(1)}, u32[]{:S(2)}, u32[]{:S(2)}) collective-permute-start(bf16[512,128]{1,0:T(8,128)(2,1)S(1)} %collective-permute-done.3.refs_3_), channel_id=1, source_target_pairs={{0,16},{16,0},{1,17},{17,1},{2,18},{18,2},{3,19},{19,3},{4,20},{20... | collective-permute-start | bytes 393224 | tf_op jit(solution)/shard_map/probes/ppermute | solution.py:229
  50.6 1.3 %collective-permute-start.6 = (bf16[512,128]{1,0:T(8,128)(2,1)S(1)}, bf16[512,128]{1,0:T(8,128)(2,1)S(1)}, u32[]{:S(2)}, u32[]{:S(2)}) collective-permute-start(bf16[512,128]{1,0:T(8,128)(2,1)S(1)} %collective-permute-done.2.refs_2_), channel_id=1, source_target_pairs={{0,16},{16,0},{1,17},{17,1},{2,18},{18,2},{3,19},{19,3},{4,20},{20... | collective-permute-start | bytes 393224 | tf_op jit(solution)/shard_map/probes/ppermute | solution.py:229
  51.9 1.3 %collective-permute-start.5 = (bf16[512,128]{1,0:T(8,128)(2,1)S(1)}, bf16[512,128]{1,0:T(8,128)(2,1)S(1)}, u32[]{:S(2)}, u32[]{:S(2)}) collective-permute-start(bf16[512,128]{1,0:T(8,128)(2,1)S(1)} %collective-permute-done.1.refs_1_), channel_id=1, source_target_pairs={{0,16},{16,0},{1,17},{17,1},{2,18},{18,2},{3,19},{19,3},{4,20},{20... | collective-permute-start | bytes 393224 | tf_op jit(solution)/shard_map/probes/ppermute | solution.py:229
  56.1 0.8 copy-start
  77.7 1.3 %collective-permute-start.8 = (bf16[32,256]{1,0:T(8,128)(2,1)S(1)}, bf16[32,256]{1,0:T(8,128)(2,1)S(1)}, u32[]{:S(2)}, u32[]{:S(2)}) collective-permute-start(bf16[32,256]{1,0:T(8,128)(2,1)S(1)} %reduce_sum.12), channel_id=1, source_target_pairs={{0,16},{16,0},{1,17},{17,1},{2,18},{18,2},{3,19},{19,3},{4,20},{20... | collective-permute-start | bytes 49160 | tf_op jit(solution)/shard_map/spread/ppermute | solution.py:238

commit v8 on v7

--- a/solution.py
+++ b/solution.py
@@ -219,12 +219,12 @@
     tiles, tile_blocks, tile_pairs, left_panel = map(stay, (tiles, tile_blocks.reshape(SLOTS), tile_pairs, left_panel))
     swap = [(0, 1), (1, 0)]
     with jax.named_scope("parts"):
+        owned = [(z, z) for z in range(8)] + [(8 + z, 8 + (z ^ 4)) for z in range(8)]
+        bank = lax.ppermute(bank, ("f", "z"), owned)
         parts = outgoing_parts(tiles, tile_blocks, tile_pairs, tile_counts)
-        parts, bank = lax.optimization_barrier((parts, bank))
+        parts = lax.dynamic_update_slice(parts, bank[None, :1, :], (0, ROWS - 1, 0))
         parts = lax.all_to_all(parts, ("k", "u", "z"), 0, 0, tiled=True, axis_index_groups=runs())
     with jax.named_scope("probes"):
-        owned = [(z, z) for z in range(8)] + [(8 + z, 8 + (z ^ 4)) for z in range(8)]
-        bank = lax.ppermute(bank, ("f", "z"), owned)
         own = [bank] + [lax.ppermute(bank, "y", [(y, (y + n) % 4) for y in range(4)]) for n in (1, 2, 3)]
         other = [lax.ppermute(columns, "k", swap) for columns in own]
         probes, weights, first_half = picked_probes(

time: 93.3 us -> 81.9 us (0.88)
  waiting for transfers between devices: 30.4 us -> 8.53 us
  starting transfers between devices: 18.7 us -> 27.8 us
  local copies, waits for them, and re-layouts: 0.86 us -> 2.15 us
    ppermute x1, waiting for transfers between devices: 21.6 us -> 0.01 us  [shards(): bank = lax.ppermute(bank, ('f', 'z'), owned)]
    ppermute x4, starting transfers between devices: 0.01 us -> 7.47 us  [shards(): other = [lax.ppermute(columns, 'k', swap) for columns in own]]
    all_to_all x1, waiting for transfers between devices: 0.01 us -> 4.81 us  [shards(): lax.all_to_all(parts, ('k', 'u', 'z'), 0, 0, tiled=True, axis_index_group...]
    ppermute x3, waiting for transfers between devices: 6.26 us -> 1.73 us  [shards(): lax.ppermute(bank, 'y', [(y, (y + n) % 4) for y in range(4)])]
    all_to_all x1, blocking collectives: 9.31 us -> 12 us  [shards(): lax.all_to_all(jnp.broadcast_to(both, (8,) + both.shape), ('f', 'y'), 0,...]
    ppermute x1, starting transfers between devices: 6.41 us -> 9.08 us  [shards(): bank = lax.ppermute(bank, ('f', 'z'), owned)]
    all_to_all x1, blocking collectives: 18.2 us -> 15.8 us  [shards(): products = lax.all_to_all(products, ('u', 'z'), 0, 0, tiled=True)]
    all_to_all x1, starting transfers between devices: 7.59 us -> 5.8 us  [shards(): lax.all_to_all(parts, ('k', 'u', 'z'), 0, 0, tiled=True, axis_index_group...]
  transfers between devices with their start and end apart: 10 -> 10, of which waited for: 6 -> 5; matrix products, arithmetic and copies ran while one was open for 0% -> 0% of each run, Pallas kernels for 3% -> 9%
where the time goes in v8:
time: 81.9 us; the launch traced here: 80.8 us
  starting transfers between devices  27.8 us (34%)
  blocking collectives  27.8 us (34%)
  Pallas kernels  13.7 us (17%)
  waiting for transfers between devices  8.53 us (10%)
  local copies, waits for them, and re-layouts  2.15 us (3%)
    all_to_all x1, blocking collectives, shards(): products = lax.all_to_all(products, ('u', 'z'), 0, 0, tiled=True)  15.8 us
    all_to_all x1, blocking collectives, shards(): lax.all_to_all(jnp.broadcast_to(both, (8,) + both.shape), ('f', 'y'), 0,...  12 us
    ppermute x1, starting transfers between devices, shards(): bank = lax.ppermute(bank, ('f', 'z'), owned)  9.08 us
    ppermute x4, starting transfers between devices, shards(): other = [lax.ppermute(columns, 'k', swap) for columns in own]  7.47 us
    all_to_all x1, starting transfers between devices, shards(): lax.all_to_all(parts, ('k', 'u', 'z'), 0, 0, tiled=True, axis_index_group...  5.8 us
    all_to_all x1, waiting for transfers between devices, shards(): lax.all_to_all(parts, ('k', 'u', 'z'), 0, 0, tiled=True, axis_index_group...  4.81 us
    pallas_call x1, Pallas kernels, outgoing_parts(): pl.pallas_call(kernel, out_shape=jax.ShapeDtypeStruct((GROUP, ROWS, LANES...  4.69 us
    ppermute x3, starting transfers between devices, shards(): lax.ppermute(bank, 'y', [(y, (y + n) % 4) for y in range(4)])  4.61 us
  transfers between devices with their start and end apart: 10, of which 5 were waited for; matrix products, arithmetic and copies ran while one was open for 0% of the time, Pallas kernels for 9%

profile of v8, /device:TPU:2, one launch (start us, length us, event | category | flops | bytes accessed | tf_op | source)
XLA Modules:
  0.0 80.8 jit_solution(9281501005390700425)
XLA Ops:
  0.0 9.1 %collective-permute-start = (bf16[512,128]{1,0:T(8,128)(2,1)}, bf16[512,128]{1,0:T(8,128)(2,1)S(1)}, u32[]{:S(2)}, u32[]{:S(2)}) collective-permute-start(bf16[512,128]{1,0:T(8,128)(2,1)} %param.18), channel_id=1, source_target_pairs={{0,0},{1,1},{2,2},{3,3},{4,4},{5,5},{6,6},{7,7},{128,132},{129,133... | collective-permute-start | bytes 393224 | tf_op jit(solution)/shard_map/parts/ppermute | solution.py:223
  9.7 4.7 %outgoing_parts.1 = bf16[8,528,128]{2,1,0:T(8,128)(2,1)} custom-call(s32[16]{0:T(128)} %bitcast.12, s32[16]{0:T(128)} %pairs_ref.1, s32[1]{0:T(128)S(6)} %copy.12.counts_ref, bf16[16,512,512]{2,1,0:T(8,128)(2,1)} %tiles_ref.1), custom_call_target="tpu_custom_call" | custom-call | tf_op jit(solution)/shard_map/parts/outgoing_parts/pallas_call | solution.py:76
  14.4 0.0 copy-start.1
  14.4 0.0 copy-start.2
  14.5 0.0 copy-start.3
  14.5 0.0 copy-start.4
  14.5 0.0 collective-permute-done.refs_0_
  14.5 1.3 %dynamic_update_slice.3 = bf16[8,528,128]{2,1,0:T(8,128)(2,1)} dynamic-update-slice(bf16[8,528,128]{2,1,0:T(8,128)(2,1)} %outgoing_parts.1, bf16[1,1,128]{2,1,0:T(2,128)(2,1)S(1)} %slice_bitcast_fusion, s32[]{:T(128)} %constant.1.clone.1, s32[]{:T(128)} %constant.2.clone.1, s32[]{:T(128)} %constant.1.clone.1) | dynamic-update-slice | bytes 516 | tf_op jit(solution)/shard_map/parts/dynamic_update_slice | solution.py:225
  15.8 5.8 %all-to-all-start = ((bf16[8,528,128]{2,1,0:T(8,128)(2,1)}), bf16[8,528,128]{2,1,0:T(8,128)(2,1)S(1)}, u32[]{:S(2)}, u32[]{:S(2)}) async-start(bf16[8,528,128]{2,1,0:T(8,128)(2,1)} %dynamic_update_slice.3), calls=%async_computation | async-start | bytes 2162688 | tf_op jit(solution)/shard_map/parts/all_to_all | solution.py:226
  21.6 3.0 %collective-permute-start.3 = (bf16[512,128]{1,0:T(8,128)(2,1)S(1)}, bf16[512,128]{1,0:T(8,128)(2,1)S(1)}, u32[]{:S(2)}, u32[]{:S(2)}) collective-permute-start(bf16[512,128]{1,0:T(8,128)(2,1)S(1)} %collective-permute-done.refs_0_), channel_id=1, source_target_pairs={{0,96},{32,0},{64,32},{96,64},{1,97},{33,1},{65,33},{97,65},{2,98}... | collective-permute-start | bytes 393224 | tf_op jit(solution)/shard_map/probes/ppermute | solution.py:228
  24.6 0.6 collective-permute-start.2
  25.2 1.0 %collective-permute-start.1 = (bf16[512,128]{1,0:T(8,128)(2,1)S(1)}, bf16[512,128]{1,0:T(8,128)(2,1)S(1)}, u32[]{:S(2)}, u32[]{:S(2)}) collective-permute-start(bf16[512,128]{1,0:T(8,128)(2,1)S(1)} %collective-permute-done.refs_0_), channel_id=1, source_target_pairs={{0,32},{32,64},{64,96},{96,0},{1,33},{33,65},{65,97},{97,1},{2,34}... | collective-permute-start | bytes 393224 | tf_op jit(solution)/shard_map/probes/ppermute | solution.py:228
  26.2 1.4 %collective-permute-start.4 = (bf16[512,128]{1,0:T(8,128)(2,1)S(1)}, bf16[512,128]{1,0:T(8,128)(2,1)S(1)}, u32[]{:S(2)}, u32[]{:S(2)}) collective-permute-start(bf16[512,128]{1,0:T(8,128)(2,1)S(1)} %collective-permute-done.refs_0_), channel_id=1, source_target_pairs={{0,16},{16,0},{1,17},{17,1},{2,18},{18,2},{3,19},{19,3},{4,20},{20... | collective-permute-start | bytes 393224 | tf_op jit(solution)/shard_map/probes/ppermute | solution.py:229
  27.6 0.0 collective-permute-done.3.refs_3_
  27.6 3.8 %collective-permute-start.7 = (bf16[512,128]{1,0:T(8,128)(2,1)S(1)}, bf16[512,128]{1,0:T(8,128)(2,1)S(1)}, u32[]{:S(2)}, u32[]{:S(2)}) collective-permute-start(bf16[512,128]{1,0:T(8,128)(2,1)S(1)} %collective-permute-done.3.refs_3_), channel_id=1, source_target_pairs={{0,16},{16,0},{1,17},{17,1},{2,18},{18,2},{3,19},{19,3},{4,20},{20... | collective-permute-start | bytes 393224 | tf_op jit(solution)/shard_map/probes/ppermute | solution.py:229
  31.4 0.1 collective-permute-done.2.refs_2_
  31.5 2.1 %collective-permute-start.6 = (bf16[512,128]{1,0:T(8,128)(2,1)S(1)}, bf16[512,128]{1,0:T(8,128)(2,1)S(1)}, u32[]{:S(2)}, u32[]{:S(2)}) collective-permute-start(bf16[512,128]{1,0:T(8,128)(2,1)S(1)} %collective-permute-done.2.refs_2_), channel_id=1, source_target_pairs={{0,16},{16,0},{1,17},{17,1},{2,18},{18,2},{3,19},{19,3},{4,20},{20... | collective-permute-start | bytes 393224 | tf_op jit(solution)/shard_map/probes/ppermute | solution.py:229
  33.6 1.6 %collective-permute-done.1.refs_1_ = bf16[512,128]{1,0:T(8,128)(2,1)S(1)} collective-permute-done((bf16[512,128]{1,0:T(8,128)(2,1)S(1)}, bf16[512,128]{1,0:T(8,128)(2,1)S(1)}, u32[]{:S(2)}, u32[]{:S(2)}) %collective-permute-start.1) | collective-permute-done | bytes 131104 | tf_op jit(solution)/shard_map/probes/ppermute | solution.py:228
  35.2 0.2 collective-permute-start.5
  35.4 0.0 collective-permute-done.4.refs_4_
  35.4 0.0 collective-permute-done.7.refs_7_
  35.4 0.0 collective-permute-done.6.refs_6_
  35.4 1.1 %collective-permute-done.5.refs_5_ = bf16[512,128]{1,0:T(8,128)(2,1)S(1)} collective-permute-done((bf16[512,128]{1,0:T(8,128)(2,1)S(1)}, bf16[512,128]{1,0:T(8,128)(2,1)S(1)}, u32[]{:S(2)}, u32[]{:S(2)}) %collective-permute-start.5) | collective-permute-done | bytes 131104 | tf_op jit(solution)/shard_map/probes/ppermute | solution.py:229
  36.6 0.0 copy-done.1
  36.6 0.0 copy-done.2
  36.6 0.0 copy-done.3
  36.6 0.0 copy-done.4
  36.6 2.8 %picked_probes.1 = (bf16[512,512]{1,0:T(8,128)(2,1)S(1)}, f32[2,2048]{1,0:T(2,128)S(1)}, bf16[512,2048]{1,0:T(8,128)(2,1)S(1)}) custom-call(f32[4]{0:T(128)S(1)} %copy-done.4, f32[4,4]{1,0:T(4,128)S(1)} %copy-done.2, bf16[512,128]{1,0:T(8,128)(2,1)S(1)} %collective-permute-done.refs_0_, bf16[512,128]{1,0:T(8,128)(2,1)S(1)} %collective-permute-done.1.refs_1_, ...), custom_call_target="tpu_custom_call" | custom-call | tf_op jit(solution)/shard_map/probes/picked_probes/pallas_call | solution.py:116
  39.4 0.0 copy-start
  39.4 0.8 %copy-done = bf16[512,512]{1,0:T(8,128)(2,1)} copy-done((bf16[512,512]{1,0:T(8,128)(2,1)}, bf16[512,512]{1,0:T(8,128)(2,1)S(1)}, u32[]{:S(2)}) %copy-start) | copy-done | bytes 524312
  40.2 4.8 %all-to-all-done.parts_ref = bf16[8,528,128]{2,1,0:T(8,128)(2,1)S(1)} async-done(((bf16[8,528,128]{2,1,0:T(8,128)(2,1)}), bf16[8,528,128]{2,1,0:T(8,128)(2,1)S(1)}, u32[]{:S(2)}, u32[]{:S(2)}) %all-to-all-start) | async-done | bytes 1081376 | tf_op jit(solution)/shard_map/parts/all_to_all | solution.py:226
  45.0 2.5 %owner_products.1 = bf16[16,32,256]{2,1,0:T(8,128)(2,1)S(1)} custom-call(bf16[8,528,128]{2,1,0:T(8,128)(2,1)S(1)} %all-to-all-done.parts_ref, bf16[512,512]{1,0:T(8,128)(2,1)} %copy-done), custom_call_target="tpu_custom_call" | custom-call | tf_op jit(solution)/shard_map/products/owner_products/pallas_call | solution.py:152
  47.5 15.8 %all_to_all.15 = bf16[16,32,256]{2,1,0:T(8,128)(2,1)S(1)} all-to-all(bf16[16,32,256]{2,1,0:T(8,128)(2,1)S(1)} %owner_products.1), channel_id=1, replica_groups=mesh['f'=2,'y'=4,'k'=2,'u'=2,'z'=8] {'u','z'}, dimensions={0} | all-to-all | bytes 524288 | tf_op jit(solution)/shard_map/products/all_to_all | solution.py:235
  63.4 0.8 %collective-permute-start.8 = (bf16[32,256]{1,0:T(8,128)(2,1)S(1)}, bf16[32,256]{1,0:T(8,128)(2,1)S(1)}, u32[]{:S(2)}, u32[]{:S(2)}) collective-permute-start(bf16[32,256]{1,0:T(8,128)(2,1)S(1)} %reduce_sum.12), channel_id=1, source_target_pairs={{0,16},{16,0},{1,17},{17,1},{2,18},{18,2},{3,19},{19,3},{4,20},{20... | collective-permute-start | bytes 49160 | tf_op jit(solution)/shard_map/spread/ppermute | solution.py:238
  64.2 0.8 %collective-permute-done.8 = bf16[32,256]{1,0:T(8,128)(2,1)S(1)} collective-permute-done((bf16[32,256]{1,0:T(8,128)(2,1)S(1)}, bf16[32,256]{1,0:T(8,128)(2,1)S(1)}, u32[]{:S(2)}, u32[]{:S(2)}) %collective-permute-start.8) | collective-permute-done | bytes 16416 | tf_op jit(solution)/shard_map/spread/ppermute | solution.py:238
  65.1 12.0 %all_to_all.16.parts_ref = bf16[8,2,32,256]{3,2,1,0:T(8,128)(2,1)S(1)} all-to-all(bf16[8,2,32,256]{3,2,1,0:T(8,128)(2,1)S(1)} %broadcast_in_dim.7), channel_id=1, replica_groups=mesh['f'=2,'y'=4,'k'=2,'u'=2,'z'=8] {'f','y'}, dimensions={0} | all-to-all | bytes 524288 | tf_op jit(solution)/shard_map/spread/all_to_all | solution.py:239
  77.1 3.7 %screened_response.1 = f32[2,32,1024]{2,1,0:T(8,128)} custom-call(bf16[8,2,32,256]{3,2,1,0:T(8,128)(2,1)S(1)} %all_to_all.16.parts_ref, bf16[512,2048]{1,0:T(8,128)(2,1)S(1)} %get-tuple-element.9.first_ref, bf16[1024,2048]{1,0:T(8,128)(2,1)} %left_ref.1, f32[2,2048]{1,0:T(2,128)S(1)} %get-tuple-element.10.weights_ref), custom_call_target="tpu_custom_call" | custom-call | tf_op jit(solution)/shard_map/response/screened_response/pallas_call | solution.py:200
  (4 shorter events, 0.1 us)
Async XLA Ops:
  0.0 14.5 %collective-permute-start = (bf16[512,128]{1,0:T(8,128)(2,1)}, bf16[512,128]{1,0:T(8,128)(2,1)S(1)}, u32[]{:S(2)}, u32[]{:S(2)}) collective-permute-start(bf16[512,128]{1,0:T(8,128)(2,1)} %param.18), channel_id=1, source_target_pairs={{0,0},{1,1},{2,2},{3,3},{4,4},{5,5},{6,6},{7,7},{128,132},{129,133... | collective-permute-start | bytes 393224 | tf_op jit(solution)/shard_map/parts/ppermute | solution.py:223
  14.4 22.1 %copy-start.1 = (f32[2048]{0:T(1024)S(1)}, f32[2048]{0:T(1024)}, u32[]{:S(2)}) copy-start(f32[2048]{0:T(1024)} %param.15) | copy-start | bytes 24580
  14.4 22.1 %copy-start.2 = (f32[4,4]{1,0:T(4,128)S(1)}, f32[4,4]{1,0:T(4,128)}, u32[]{:S(2)}) copy-start(f32[4,4]{1,0:T(4,128)} %cos_ref.1) | copy-start | bytes 196
  14.5 22.1 %copy-start.3 = (s32[512]{0:T(512)S(1)}, s32[512]{0:T(512)}, u32[]{:S(2)}) copy-start(s32[512]{0:T(512)} %param.19) | copy-start | bytes 6148
  14.5 22.1 %copy-start.4 = (f32[4]{0:T(128)S(1)}, f32[4]{0:T(128)}, u32[]{:S(2)}) copy-start(f32[4]{0:T(128)} %times_ref.1) | copy-start | bytes 52
  15.8 29.2 %all-to-all-start = ((bf16[8,528,128]{2,1,0:T(8,128)(2,1)}), bf16[8,528,128]{2,1,0:T(8,128)(2,1)S(1)}, u32[]{:S(2)}, u32[]{:S(2)}) async-start(bf16[8,528,128]{2,1,0:T(8,128)(2,1)} %dynamic_update_slice.3), calls=%async_computation | async-start | bytes 2162688 | tf_op jit(solution)/shard_map/parts/all_to_all | solution.py:226
  21.6 6.1 %collective-permute-start.3 = (bf16[512,128]{1,0:T(8,128)(2,1)S(1)}, bf16[512,128]{1,0:T(8,128)(2,1)S(1)}, u32[]{:S(2)}, u32[]{:S(2)}) collective-permute-start(bf16[512,128]{1,0:T(8,128)(2,1)S(1)} %collective-permute-done.refs_0_), channel_id=1, source_target_pairs={{0,96},{32,0},{64,32},{96,64},{1,97},{33,1},{65,33},{97,65},{2,98}... | collective-permute-start | bytes 393224 | tf_op jit(solution)/shard_map/probes/ppermute | solution.py:228
  24.6 6.9 %collective-permute-start.2 = (bf16[512,128]{1,0:T(8,128)(2,1)S(1)}, bf16[512,128]{1,0:T(8,128)(2,1)S(1)}, u32[]{:S(2)}, u32[]{:S(2)}) collective-permute-start(bf16[512,128]{1,0:T(8,128)(2,1)S(1)} %collective-permute-done.refs_0_), channel_id=1, source_target_pairs={{0,64},{32,96},{64,0},{96,32},{1,65},{33,97},{65,1},{97,33},{2,66}... | collective-permute-start | bytes 393224 | tf_op jit(solution)/shard_map/probes/ppermute | solution.py:228
  25.2 10.0 %collective-permute-start.1 = (bf16[512,128]{1,0:T(8,128)(2,1)S(1)}, bf16[512,128]{1,0:T(8,128)(2,1)S(1)}, u32[]{:S(2)}, u32[]{:S(2)}) collective-permute-start(bf16[512,128]{1,0:T(8,128)(2,1)S(1)} %collective-permute-done.refs_0_), channel_id=1, source_target_pairs={{0,32},{32,64},{64,96},{96,0},{1,33},{33,65},{65,97},{97,1},{2,34}... | collective-permute-start | bytes 393224 | tf_op jit(solution)/shard_map/probes/ppermute | solution.py:228
  26.2 9.2 %collective-permute-start.4 = (bf16[512,128]{1,0:T(8,128)(2,1)S(1)}, bf16[512,128]{1,0:T(8,128)(2,1)S(1)}, u32[]{:S(2)}, u32[]{:S(2)}) collective-permute-start(bf16[512,128]{1,0:T(8,128)(2,1)S(1)} %collective-permute-done.refs_0_), channel_id=1, source_target_pairs={{0,16},{16,0},{1,17},{17,1},{2,18},{18,2},{3,19},{19,3},{4,20},{20... | collective-permute-start | bytes 393224 | tf_op jit(solution)/shard_map/probes/ppermute | solution.py:229
  27.6 7.8 %collective-permute-start.7 = (bf16[512,128]{1,0:T(8,128)(2,1)S(1)}, bf16[512,128]{1,0:T(8,128)(2,1)S(1)}, u32[]{:S(2)}, u32[]{:S(2)}) collective-permute-start(bf16[512,128]{1,0:T(8,128)(2,1)S(1)} %collective-permute-done.3.refs_3_), channel_id=1, source_target_pairs={{0,16},{16,0},{1,17},{17,1},{2,18},{18,2},{3,19},{19,3},{4,20},{20... | collective-permute-start | bytes 393224 | tf_op jit(solution)/shard_map/probes/ppermute | solution.py:229
  31.5 3.9 %collective-permute-start.6 = (bf16[512,128]{1,0:T(8,128)(2,1)S(1)}, bf16[512,128]{1,0:T(8,128)(2,1)S(1)}, u32[]{:S(2)}, u32[]{:S(2)}) collective-permute-start(bf16[512,128]{1,0:T(8,128)(2,1)S(1)} %collective-permute-done.2.refs_2_), channel_id=1, source_target_pairs={{0,16},{16,0},{1,17},{17,1},{2,18},{18,2},{3,19},{19,3},{4,20},{20... | collective-permute-start | bytes 393224 | tf_op jit(solution)/shard_map/probes/ppermute | solution.py:229
  35.2 1.3 %collective-permute-start.5 = (bf16[512,128]{1,0:T(8,128)(2,1)S(1)}, bf16[512,128]{1,0:T(8,128)(2,1)S(1)}, u32[]{:S(2)}, u32[]{:S(2)}) collective-permute-start(bf16[512,128]{1,0:T(8,128)(2,1)S(1)} %collective-permute-done.1.refs_1_), channel_id=1, source_target_pairs={{0,16},{16,0},{1,17},{17,1},{2,18},{18,2},{3,19},{19,3},{4,20},{20... | collective-permute-start | bytes 393224 | tf_op jit(solution)/shard_map/probes/ppermute | solution.py:229
  39.4 0.8 %copy-start = (bf16[512,512]{1,0:T(8,128)(2,1)}, bf16[512,512]{1,0:T(8,128)(2,1)S(1)}, u32[]{:S(2)}) copy-start(bf16[512,512]{1,0:T(8,128)(2,1)S(1)} %get-tuple-element.8.probes_ref) | copy-start | bytes 1572868
  63.4 1.7 %collective-permute-start.8 = (bf16[32,256]{1,0:T(8,128)(2,1)S(1)}, bf16[32,256]{1,0:T(8,128)(2,1)S(1)}, u32[]{:S(2)}, u32[]{:S(2)}) collective-permute-start(bf16[32,256]{1,0:T(8,128)(2,1)S(1)} %reduce_sum.12), channel_id=1, source_target_pairs={{0,16},{16,0},{1,17},{17,1},{2,18},{18,2},{3,19},{19,3},{4,20},{20... | collective-permute-start | bytes 49160 | tf_op jit(solution)/shard_map/spread/ppermute | solution.py:238

commit v9 on v8

--- a/solution.py
+++ b/solution.py
@@ -47,8 +47,8 @@
             source[d] = -1
         for s in range(SLOTS):
             block = blocks_ref[s]
-            along = (block % 8 + 8 - 2 * core) % 8
-            mine = jnp.where(along // 4 == run, 0, 1) == far
+            along = (block % 8 + 14 + 4 * far - 2 * core) % 8
+            mine = along // 4 == run
             at = (block // 8 * 4 + along % 4) * CAP
             at = jnp.where(source[at] >= 0, at + 1, at)
             source[at] = jnp.where(jnp.logical_and(s < live, mine), s, source[at])
@@ -87,6 +87,19 @@
         compiler_params=pltpu.CompilerParams(vmem_limit_bytes=8 << 20),
         name="outgoing_parts",
     )(blocks, pairs, counts, tiles)
+
+
+def after(array, other):
+    anywhere = pl.BlockSpec(memory_space=pl.ANY)
+    return pl.pallas_call(
+        lambda array_ref, other_ref, out_ref: None,
+        out_shape=jax.ShapeDtypeStruct(array.shape, array.dtype),
+        in_specs=[anywhere, anywhere],
+        out_specs=anywhere,
+        input_output_aliases={0: 0},
+        compiler_params=pltpu.CompilerParams(vmem_limit_bytes=1 << 20),
+        name="after",
+    )(array, other)
 
 
 def picked_probes(own, other, probe_idx, gaps, times, cos_weights, left_panel):
@@ -219,11 +232,10 @@
     tiles, tile_blocks, tile_pairs, left_panel = map(stay, (tiles, tile_blocks.reshape(SLOTS), tile_pairs, left_panel))
     swap = [(0, 1), (1, 0)]
     with jax.named_scope("parts"):
-        owned = [(z, z) for z in range(8)] + [(8 + z, 8 + (z ^ 4)) for z in range(8)]
+        owned = [(f * 8 + z, f * 8 + (z + 4 * f - 2) % 8) for f in range(2) for z in range(8)]
         bank = lax.ppermute(bank, ("f", "z"), owned)
         parts = outgoing_parts(tiles, tile_blocks, tile_pairs, tile_counts)
-        parts = lax.dynamic_update_slice(parts, bank[None, :1, :], (0, ROWS - 1, 0))
-        parts = lax.all_to_all(parts, ("k", "u", "z"), 0, 0, tiled=True, axis_index_groups=runs())
+        parts = lax.all_to_all(after(parts, bank), ("k", "u", "z"), 0, 0, tiled=True, axis_index_groups=runs())
     with jax.named_scope("probes"):
         own = [bank] + [lax.ppermute(bank, "y", [(y, (y + n) % 4) for y in range(4)]) for n in (1, 2, 3)]
         other = [lax.ppermute(columns, "k", swap) for columns in own]

time: 81.9 us -> 77.9 us (0.951)
  starting transfers between devices: 27.8 us -> 22.1 us
  blocking collectives: 27.8 us -> 30 us
  local copies, waits for them, and re-layouts: 2.15 us -> 0.86 us
  waiting for transfers between devices: 8.53 us -> 9.73 us
    ppermute x1, starting transfers between devices: 9.08 us -> 3.27 us  [shards(): bank = lax.ppermute(bank, ('f', 'z'), owned)]
    all_to_all x1, blocking collectives: 15.8 us -> 18.1 us  [shards(): products = lax.all_to_all(products, ('u', 'z'), 0, 0, tiled=True)]
    ppermute x1, waiting for transfers between devices: 0.01 us -> 1.95 us  [shards(): bank = lax.ppermute(bank, ('f', 'z'), owned)]
    dynamic_update_slice x1 -> x0, local copies, waits for them, and re-layouts: 1.29 us -> none  [shards(): parts = lax.dynamic_update_slice(parts, bank[None, :1, :], (0, ROWS - 1, 0))]
  transfers between devices with their start and end apart: 10 -> 10, of which waited for: 5 -> 5; matrix products, arithmetic and copies ran while one was open for 0% -> 0% of each run, Pallas kernels for 9% -> 10%
where the time goes in v9:
time: 77.9 us; the launch traced here: 77.1 us
  blocking collectives  30 us (39%)
  starting transfers between devices  22.1 us (28%)
  Pallas kernels  13.6 us (17%)
  waiting for transfers between devices  9.73 us (12%)
  local copies, waits for them, and re-layouts  0.86 us (1%)
    all_to_all x1, blocking collectives, shards(): products = lax.all_to_all(products, ('u', 'z'), 0, 0, tiled=True)  18.1 us
    all_to_all x1, blocking collectives, shards(): lax.all_to_all(jnp.broadcast_to(both, (8,) + both.shape), ('f', 'y'), 0,...  11.9 us
    ppermute x4, starting transfers between devices, shards(): other = [lax.ppermute(columns, 'k', swap) for columns in own]  7.9 us
    all_to_all x1, starting transfers between devices, shards(): lax.all_to_all(after(parts, bank), ('k', 'u', 'z'), 0, 0, tiled=True, axi...  6.08 us
    pallas_call x1, Pallas kernels, outgoing_parts(): pl.pallas_call(kernel, out_shape=jax.ShapeDtypeStruct((GROUP, ROWS, LANES...  4.66 us
    ppermute x3, starting transfers between devices, shards(): lax.ppermute(bank, 'y', [(y, (y + n) % 4) for y in range(4)])  4.61 us
    all_to_all x1, waiting for transfers between devices, shards(): lax.all_to_all(after(parts, bank), ('k', 'u', 'z'), 0, 0, tiled=True, axi...  4.29 us
    pallas_call x1, Pallas kernels, screened_response(): pl.pallas_call(kernel, out_shape=jax.ShapeDtypeStruct((2, SET, 2 * half),...  3.68 us
  transfers between devices with their start and end apart: 10, of which 5 were waited for; matrix products, arithmetic and copies ran while one was open for 0% of the time, Pallas kernels for 10%

profile of v9, /device:TPU:2, one launch (start us, length us, event | category | flops | bytes accessed | tf_op | source)
XLA Modules:
  0.0 77.1 jit_solution(13339318445445250923)
XLA Ops:
  0.0 3.3 %collective-permute-start = (bf16[512,128]{1,0:T(8,128)(2,1)}, bf16[512,128]{1,0:T(8,128)(2,1)S(1)}, u32[]{:S(2)}, u32[]{:S(2)}) collective-permute-start(bf16[512,128]{1,0:T(8,128)(2,1)} %param.18), channel_id=1, source_target_pairs={{0,6},{1,7},{2,0},{3,1},{4,2},{5,3},{6,4},{7,5},{128,130},{129,131... | collective-permute-start | bytes 393224 | tf_op jit(solution)/shard_map/parts/ppermute | solution.py:236
  3.9 4.7 %outgoing_parts.1.array_ref = bf16[8,528,128]{2,1,0:T(8,128)(2,1)} custom-call(s32[16]{0:T(128)} %bitcast.10, s32[16]{0:T(128)} %pairs_ref.1, s32[1]{0:T(128)S(6)} %copy.13.counts_ref, bf16[16,512,512]{2,1,0:T(8,128)(2,1)} %tiles_ref.1), custom_call_target="tpu_custom_call" | custom-call | tf_op jit(solution)/shard_map/parts/outgoing_parts/pallas_call | solution.py:76
  8.6 0.0 copy-start.1
  8.6 0.0 copy-start.2
  8.6 0.0 copy-start.3
  8.6 0.0 copy-start.4
  8.6 1.9 %collective-permute-done.other_ref.refs_0_ = bf16[512,128]{1,0:T(8,128)(2,1)S(1)} collective-permute-done((bf16[512,128]{1,0:T(8,128)(2,1)}, bf16[512,128]{1,0:T(8,128)(2,1)S(1)}, u32[]{:S(2)}, u32[]{:S(2)}) %collective-permute-start) | collective-permute-done | bytes 131104 | tf_op jit(solution)/shard_map/parts/ppermute | solution.py:236
  10.6 6.1 %all-to-all-start = ((bf16[8,528,128]{2,1,0:T(8,128)(2,1)}), bf16[8,528,128]{2,1,0:T(8,128)(2,1)S(1)}, u32[]{:S(2)}, u32[]{:S(2)}) async-start(bf16[8,528,128]{2,1,0:T(8,128)(2,1)} %after.1), calls=%async_computation | async-start | bytes 2162688 | tf_op jit(solution)/shard_map/parts/all_to_all | solution.py:238
  16.7 3.0 %collective-permute-start.3 = (bf16[512,128]{1,0:T(8,128)(2,1)S(1)}, bf16[512,128]{1,0:T(8,128)(2,1)S(1)}, u32[]{:S(2)}, u32[]{:S(2)}) collective-permute-start(bf16[512,128]{1,0:T(8,128)(2,1)S(1)} %collective-permute-done.other_ref.refs_0_), channel_id=1, source_target_pairs={{0,96},{32,0},{64,32},{96,64},{1,97},{33,1},{65,33},{97,65},{2,98}... | collective-permute-start | bytes 393224 | tf_op jit(solution)/shard_map/probes/ppermute | solution.py:240
  19.7 0.6 collective-permute-start.2
  20.3 1.0 %collective-permute-start.1 = (bf16[512,128]{1,0:T(8,128)(2,1)S(1)}, bf16[512,128]{1,0:T(8,128)(2,1)S(1)}, u32[]{:S(2)}, u32[]{:S(2)}) collective-permute-start(bf16[512,128]{1,0:T(8,128)(2,1)S(1)} %collective-permute-done.other_ref.refs_0_), channel_id=1, source_target_pairs={{0,32},{32,64},{64,96},{96,0},{1,33},{33,65},{65,97},{97,1},{2,34}... | collective-permute-start | bytes 393224 | tf_op jit(solution)/shard_map/probes/ppermute | solution.py:240
  21.3 1.8 %collective-permute-start.4 = (bf16[512,128]{1,0:T(8,128)(2,1)S(1)}, bf16[512,128]{1,0:T(8,128)(2,1)S(1)}, u32[]{:S(2)}, u32[]{:S(2)}) collective-permute-start(bf16[512,128]{1,0:T(8,128)(2,1)S(1)} %collective-permute-done.other_ref.refs_0_), channel_id=1, source_target_pairs={{0,16},{16,0},{1,17},{17,1},{2,18},{18,2},{3,19},{19,3},{4,20},{20... | collective-permute-start | bytes 393224 | tf_op jit(solution)/shard_map/probes/ppermute | solution.py:241
  23.1 0.0 collective-permute-done.3.refs_3_
  23.1 3.4 %collective-permute-start.7 = (bf16[512,128]{1,0:T(8,128)(2,1)S(1)}, bf16[512,128]{1,0:T(8,128)(2,1)S(1)}, u32[]{:S(2)}, u32[]{:S(2)}) collective-permute-start(bf16[512,128]{1,0:T(8,128)(2,1)S(1)} %collective-permute-done.3.refs_3_), channel_id=1, source_target_pairs={{0,16},{16,0},{1,17},{17,1},{2,18},{18,2},{3,19},{19,3},{4,20},{20... | collective-permute-start | bytes 393224 | tf_op jit(solution)/shard_map/probes/ppermute | solution.py:241
  26.5 0.0 collective-permute-done.2.refs_2_
  26.5 2.6 %collective-permute-start.6 = (bf16[512,128]{1,0:T(8,128)(2,1)S(1)}, bf16[512,128]{1,0:T(8,128)(2,1)S(1)}, u32[]{:S(2)}, u32[]{:S(2)}) collective-permute-start(bf16[512,128]{1,0:T(8,128)(2,1)S(1)} %collective-permute-done.2.refs_2_), channel_id=1, source_target_pairs={{0,16},{16,0},{1,17},{17,1},{2,18},{18,2},{3,19},{19,3},{4,20},{20... | collective-permute-start | bytes 393224 | tf_op jit(solution)/shard_map/probes/ppermute | solution.py:241
  29.1 1.2 %collective-permute-done.1.refs_1_ = bf16[512,128]{1,0:T(8,128)(2,1)S(1)} collective-permute-done((bf16[512,128]{1,0:T(8,128)(2,1)S(1)}, bf16[512,128]{1,0:T(8,128)(2,1)S(1)}, u32[]{:S(2)}, u32[]{:S(2)}) %collective-permute-start.1) | collective-permute-done | bytes 131104 | tf_op jit(solution)/shard_map/probes/ppermute | solution.py:240
  30.3 0.1 collective-permute-start.5
  30.4 0.0 collective-permute-done.4.refs_4_
  30.4 0.0 collective-permute-done.7.refs_7_
  30.4 0.0 collective-permute-done.6.refs_6_
  30.4 1.2 %collective-permute-done.5.refs_5_ = bf16[512,128]{1,0:T(8,128)(2,1)S(1)} collective-permute-done((bf16[512,128]{1,0:T(8,128)(2,1)S(1)}, bf16[512,128]{1,0:T(8,128)(2,1)S(1)}, u32[]{:S(2)}, u32[]{:S(2)}) %collective-permute-start.5) | collective-permute-done | bytes 131104 | tf_op jit(solution)/shard_map/probes/ppermute | solution.py:241
  31.6 0.0 copy-done.1
  31.6 0.0 copy-done.2
  31.6 0.0 copy-done.3
  31.6 0.0 copy-done.4
  31.6 2.8 %picked_probes.1 = (bf16[512,512]{1,0:T(8,128)(2,1)S(1)}, f32[2,2048]{1,0:T(2,128)S(1)}, bf16[512,2048]{1,0:T(8,128)(2,1)S(1)}) custom-call(f32[4]{0:T(128)S(1)} %copy-done.4, f32[4,4]{1,0:T(4,128)S(1)} %copy-done.2, bf16[512,128]{1,0:T(8,128)(2,1)S(1)} %collective-permute-done.other_ref.refs_0_, bf16[512,128]{1,0:T(8,128)(2,1)S(1)} %collective-permute-done.1.refs_1_, ...), custom_call_target="tpu_custom_call" | custom-call | tf_op jit(solution)/shard_map/probes/picked_probes/pallas_call | solution.py:129
  34.4 0.0 copy-start
  34.4 0.8 %copy-done = bf16[512,512]{1,0:T(8,128)(2,1)} copy-done((bf16[512,512]{1,0:T(8,128)(2,1)}, bf16[512,512]{1,0:T(8,128)(2,1)S(1)}, u32[]{:S(2)}) %copy-start) | copy-done | bytes 524312
  35.3 4.3 %all-to-all-done.parts_ref = bf16[8,528,128]{2,1,0:T(8,128)(2,1)S(1)} async-done(((bf16[8,528,128]{2,1,0:T(8,128)(2,1)}), bf16[8,528,128]{2,1,0:T(8,128)(2,1)S(1)}, u32[]{:S(2)}, u32[]{:S(2)}) %all-to-all-start) | async-done | bytes 1081376 | tf_op jit(solution)/shard_map/parts/all_to_all | solution.py:238
  39.6 2.5 %owner_products.1 = bf16[16,32,256]{2,1,0:T(8,128)(2,1)S(1)} custom-call(bf16[8,528,128]{2,1,0:T(8,128)(2,1)S(1)} %all-to-all-done.parts_ref, bf16[512,512]{1,0:T(8,128)(2,1)} %copy-done), custom_call_target="tpu_custom_call" | custom-call | tf_op jit(solution)/shard_map/products/owner_products/pallas_call | solution.py:165
  42.1 18.1 %all_to_all.15 = bf16[16,32,256]{2,1,0:T(8,128)(2,1)S(1)} all-to-all(bf16[16,32,256]{2,1,0:T(8,128)(2,1)S(1)} %owner_products.1), channel_id=1, replica_groups=mesh['f'=2,'y'=4,'k'=2,'u'=2,'z'=8] {'u','z'}, dimensions={0} | all-to-all | bytes 524288 | tf_op jit(solution)/shard_map/products/all_to_all | solution.py:247
  60.3 0.2 collective-permute-start.8
  60.5 1.1 %collective-permute-done.8 = bf16[32,256]{1,0:T(8,128)(2,1)S(1)} collective-permute-done((bf16[32,256]{1,0:T(8,128)(2,1)S(1)}, bf16[32,256]{1,0:T(8,128)(2,1)S(1)}, u32[]{:S(2)}, u32[]{:S(2)}) %collective-permute-start.8) | collective-permute-done | bytes 16416 | tf_op jit(solution)/shard_map/spread/ppermute | solution.py:250
  61.6 11.9 %all_to_all.16.parts_ref = bf16[8,2,32,256]{3,2,1,0:T(8,128)(2,1)S(1)} all-to-all(bf16[8,2,32,256]{3,2,1,0:T(8,128)(2,1)S(1)} %broadcast_in_dim.3), channel_id=1, replica_groups=mesh['f'=2,'y'=4,'k'=2,'u'=2,'z'=8] {'f','y'}, dimensions={0} | all-to-all | bytes 524288 | tf_op jit(solution)/shard_map/spread/all_to_all | solution.py:251
  73.4 3.7 %screened_response.1 = f32[2,32,1024]{2,1,0:T(8,128)} custom-call(bf16[8,2,32,256]{3,2,1,0:T(8,128)(2,1)S(1)} %all_to_all.16.parts_ref, bf16[512,2048]{1,0:T(8,128)(2,1)S(1)} %get-tuple-element.9.first_ref, bf16[1024,2048]{1,0:T(8,128)(2,1)} %left_ref.1, f32[2,2048]{1,0:T(2,128)S(1)} %get-tuple-element.10.weights_ref), custom_call_target="tpu_custom_call" | custom-call | tf_op jit(solution)/shard_map/response/screened_response/pallas_call | solution.py:213
  (4 shorter events, 0.1 us)
Async XLA Ops:
  0.0 10.6 %collective-permute-start = (bf16[512,128]{1,0:T(8,128)(2,1)}, bf16[512,128]{1,0:T(8,128)(2,1)S(1)}, u32[]{:S(2)}, u32[]{:S(2)}) collective-permute-start(bf16[512,128]{1,0:T(8,128)(2,1)} %param.18), channel_id=1, source_target_pairs={{0,6},{1,7},{2,0},{3,1},{4,2},{5,3},{6,4},{7,5},{128,130},{129,131... | collective-permute-start | bytes 393224 | tf_op jit(solution)/shard_map/parts/ppermute | solution.py:236
  8.6 23.0 %copy-start.1 = (f32[2048]{0:T(1024)S(1)}, f32[2048]{0:T(1024)}, u32[]{:S(2)}) copy-start(f32[2048]{0:T(1024)} %param.15) | copy-start | bytes 24580
  8.6 23.0 %copy-start.2 = (f32[4,4]{1,0:T(4,128)S(1)}, f32[4,4]{1,0:T(4,128)}, u32[]{:S(2)}) copy-start(f32[4,4]{1,0:T(4,128)} %cos_ref.1) | copy-start | bytes 196
  8.6 23.0 %copy-start.3 = (s32[512]{0:T(512)S(1)}, s32[512]{0:T(512)}, u32[]{:S(2)}) copy-start(s32[512]{0:T(512)} %param.19) | copy-start | bytes 6148
  8.6 23.0 %copy-start.4 = (f32[4]{0:T(128)S(1)}, f32[4]{0:T(128)}, u32[]{:S(2)}) copy-start(f32[4]{0:T(128)} %times_ref.1) | copy-start | bytes 52
  10.6 29.0 %all-to-all-start = ((bf16[8,528,128]{2,1,0:T(8,128)(2,1)}), bf16[8,528,128]{2,1,0:T(8,128)(2,1)S(1)}, u32[]{:S(2)}, u32[]{:S(2)}) async-start(bf16[8,528,128]{2,1,0:T(8,128)(2,1)} %after.1), calls=%async_computation | async-start | bytes 2162688 | tf_op jit(solution)/shard_map/parts/all_to_all | solution.py:238
  16.7 6.4 %collective-permute-start.3 = (bf16[512,128]{1,0:T(8,128)(2,1)S(1)}, bf16[512,128]{1,0:T(8,128)(2,1)S(1)}, u32[]{:S(2)}, u32[]{:S(2)}) collective-permute-start(bf16[512,128]{1,0:T(8,128)(2,1)S(1)} %collective-permute-done.other_ref.refs_0_), channel_id=1, source_target_pairs={{0,96},{32,0},{64,32},{96,64},{1,97},{33,1},{65,33},{97,65},{2,98}... | collective-permute-start | bytes 393224 | tf_op jit(solution)/shard_map/probes/ppermute | solution.py:240
  19.7 6.8 %collective-permute-start.2 = (bf16[512,128]{1,0:T(8,128)(2,1)S(1)}, bf16[512,128]{1,0:T(8,128)(2,1)S(1)}, u32[]{:S(2)}, u32[]{:S(2)}) collective-permute-start(bf16[512,128]{1,0:T(8,128)(2,1)S(1)} %collective-permute-done.other_ref.refs_0_), channel_id=1, source_target_pairs={{0,64},{32,96},{64,0},{96,32},{1,65},{33,97},{65,1},{97,33},{2,66}... | collective-permute-start | bytes 393224 | tf_op jit(solution)/shard_map/probes/ppermute | solution.py:240
  20.3 10.0 %collective-permute-start.1 = (bf16[512,128]{1,0:T(8,128)(2,1)S(1)}, bf16[512,128]{1,0:T(8,128)(2,1)S(1)}, u32[]{:S(2)}, u32[]{:S(2)}) collective-permute-start(bf16[512,128]{1,0:T(8,128)(2,1)S(1)} %collective-permute-done.other_ref.refs_0_), channel_id=1, source_target_pairs={{0,32},{32,64},{64,96},{96,0},{1,33},{33,65},{65,97},{97,1},{2,34}... | collective-permute-start | bytes 393224 | tf_op jit(solution)/shard_map/probes/ppermute | solution.py:240
  21.3 9.1 %collective-permute-start.4 = (bf16[512,128]{1,0:T(8,128)(2,1)S(1)}, bf16[512,128]{1,0:T(8,128)(2,1)S(1)}, u32[]{:S(2)}, u32[]{:S(2)}) collective-permute-start(bf16[512,128]{1,0:T(8,128)(2,1)S(1)} %collective-permute-done.other_ref.refs_0_), channel_id=1, source_target_pairs={{0,16},{16,0},{1,17},{17,1},{2,18},{18,2},{3,19},{19,3},{4,20},{20... | collective-permute-start | bytes 393224 | tf_op jit(solution)/shard_map/probes/ppermute | solution.py:241
  23.1 7.3 %collective-permute-start.7 = (bf16[512,128]{1,0:T(8,128)(2,1)S(1)}, bf16[512,128]{1,0:T(8,128)(2,1)S(1)}, u32[]{:S(2)}, u32[]{:S(2)}) collective-permute-start(bf16[512,128]{1,0:T(8,128)(2,1)S(1)} %collective-permute-done.3.refs_3_), channel_id=1, source_target_pairs={{0,16},{16,0},{1,17},{17,1},{2,18},{18,2},{3,19},{19,3},{4,20},{20... | collective-permute-start | bytes 393224 | tf_op jit(solution)/shard_map/probes/ppermute | solution.py:241
  26.5 3.9 %collective-permute-start.6 = (bf16[512,128]{1,0:T(8,128)(2,1)S(1)}, bf16[512,128]{1,0:T(8,128)(2,1)S(1)}, u32[]{:S(2)}, u32[]{:S(2)}) collective-permute-start(bf16[512,128]{1,0:T(8,128)(2,1)S(1)} %collective-permute-done.2.refs_2_), channel_id=1, source_target_pairs={{0,16},{16,0},{1,17},{17,1},{2,18},{18,2},{3,19},{19,3},{4,20},{20... | collective-permute-start | bytes 393224 | tf_op jit(solution)/shard_map/probes/ppermute | solution.py:241
  30.3 1.3 %collective-permute-start.5 = (bf16[512,128]{1,0:T(8,128)(2,1)S(1)}, bf16[512,128]{1,0:T(8,128)(2,1)S(1)}, u32[]{:S(2)}, u32[]{:S(2)}) collective-permute-start(bf16[512,128]{1,0:T(8,128)(2,1)S(1)} %collective-permute-done.1.refs_1_), channel_id=1, source_target_pairs={{0,16},{16,0},{1,17},{17,1},{2,18},{18,2},{3,19},{19,3},{4,20},{20... | collective-permute-start | bytes 393224 | tf_op jit(solution)/shard_map/probes/ppermute | solution.py:241
  34.4 0.8 %copy-start = (bf16[512,512]{1,0:T(8,128)(2,1)}, bf16[512,512]{1,0:T(8,128)(2,1)S(1)}, u32[]{:S(2)}) copy-start(bf16[512,512]{1,0:T(8,128)(2,1)S(1)} %get-tuple-element.8.probes_ref) | copy-start | bytes 1572868
  60.3 1.3 %collective-permute-start.8 = (bf16[32,256]{1,0:T(8,128)(2,1)S(1)}, bf16[32,256]{1,0:T(8,128)(2,1)S(1)}, u32[]{:S(2)}, u32[]{:S(2)}) collective-permute-start(bf16[32,256]{1,0:T(8,128)(2,1)S(1)} %reduce_sum.12), channel_id=1, source_target_pairs={{0,16},{16,0},{1,17},{17,1},{2,18},{18,2},{3,19},{19,3},{4,20},{20... | collective-permute-start | bytes 49160 | tf_op jit(solution)/shard_map/spread/ppermute | solution.py:250

commit v10 on v9

--- a/solution.py
+++ b/solution.py
@@ -103,11 +103,11 @@
 
 
 def picked_probes(own, other, probe_idx, gaps, times, cos_weights, left_panel):
-    half = left_panel.shape[0] // 2
+    cut = left_panel.shape[0] // 8 * 3
 
     def kernel(times_ref, cos_ref, *refs):
         bank_refs, (idx_ref, gaps_ref, left_ref, out_ref, weights_ref, first_ref, sem) = refs[:8], refs[8:]
-        fetch = pltpu.make_async_copy(left_ref.at[pl.ds(0, half), :], first_ref, sem)
+        fetch = pltpu.make_async_copy(left_ref.at[pl.ds(0, cut), :], first_ref, sem)
         fetch.start()
         core, y = lax.axis_index("k"), lax.axis_index("y")
         total = jnp.zeros((TILE, NPROBE), F32)
@@ -131,7 +131,7 @@
         out_shape=(
             jax.ShapeDtypeStruct((TILE, NPROBE), BF16),
             jax.ShapeDtypeStruct((2, NPAIR), F32),
-            jax.ShapeDtypeStruct((half, NPAIR), BF16),
+            jax.ShapeDtypeStruct((cut, NPAIR), BF16),
         ),
         in_specs=[SMEM, SMEM] + [VMEM] * 10 + [HBM],
         out_specs=(VMEM, VMEM, VMEM),
@@ -142,13 +142,10 @@
 
 
 def owner_products(parts, probes):
-    def kernel(parts_ref, probes_ref, out_ref, held, product, sem):
-        fetch = pltpu.make_async_copy(probes_ref, held, sem)
-        fetch.start()
+    def kernel(parts_ref, probes_ref, out_ref, product):
         units = parts_ref[:, : CAP * UNIT, :].reshape(GROUP * CAP, TILE // LANES, PART, LANES)
         rows = jnp.concatenate([units[:, n] for n in range(TILE // LANES)], axis=-1).reshape(GROUP * CAP * PART, TILE)
-        fetch.wait()
-        product[...] = jnp.dot(rows, held[...], preferred_element_type=F32)
+        product[...] = jnp.dot(rows, probes_ref[...], preferred_element_type=F32)
         codes = [
             parts_ref[c, CAP * UNIT :, :].astype(F32)[j * (CODE // CAP) : j * (CODE // CAP) + 1, :1]
             for c in range(GROUP)
@@ -165,23 +162,19 @@
     return pl.pallas_call(
         kernel,
         out_shape=jax.ShapeDtypeStruct((NB, SET, MB * PART), BF16),
-        in_specs=[VMEM, HBM],
+        in_specs=[VMEM, VMEM],
         out_specs=VMEM,
-        scratch_shapes=[
-            pltpu.VMEM((TILE, NPROBE), BF16),
-            pltpu.VMEM((GROUP * CAP * PART, NPROBE), F32),
-            pltpu.SemaphoreType.DMA,
-        ],
+        scratch_shapes=[pltpu.VMEM((GROUP * CAP * PART, NPROBE), F32)],
         compiler_params=pltpu.CompilerParams(vmem_limit_bytes=16 << 20),
         name="owner_products",
     )(parts, probes)
 
 
-def screened_response(parts, first_half, left_panel, weights):
-    half = first_half.shape[0]
+def screened_response(parts, first, left_panel, weights):
+    cut, rows = first.shape[0], left_panel.shape[0]
 
     def kernel(parts_ref, first_ref, left_ref, weights_ref, out_ref, scaled, second, sem):
-        fetch = pltpu.make_async_copy(left_ref.at[pl.ds(half, half), :], second, sem)
+        fetch = pltpu.make_async_copy(left_ref.at[pl.ds(cut, rows - cut), :], second, sem)
         fetch.start()
         core = lax.axis_index("k")
         low = lax.broadcasted_iota(jnp.int32, (SET, LANES), 1) < PART
@@ -201,28 +194,28 @@
                     scaled[f * SET : (f + 1) * SET, at : at + LANES] = (
                         whole * weights_ref[f : f + 1, at : at + LANES]
                     ).astype(BF16)
-        for n, left in enumerate((first_ref, second)):
-            if n == 1:
+        for left, start, stop in ((first_ref, 0, cut), (second, cut, rows)):
+            if start == cut:
                 fetch.wait()
             product = lax.dot_general(
                 scaled[...], left[...], (((1,), (1,)), ((), ())), preferred_element_type=F32
             )
-            out_ref[0, :, n * half : (n + 1) * half] = product[:SET]
-            out_ref[1, :, n * half : (n + 1) * half] = product[SET:]
-
-    return pl.pallas_call(
-        kernel,
-        out_shape=jax.ShapeDtypeStruct((2, SET, 2 * half), F32),
+            out_ref[0, :, start:stop] = product[:SET]
+            out_ref[1, :, start:stop] = product[SET:]
+
+    return pl.pallas_call(
+        kernel,
+        out_shape=jax.ShapeDtypeStruct((2, SET, rows), F32),
         in_specs=[VMEM, VMEM, HBM, VMEM],
         out_specs=VMEM,
         scratch_shapes=[
             pltpu.VMEM((2 * SET, NPAIR), BF16),
-            pltpu.VMEM((half, NPAIR), BF16),
+            pltpu.VMEM((rows - cut, NPAIR), BF16),
             pltpu.SemaphoreType.DMA,
         ],
         compiler_params=pltpu.CompilerParams(vmem_limit_bytes=12 << 20),
         name="screened_response",
-    )(parts, first_half, left_panel, weights)
+    )(parts, first, left_panel, weights)
 
 
 def shards(
@@ -239,18 +232,18 @@
     with jax.named_scope("probes"):
         own = [bank] + [lax.ppermute(bank, "y", [(y, (y + n) % 4) for y in range(4)]) for n in (1, 2, 3)]
         other = [lax.ppermute(columns, "k", swap) for columns in own]
-        probes, weights, first_half = picked_probes(
+        probes, weights, first = picked_probes(
             own, other, probe_idx.reshape(1, NPROBE), gaps.reshape(1, NPAIR), times, cos_weights, left_panel
         )
     with jax.named_scope("products"):
-        products = owner_products(parts, stay(probes))
+        products = owner_products(parts, probes)
         products = lax.all_to_all(products, ("u", "z"), 0, 0, tiled=True)
         product = jnp.sum(products.astype(F32), axis=0).astype(BF16)
     with jax.named_scope("spread"):
         both = jnp.stack([product, lax.ppermute(product, "k", swap)])
         both = lax.all_to_all(jnp.broadcast_to(both, (8,) + both.shape), ("f", "y"), 0, 0, tiled=True)
     with jax.named_scope("response"):
-        turned = screened_response(both, first_half, left_panel, weights)
+        turned = screened_response(both, first, left_panel, weights)
         return jnp.swapaxes(turned, 1, 2)
 
 

time: 77.9 us -> 77.4 us (level)
  waiting for transfers between devices: 9.73 us -> 10.8 us
  local copies, waits for them, and re-layouts: 0.86 us -> 0.04 us
  Pallas kernels: 13.6 us -> 12.8 us
    pallas_call x1, Pallas kernels: 2.52 us -> 1.47 us  [owner_products(): pl.pallas_call(kernel, out_shape=jax.ShapeDtypeStruct((NB, SET, MB * PART...]
    all_to_all x1, waiting for transfers between devices: 4.29 us -> 5.3 us  [shards(): lax.all_to_all(after(parts, bank), ('k', 'u', 'z'), 0, 0, tiled=True, axi...]
    unnamed x10 -> x8, local copies, waits for them, and re-layouts: 0.84 us -> 0.01 us
  transfers between devices with their start and end apart: 10 -> 10, of which waited for: 5 -> 5; matrix products, arithmetic and copies ran while one was open for 0% -> 0% of each run, Pallas kernels for 10% -> 9%
where the time goes in v10:
time: 77.4 us; the launch traced here: 76.6 us
  blocking collectives  30 us (39%)
  starting transfers between devices  22.2 us (29%)
  Pallas kernels  12.8 us (17%)
  waiting for transfers between devices  10.8 us (14%)
    all_to_all x1, blocking collectives, shards(): products = lax.all_to_all(products, ('u', 'z'), 0, 0, tiled=True)  18.1 us
    all_to_all x1, blocking collectives, shards(): lax.all_to_all(jnp.broadcast_to(both, (8,) + both.shape), ('f', 'y'), 0,...  11.9 us
    ppermute x4, starting transfers between devices, shards(): other = [lax.ppermute(columns, 'k', swap) for columns in own]  7.9 us
    all_to_all x1, starting transfers between devices, shards(): lax.all_to_all(after(parts, bank), ('k', 'u', 'z'), 0, 0, tiled=True, axi...  6.22 us
    all_to_all x1, waiting for transfers between devices, shards(): lax.all_to_all(after(parts, bank), ('k', 'u', 'z'), 0, 0, tiled=True, axi...  5.3 us
    pallas_call x1, Pallas kernels, outgoing_parts(): pl.pallas_call(kernel, out_shape=jax.ShapeDtypeStruct((GROUP, ROWS, LANES...  4.67 us
    ppermute x3, starting transfers between devices, shards(): lax.ppermute(bank, 'y', [(y, (y + n) % 4) for y in range(4)])  4.61 us
    pallas_call x1, Pallas kernels, screened_response(): pl.pallas_call(kernel, out_shape=jax.ShapeDtypeStruct((2, SET, rows), F32...  4.06 us
  transfers between devices with their start and end apart: 10, of which 5 were waited for; matrix products, arithmetic and copies ran while one was open for 0% of the time, Pallas kernels for 9%

profile of v10, /device:TPU:2, one launch (start us, length us, event | category | flops | bytes accessed | tf_op | source)
XLA Modules:
  0.0 76.6 jit_solution(4871015606899302502)
XLA Ops:
  0.0 3.3 %collective-permute-start = (bf16[512,128]{1,0:T(8,128)(2,1)}, bf16[512,128]{1,0:T(8,128)(2,1)S(1)}, u32[]{:S(2)}, u32[]{:S(2)}) collective-permute-start(bf16[512,128]{1,0:T(8,128)(2,1)} %param.18), channel_id=1, source_target_pairs={{0,6},{1,7},{2,0},{3,1},{4,2},{5,3},{6,4},{7,5},{128,130},{129,131... | collective-permute-start | bytes 393224 | tf_op jit(solution)/shard_map/parts/ppermute | solution.py:229
  3.9 4.7 %outgoing_parts.1.array_ref = bf16[8,528,128]{2,1,0:T(8,128)(2,1)} custom-call(s32[16]{0:T(128)} %bitcast.10, s32[16]{0:T(128)} %pairs_ref.1, s32[1]{0:T(128)S(6)} %copy.13.counts_ref, bf16[16,512,512]{2,1,0:T(8,128)(2,1)} %tiles_ref.1), custom_call_target="tpu_custom_call" | custom-call | tf_op jit(solution)/shard_map/parts/outgoing_parts/pallas_call | solution.py:76
  8.6 2.0 %collective-permute-done.other_ref.refs_0_ = bf16[512,128]{1,0:T(8,128)(2,1)S(1)} collective-permute-done((bf16[512,128]{1,0:T(8,128)(2,1)}, bf16[512,128]{1,0:T(8,128)(2,1)S(1)}, u32[]{:S(2)}, u32[]{:S(2)}) %collective-permute-start) | collective-permute-done | bytes 131104 | tf_op jit(solution)/shard_map/parts/ppermute | solution.py:229
  10.6 0.0 copy-start
  10.6 0.0 copy-start.1
  10.6 0.0 copy-start.2
  10.6 0.0 copy-start.3
  10.6 6.2 %all-to-all-start = ((bf16[8,528,128]{2,1,0:T(8,128)(2,1)}), bf16[8,528,128]{2,1,0:T(8,128)(2,1)S(1)}, u32[]{:S(2)}, u32[]{:S(2)}) async-start(bf16[8,528,128]{2,1,0:T(8,128)(2,1)} %after.1), calls=%async_computation | async-start | bytes 2162688 | tf_op jit(solution)/shard_map/parts/all_to_all | solution.py:231
  16.8 3.0 %collective-permute-start.3 = (bf16[512,128]{1,0:T(8,128)(2,1)S(1)}, bf16[512,128]{1,0:T(8,128)(2,1)S(1)}, u32[]{:S(2)}, u32[]{:S(2)}) collective-permute-start(bf16[512,128]{1,0:T(8,128)(2,1)S(1)} %collective-permute-done.other_ref.refs_0_), channel_id=1, source_target_pairs={{0,96},{32,0},{64,32},{96,64},{1,97},{33,1},{65,33},{97,65},{2,98}... | collective-permute-start | bytes 393224 | tf_op jit(solution)/shard_map/probes/ppermute | solution.py:233
  19.8 0.6 collective-permute-start.2
  20.5 1.0 %collective-permute-start.1 = (bf16[512,128]{1,0:T(8,128)(2,1)S(1)}, bf16[512,128]{1,0:T(8,128)(2,1)S(1)}, u32[]{:S(2)}, u32[]{:S(2)}) collective-permute-start(bf16[512,128]{1,0:T(8,128)(2,1)S(1)} %collective-permute-done.other_ref.refs_0_), channel_id=1, source_target_pairs={{0,32},{32,64},{64,96},{96,0},{1,33},{33,65},{65,97},{97,1},{2,34}... | collective-permute-start | bytes 393224 | tf_op jit(solution)/shard_map/probes/ppermute | solution.py:233
  21.4 1.8 %collective-permute-start.4 = (bf16[512,128]{1,0:T(8,128)(2,1)S(1)}, bf16[512,128]{1,0:T(8,128)(2,1)S(1)}, u32[]{:S(2)}, u32[]{:S(2)}) collective-permute-start(bf16[512,128]{1,0:T(8,128)(2,1)S(1)} %collective-permute-done.other_ref.refs_0_), channel_id=1, source_target_pairs={{0,16},{16,0},{1,17},{17,1},{2,18},{18,2},{3,19},{19,3},{4,20},{20... | collective-permute-start | bytes 393224 | tf_op jit(solution)/shard_map/probes/ppermute | solution.py:234
  23.2 0.0 collective-permute-done.3.refs_3_
  23.2 3.4 %collective-permute-start.7 = (bf16[512,128]{1,0:T(8,128)(2,1)S(1)}, bf16[512,128]{1,0:T(8,128)(2,1)S(1)}, u32[]{:S(2)}, u32[]{:S(2)}) collective-permute-start(bf16[512,128]{1,0:T(8,128)(2,1)S(1)} %collective-permute-done.3.refs_3_), channel_id=1, source_target_pairs={{0,16},{16,0},{1,17},{17,1},{2,18},{18,2},{3,19},{19,3},{4,20},{20... | collective-permute-start | bytes 393224 | tf_op jit(solution)/shard_map/probes/ppermute | solution.py:234
  26.7 0.0 collective-permute-done.2.refs_2_
  26.7 2.6 %collective-permute-start.6 = (bf16[512,128]{1,0:T(8,128)(2,1)S(1)}, bf16[512,128]{1,0:T(8,128)(2,1)S(1)}, u32[]{:S(2)}, u32[]{:S(2)}) collective-permute-start(bf16[512,128]{1,0:T(8,128)(2,1)S(1)} %collective-permute-done.2.refs_2_), channel_id=1, source_target_pairs={{0,16},{16,0},{1,17},{17,1},{2,18},{18,2},{3,19},{19,3},{4,20},{20... | collective-permute-start | bytes 393224 | tf_op jit(solution)/shard_map/probes/ppermute | solution.py:234
  29.2 1.2 %collective-permute-done.1.refs_1_ = bf16[512,128]{1,0:T(8,128)(2,1)S(1)} collective-permute-done((bf16[512,128]{1,0:T(8,128)(2,1)S(1)}, bf16[512,128]{1,0:T(8,128)(2,1)S(1)}, u32[]{:S(2)}, u32[]{:S(2)}) %collective-permute-start.1) | collective-permute-done | bytes 131104 | tf_op jit(solution)/shard_map/probes/ppermute | solution.py:233
  30.4 0.1 collective-permute-start.5
  30.5 0.0 collective-permute-done.4.refs_4_
  30.6 0.0 collective-permute-done.7.refs_7_
  30.6 0.0 collective-permute-done.6.refs_6_
  30.6 1.2 %collective-permute-done.5.refs_5_ = bf16[512,128]{1,0:T(8,128)(2,1)S(1)} collective-permute-done((bf16[512,128]{1,0:T(8,128)(2,1)S(1)}, bf16[512,128]{1,0:T(8,128)(2,1)S(1)}, u32[]{:S(2)}, u32[]{:S(2)}) %collective-permute-start.5) | collective-permute-done | bytes 131104 | tf_op jit(solution)/shard_map/probes/ppermute | solution.py:234
  31.8 0.0 copy-done
  31.8 0.0 copy-done.1
  31.8 0.0 copy-done.2
  31.8 0.0 copy-done.3
  31.8 2.6 %picked_probes.1 = (bf16[512,512]{1,0:T(8,128)(2,1)S(1)}, f32[2,2048]{1,0:T(2,128)S(1)}, bf16[384,2048]{1,0:T(8,128)(2,1)S(1)}) custom-call(f32[4]{0:T(128)S(1)} %copy-done.3, f32[4,4]{1,0:T(4,128)S(1)} %copy-done.1, bf16[512,128]{1,0:T(8,128)(2,1)S(1)} %collective-permute-done.other_ref.refs_0_, bf16[512,128]{1,0:T(8,128)(2,1)S(1)} %collective-permute-done.1.refs_1_, ...), custom_call_target="tpu_custom_call" | custom-call | tf_op jit(solution)/shard_map/probes/picked_probes/pallas_call | solution.py:129
  34.4 5.3 %all-to-all-done.parts_ref = bf16[8,528,128]{2,1,0:T(8,128)(2,1)S(1)} async-done(((bf16[8,528,128]{2,1,0:T(8,128)(2,1)}), bf16[8,528,128]{2,1,0:T(8,128)(2,1)S(1)}, u32[]{:S(2)}, u32[]{:S(2)}) %all-to-all-start) | async-done | bytes 1081376 | tf_op jit(solution)/shard_map/parts/all_to_all | solution.py:231
  39.7 1.5 %owner_products.1 = bf16[16,32,256]{2,1,0:T(8,128)(2,1)S(1)} custom-call(bf16[8,528,128]{2,1,0:T(8,128)(2,1)S(1)} %all-to-all-done.parts_ref, bf16[512,512]{1,0:T(8,128)(2,1)S(1)} %get-tuple-element.8.probes_ref), custom_call_target="tpu_custom_call" | custom-call | tf_op jit(solution)/shard_map/products/owner_products/pallas_call | solution.py:162
  41.2 18.1 %all_to_all.15 = bf16[16,32,256]{2,1,0:T(8,128)(2,1)S(1)} all-to-all(bf16[16,32,256]{2,1,0:T(8,128)(2,1)S(1)} %owner_products.1), channel_id=1, replica_groups=mesh['f'=2,'y'=4,'k'=2,'u'=2,'z'=8] {'u','z'}, dimensions={0} | all-to-all | bytes 524288 | tf_op jit(solution)/shard_map/products/all_to_all | solution.py:240
  59.4 0.2 collective-permute-start.8
  59.6 1.1 %collective-permute-done.8 = bf16[32,256]{1,0:T(8,128)(2,1)S(1)} collective-permute-done((bf16[32,256]{1,0:T(8,128)(2,1)S(1)}, bf16[32,256]{1,0:T(8,128)(2,1)S(1)}, u32[]{:S(2)}, u32[]{:S(2)}) %collective-permute-start.8) | collective-permute-done | bytes 16416 | tf_op jit(solution)/shard_map/spread/ppermute | solution.py:243
  60.7 11.9 %all_to_all.16.parts_ref = bf16[8,2,32,256]{3,2,1,0:T(8,128)(2,1)S(1)} all-to-all(bf16[8,2,32,256]{3,2,1,0:T(8,128)(2,1)S(1)} %broadcast_in_dim.3), channel_id=1, replica_groups=mesh['f'=2,'y'=4,'k'=2,'u'=2,'z'=8] {'f','y'}, dimensions={0} | all-to-all | bytes 524288 | tf_op jit(solution)/shard_map/spread/all_to_all | solution.py:244
  72.5 4.1 %screened_response.1 = f32[2,32,1024]{2,1,0:T(8,128)} custom-call(bf16[8,2,32,256]{3,2,1,0:T(8,128)(2,1)S(1)} %all_to_all.16.parts_ref, bf16[384,2048]{1,0:T(8,128)(2,1)S(1)} %get-tuple-element.9.first_ref, bf16[1024,2048]{1,0:T(8,128)(2,1)} %left_ref.1, f32[2,2048]{1,0:T(2,128)S(1)} %get-tuple-element.10.weights_ref), custom_call_target="tpu_custom_call" | custom-call | tf_op jit(solution)/shard_map/response/screened_response/pallas_call | solution.py:206
  (4 shorter events, 0.1 us)
Async XLA Ops:
  0.0 10.6 %collective-permute-start = (bf16[512,128]{1,0:T(8,128)(2,1)}, bf16[512,128]{1,0:T(8,128)(2,1)S(1)}, u32[]{:S(2)}, u32[]{:S(2)}) collective-permute-start(bf16[512,128]{1,0:T(8,128)(2,1)} %param.18), channel_id=1, source_target_pairs={{0,6},{1,7},{2,0},{3,1},{4,2},{5,3},{6,4},{7,5},{128,130},{129,131... | collective-permute-start | bytes 393224 | tf_op jit(solution)/shard_map/parts/ppermute | solution.py:229
  10.6 21.2 %copy-start = (f32[2048]{0:T(1024)S(1)}, f32[2048]{0:T(1024)}, u32[]{:S(2)}) copy-start(f32[2048]{0:T(1024)} %param.15) | copy-start | bytes 24580
  10.6 21.2 %copy-start.1 = (f32[4,4]{1,0:T(4,128)S(1)}, f32[4,4]{1,0:T(4,128)}, u32[]{:S(2)}) copy-start(f32[4,4]{1,0:T(4,128)} %cos_ref.1) | copy-start | bytes 196
  10.6 21.2 %copy-start.2 = (s32[512]{0:T(512)S(1)}, s32[512]{0:T(512)}, u32[]{:S(2)}) copy-start(s32[512]{0:T(512)} %param.19) | copy-start | bytes 6148
  10.6 21.2 %copy-start.3 = (f32[4]{0:T(128)S(1)}, f32[4]{0:T(128)}, u32[]{:S(2)}) copy-start(f32[4]{0:T(128)} %times_ref.1) | copy-start | bytes 52
  10.6 29.1 %all-to-all-start = ((bf16[8,528,128]{2,1,0:T(8,128)(2,1)}), bf16[8,528,128]{2,1,0:T(8,128)(2,1)S(1)}, u32[]{:S(2)}, u32[]{:S(2)}) async-start(bf16[8,528,128]{2,1,0:T(8,128)(2,1)} %after.1), calls=%async_computation | async-start | bytes 2162688 | tf_op jit(solution)/shard_map/parts/all_to_all | solution.py:231
  16.8 6.4 %collective-permute-start.3 = (bf16[512,128]{1,0:T(8,128)(2,1)S(1)}, bf16[512,128]{1,0:T(8,128)(2,1)S(1)}, u32[]{:S(2)}, u32[]{:S(2)}) collective-permute-start(bf16[512,128]{1,0:T(8,128)(2,1)S(1)} %collective-permute-done.other_ref.refs_0_), channel_id=1, source_target_pairs={{0,96},{32,0},{64,32},{96,64},{1,97},{33,1},{65,33},{97,65},{2,98}... | collective-permute-start | bytes 393224 | tf_op jit(solution)/shard_map/probes/ppermute | solution.py:233
  19.8 6.8 %collective-permute-start.2 = (bf16[512,128]{1,0:T(8,128)(2,1)S(1)}, bf16[512,128]{1,0:T(8,128)(2,1)S(1)}, u32[]{:S(2)}, u32[]{:S(2)}) collective-permute-start(bf16[512,128]{1,0:T(8,128)(2,1)S(1)} %collective-permute-done.other_ref.refs_0_), channel_id=1, source_target_pairs={{0,64},{32,96},{64,0},{96,32},{1,65},{33,97},{65,1},{97,33},{2,66}... | collective-permute-start | bytes 393224 | tf_op jit(solution)/shard_map/probes/ppermute | solution.py:233
  20.5 10.0 %collective-permute-start.1 = (bf16[512,128]{1,0:T(8,128)(2,1)S(1)}, bf16[512,128]{1,0:T(8,128)(2,1)S(1)}, u32[]{:S(2)}, u32[]{:S(2)}) collective-permute-start(bf16[512,128]{1,0:T(8,128)(2,1)S(1)} %collective-permute-done.other_ref.refs_0_), channel_id=1, source_target_pairs={{0,32},{32,64},{64,96},{96,0},{1,33},{33,65},{65,97},{97,1},{2,34}... | collective-permute-start | bytes 393224 | tf_op jit(solution)/shard_map/probes/ppermute | solution.py:233
  21.4 9.1 %collective-permute-start.4 = (bf16[512,128]{1,0:T(8,128)(2,1)S(1)}, bf16[512,128]{1,0:T(8,128)(2,1)S(1)}, u32[]{:S(2)}, u32[]{:S(2)}) collective-permute-start(bf16[512,128]{1,0:T(8,128)(2,1)S(1)} %collective-permute-done.other_ref.refs_0_), channel_id=1, source_target_pairs={{0,16},{16,0},{1,17},{17,1},{2,18},{18,2},{3,19},{19,3},{4,20},{20... | collective-permute-start | bytes 393224 | tf_op jit(solution)/shard_map/probes/ppermute | solution.py:234
  23.2 7.3 %collective-permute-start.7 = (bf16[512,128]{1,0:T(8,128)(2,1)S(1)}, bf16[512,128]{1,0:T(8,128)(2,1)S(1)}, u32[]{:S(2)}, u32[]{:S(2)}) collective-permute-start(bf16[512,128]{1,0:T(8,128)(2,1)S(1)} %collective-permute-done.3.refs_3_), channel_id=1, source_target_pairs={{0,16},{16,0},{1,17},{17,1},{2,18},{18,2},{3,19},{19,3},{4,20},{20... | collective-permute-start | bytes 393224 | tf_op jit(solution)/shard_map/probes/ppermute | solution.py:234
  26.7 3.9 %collective-permute-start.6 = (bf16[512,128]{1,0:T(8,128)(2,1)S(1)}, bf16[512,128]{1,0:T(8,128)(2,1)S(1)}, u32[]{:S(2)}, u32[]{:S(2)}) collective-permute-start(bf16[512,128]{1,0:T(8,128)(2,1)S(1)} %collective-permute-done.2.refs_2_), channel_id=1, source_target_pairs={{0,16},{16,0},{1,17},{17,1},{2,18},{18,2},{3,19},{19,3},{4,20},{20... | collective-permute-start | bytes 393224 | tf_op jit(solution)/shard_map/probes/ppermute | solution.py:234
  30.4 1.3 %collective-permute-start.5 = (bf16[512,128]{1,0:T(8,128)(2,1)S(1)}, bf16[512,128]{1,0:T(8,128)(2,1)S(1)}, u32[]{:S(2)}, u32[]{:S(2)}) collective-permute-start(bf16[512,128]{1,0:T(8,128)(2,1)S(1)} %collective-permute-done.1.refs_1_), channel_id=1, source_target_pairs={{0,16},{16,0},{1,17},{17,1},{2,18},{18,2},{3,19},{19,3},{4,20},{20... | collective-permute-start | bytes 393224 | tf_op jit(solution)/shard_map/probes/ppermute | solution.py:234
  59.4 1.3 %collective-permute-start.8 = (bf16[32,256]{1,0:T(8,128)(2,1)S(1)}, bf16[32,256]{1,0:T(8,128)(2,1)S(1)}, u32[]{:S(2)}, u32[]{:S(2)}) collective-permute-start(bf16[32,256]{1,0:T(8,128)(2,1)S(1)} %reduce_sum.12), channel_id=1, source_target_pairs={{0,16},{16,0},{1,17},{17,1},{2,18},{18,2},{3,19},{19,3},{4,20},{20... | collective-permute-start | bytes 49160 | tf_op jit(solution)/shard_map/spread/ppermute | solution.py:243

commit v11 on v10

--- a/solution.py
+++ b/solution.py
@@ -31,7 +31,7 @@
 
 
 def outgoing_parts(tiles, blocks, pairs, counts):
-    def kernel(blocks_ref, pairs_ref, counts_ref, tiles_ref, out_ref, held, parts, source, sems):
+    def kernel(blocks_ref, pairs_ref, counts_ref, tiles_ref, out_ref, held, source, sems):
         core = lax.axis_index("k")
         lanes = pl.ds(pl.multiple_of(lax.axis_index("y") * LANES, LANES), LANES)
 
@@ -57,19 +57,17 @@
         pick = jnp.where(wanted == lax.broadcasted_iota(jnp.int32, (PART, LANES), 1), 1.0, 0.0).astype(BF16)
         for s in range(SLOTS):
             copy(s).wait()
-        for s in range(SLOTS):
-            part = lax.dot_general(pick, held[s], (((1,), (1,)), ((), ())), preferred_element_type=F32)
-            for n in range(TILE // LANES):
-                parts[s, n * PART : (n + 1) * PART, :] = part[:, n * LANES : (n + 1) * LANES].astype(BF16)
-
         second = lax.broadcasted_iota(jnp.int32, (CODE, LANES), 0) >= CODE // CAP
         for d in range(GROUP):
             codes = []
             for j in range(CAP):
                 s = source[d * CAP + j]
                 there = jnp.maximum(s, 0)
-                full = jnp.where(s >= 0, 1.0, 0.0).astype(BF16)
-                out_ref[d, j * UNIT : (j + 1) * UNIT, :] = parts[there] * full
+                full = jnp.where(s >= 0, 1.0, 0.0)
+                part = lax.dot_general(pick, held[there], (((1,), (1,)), ((), ())), preferred_element_type=F32) * full
+                for n in range(TILE // LANES):
+                    start = j * UNIT + n * PART
+                    out_ref[d, start : start + PART, :] = part[:, n * LANES : (n + 1) * LANES].astype(BF16)
                 codes.append(pairs_ref[there].astype(F32))
             out_ref[d, CAP * UNIT :, :] = jnp.where(second, codes[1], codes[0]).astype(BF16)
 
@@ -80,7 +78,6 @@
         out_specs=VMEM,
         scratch_shapes=[
             pltpu.VMEM((SLOTS, TILE, LANES), BF16),
-            pltpu.VMEM((SLOTS, UNIT, LANES), BF16),
             pltpu.SMEM((GROUP * CAP,), jnp.int32),
             pltpu.SemaphoreType.DMA((SLOTS,)),
         ],

time: 77.4 us -> 77.4 us (level)
  no operation moved by 1% of the time
where the time goes in v11:
time: 77.4 us; the launch traced here: 76.6 us
  blocking collectives  30 us (39%)
  starting transfers between devices  22.2 us (29%)
  Pallas kernels  12.7 us (16%)
  waiting for transfers between devices  10.9 us (14%)
    all_to_all x1, blocking collectives, shards(): products = lax.all_to_all(products, ('u', 'z'), 0, 0, tiled=True)  18.1 us
    all_to_all x1, blocking collectives, shards(): lax.all_to_all(jnp.broadcast_to(both, (8,) + both.shape), ('f', 'y'), 0,...  11.9 us
    ppermute x4, starting transfers between devices, shards(): other = [lax.ppermute(columns, 'k', swap) for columns in own]  7.9 us
    all_to_all x1, starting transfers between devices, shards(): lax.all_to_all(after(parts, bank), ('k', 'u', 'z'), 0, 0, tiled=True, axi...  6.22 us
    all_to_all x1, waiting for transfers between devices, shards(): lax.all_to_all(after(parts, bank), ('k', 'u', 'z'), 0, 0, tiled=True, axi...  5.3 us
    ppermute x3, starting transfers between devices, shards(): lax.ppermute(bank, 'y', [(y, (y + n) % 4) for y in range(4)])  4.61 us
    pallas_call x1, Pallas kernels, outgoing_parts(): pl.pallas_call(kernel, out_shape=jax.ShapeDtypeStruct((GROUP, ROWS, LANES...  4.54 us
    pallas_call x1, Pallas kernels, screened_response(): pl.pallas_call(kernel, out_shape=jax.ShapeDtypeStruct((2, SET, rows), F32...  4.06 us
  transfers between devices with their start and end apart: 10, of which 5 were waited for; matrix products, arithmetic and copies ran while one was open for 0% of the time, Pallas kernels for 9%

profile of v11, /device:TPU:2, one launch (start us, length us, event | category | flops | bytes accessed | tf_op | source)
XLA Modules:
  0.0 76.6 jit_solution(9263171318200407638)
XLA Ops:
  0.0 3.3 %collective-permute-start = (bf16[512,128]{1,0:T(8,128)(2,1)}, bf16[512,128]{1,0:T(8,128)(2,1)S(1)}, u32[]{:S(2)}, u32[]{:S(2)}) collective-permute-start(bf16[512,128]{1,0:T(8,128)(2,1)} %param.18), channel_id=1, source_target_pairs={{0,6},{1,7},{2,0},{3,1},{4,2},{5,3},{6,4},{7,5},{128,130},{129,131... | collective-permute-start | bytes 393224 | tf_op jit(solution)/shard_map/parts/ppermute | solution.py:226
  3.9 4.5 %outgoing_parts.1.array_ref = bf16[8,528,128]{2,1,0:T(8,128)(2,1)} custom-call(s32[16]{0:T(128)} %bitcast.10, s32[16]{0:T(128)} %pairs_ref.1, s32[1]{0:T(128)S(6)} %copy.13.counts_ref, bf16[16,512,512]{2,1,0:T(8,128)(2,1)} %tiles_ref.1), custom_call_target="tpu_custom_call" | custom-call | tf_op jit(solution)/shard_map/parts/outgoing_parts/pallas_call | solution.py:74
  8.5 2.1 %collective-permute-done.other_ref.refs_0_ = bf16[512,128]{1,0:T(8,128)(2,1)S(1)} collective-permute-done((bf16[512,128]{1,0:T(8,128)(2,1)}, bf16[512,128]{1,0:T(8,128)(2,1)S(1)}, u32[]{:S(2)}, u32[]{:S(2)}) %collective-permute-start) | collective-permute-done | bytes 131104 | tf_op jit(solution)/shard_map/parts/ppermute | solution.py:226
  10.6 0.0 copy-start
  10.6 0.0 copy-start.1
  10.6 0.0 copy-start.2
  10.6 0.0 copy-start.3
  10.6 6.2 %all-to-all-start = ((bf16[8,528,128]{2,1,0:T(8,128)(2,1)}), bf16[8,528,128]{2,1,0:T(8,128)(2,1)S(1)}, u32[]{:S(2)}, u32[]{:S(2)}) async-start(bf16[8,528,128]{2,1,0:T(8,128)(2,1)} %after.1), calls=%async_computation | async-start | bytes 2162688 | tf_op jit(solution)/shard_map/parts/all_to_all | solution.py:228
  16.8 3.0 %collective-permute-start.3 = (bf16[512,128]{1,0:T(8,128)(2,1)S(1)}, bf16[512,128]{1,0:T(8,128)(2,1)S(1)}, u32[]{:S(2)}, u32[]{:S(2)}) collective-permute-start(bf16[512,128]{1,0:T(8,128)(2,1)S(1)} %collective-permute-done.other_ref.refs_0_), channel_id=1, source_target_pairs={{0,96},{32,0},{64,32},{96,64},{1,97},{33,1},{65,33},{97,65},{2,98}... | collective-permute-start | bytes 393224 | tf_op jit(solution)/shard_map/probes/ppermute | solution.py:230
  19.8 0.6 collective-permute-start.2
  20.5 1.0 %collective-permute-start.1 = (bf16[512,128]{1,0:T(8,128)(2,1)S(1)}, bf16[512,128]{1,0:T(8,128)(2,1)S(1)}, u32[]{:S(2)}, u32[]{:S(2)}) collective-permute-start(bf16[512,128]{1,0:T(8,128)(2,1)S(1)} %collective-permute-done.other_ref.refs_0_), channel_id=1, source_target_pairs={{0,32},{32,64},{64,96},{96,0},{1,33},{33,65},{65,97},{97,1},{2,34}... | collective-permute-start | bytes 393224 | tf_op jit(solution)/shard_map/probes/ppermute | solution.py:230
  21.4 1.8 %collective-permute-start.4 = (bf16[512,128]{1,0:T(8,128)(2,1)S(1)}, bf16[512,128]{1,0:T(8,128)(2,1)S(1)}, u32[]{:S(2)}, u32[]{:S(2)}) collective-permute-start(bf16[512,128]{1,0:T(8,128)(2,1)S(1)} %collective-permute-done.other_ref.refs_0_), channel_id=1, source_target_pairs={{0,16},{16,0},{1,17},{17,1},{2,18},{18,2},{3,19},{19,3},{4,20},{20... | collective-permute-start | bytes 393224 | tf_op jit(solution)/shard_map/probes/ppermute | solution.py:231
  23.2 0.0 collective-permute-done.3.refs_3_
  23.2 3.4 %collective-permute-start.7 = (bf16[512,128]{1,0:T(8,128)(2,1)S(1)}, bf16[512,128]{1,0:T(8,128)(2,1)S(1)}, u32[]{:S(2)}, u32[]{:S(2)}) collective-permute-start(bf16[512,128]{1,0:T(8,128)(2,1)S(1)} %collective-permute-done.3.refs_3_), channel_id=1, source_target_pairs={{0,16},{16,0},{1,17},{17,1},{2,18},{18,2},{3,19},{19,3},{4,20},{20... | collective-permute-start | bytes 393224 | tf_op jit(solution)/shard_map/probes/ppermute | solution.py:231
  26.7 0.0 collective-permute-done.2.refs_2_
  26.7 2.6 %collective-permute-start.6 = (bf16[512,128]{1,0:T(8,128)(2,1)S(1)}, bf16[512,128]{1,0:T(8,128)(2,1)S(1)}, u32[]{:S(2)}, u32[]{:S(2)}) collective-permute-start(bf16[512,128]{1,0:T(8,128)(2,1)S(1)} %collective-permute-done.2.refs_2_), channel_id=1, source_target_pairs={{0,16},{16,0},{1,17},{17,1},{2,18},{18,2},{3,19},{19,3},{4,20},{20... | collective-permute-start | bytes 393224 | tf_op jit(solution)/shard_map/probes/ppermute | solution.py:231
  29.2 1.2 %collective-permute-done.1.refs_1_ = bf16[512,128]{1,0:T(8,128)(2,1)S(1)} collective-permute-done((bf16[512,128]{1,0:T(8,128)(2,1)S(1)}, bf16[512,128]{1,0:T(8,128)(2,1)S(1)}, u32[]{:S(2)}, u32[]{:S(2)}) %collective-permute-start.1) | collective-permute-done | bytes 131104 | tf_op jit(solution)/shard_map/probes/ppermute | solution.py:230
  30.4 0.1 collective-permute-start.5
  30.5 0.0 collective-permute-done.4.refs_4_
  30.6 0.0 collective-permute-done.7.refs_7_
  30.6 0.0 collective-permute-done.6.refs_6_
  30.6 1.2 %collective-permute-done.5.refs_5_ = bf16[512,128]{1,0:T(8,128)(2,1)S(1)} collective-permute-done((bf16[512,128]{1,0:T(8,128)(2,1)S(1)}, bf16[512,128]{1,0:T(8,128)(2,1)S(1)}, u32[]{:S(2)}, u32[]{:S(2)}) %collective-permute-start.5) | collective-permute-done | bytes 131104 | tf_op jit(solution)/shard_map/probes/ppermute | solution.py:231
  31.8 0.0 copy-done
  31.8 0.0 copy-done.1
  31.8 0.0 copy-done.2
  31.8 0.0 copy-done.3
  31.8 2.6 %picked_probes.1 = (bf16[512,512]{1,0:T(8,128)(2,1)S(1)}, f32[2,2048]{1,0:T(2,128)S(1)}, bf16[384,2048]{1,0:T(8,128)(2,1)S(1)}) custom-call(f32[4]{0:T(128)S(1)} %copy-done.3, f32[4,4]{1,0:T(4,128)S(1)} %copy-done.1, bf16[512,128]{1,0:T(8,128)(2,1)S(1)} %collective-permute-done.other_ref.refs_0_, bf16[512,128]{1,0:T(8,128)(2,1)S(1)} %collective-permute-done.1.refs_1_, ...), custom_call_target="tpu_custom_call" | custom-call | tf_op jit(solution)/shard_map/probes/picked_probes/pallas_call | solution.py:126
  34.4 5.3 %all-to-all-done.parts_ref = bf16[8,528,128]{2,1,0:T(8,128)(2,1)S(1)} async-done(((bf16[8,528,128]{2,1,0:T(8,128)(2,1)}), bf16[8,528,128]{2,1,0:T(8,128)(2,1)S(1)}, u32[]{:S(2)}, u32[]{:S(2)}) %all-to-all-start) | async-done | bytes 1081376 | tf_op jit(solution)/shard_map/parts/all_to_all | solution.py:228
  39.7 1.5 %owner_products.1 = bf16[16,32,256]{2,1,0:T(8,128)(2,1)S(1)} custom-call(bf16[8,528,128]{2,1,0:T(8,128)(2,1)S(1)} %all-to-all-done.parts_ref, bf16[512,512]{1,0:T(8,128)(2,1)S(1)} %get-tuple-element.8.probes_ref), custom_call_target="tpu_custom_call" | custom-call | tf_op jit(solution)/shard_map/products/owner_products/pallas_call | solution.py:159
  41.2 18.1 %all_to_all.15 = bf16[16,32,256]{2,1,0:T(8,128)(2,1)S(1)} all-to-all(bf16[16,32,256]{2,1,0:T(8,128)(2,1)S(1)} %owner_products.1), channel_id=1, replica_groups=mesh['f'=2,'y'=4,'k'=2,'u'=2,'z'=8] {'u','z'}, dimensions={0} | all-to-all | bytes 524288 | tf_op jit(solution)/shard_map/products/all_to_all | solution.py:237
  59.4 0.2 collective-permute-start.8
  59.6 1.1 %collective-permute-done.8 = bf16[32,256]{1,0:T(8,128)(2,1)S(1)} collective-permute-done((bf16[32,256]{1,0:T(8,128)(2,1)S(1)}, bf16[32,256]{1,0:T(8,128)(2,1)S(1)}, u32[]{:S(2)}, u32[]{:S(2)}) %collective-permute-start.8) | collective-permute-done | bytes 16416 | tf_op jit(solution)/shard_map/spread/ppermute | solution.py:240
  60.7 11.9 %all_to_all.16.parts_ref = bf16[8,2,32,256]{3,2,1,0:T(8,128)(2,1)S(1)} all-to-all(bf16[8,2,32,256]{3,2,1,0:T(8,128)(2,1)S(1)} %broadcast_in_dim.3), channel_id=1, replica_groups=mesh['f'=2,'y'=4,'k'=2,'u'=2,'z'=8] {'f','y'}, dimensions={0} | all-to-all | bytes 524288 | tf_op jit(solution)/shard_map/spread/all_to_all | solution.py:241
  72.5 4.1 %screened_response.1 = f32[2,32,1024]{2,1,0:T(8,128)} custom-call(bf16[8,2,32,256]{3,2,1,0:T(8,128)(2,1)S(1)} %all_to_all.16.parts_ref, bf16[384,2048]{1,0:T(8,128)(2,1)S(1)} %get-tuple-element.9.first_ref, bf16[1024,2048]{1,0:T(8,128)(2,1)} %left_ref.1, f32[2,2048]{1,0:T(2,128)S(1)} %get-tuple-element.10.weights_ref), custom_call_target="tpu_custom_call" | custom-call | tf_op jit(solution)/shard_map/response/screened_response/pallas_call | solution.py:203
  (4 shorter events, 0.1 us)
Async XLA Ops:
  0.0 10.6 %collective-permute-start = (bf16[512,128]{1,0:T(8,128)(2,1)}, bf16[512,128]{1,0:T(8,128)(2,1)S(1)}, u32[]{:S(2)}, u32[]{:S(2)}) collective-permute-start(bf16[512,128]{1,0:T(8,128)(2,1)} %param.18), channel_id=1, source_target_pairs={{0,6},{1,7},{2,0},{3,1},{4,2},{5,3},{6,4},{7,5},{128,130},{129,131... | collective-permute-start | bytes 393224 | tf_op jit(solution)/shard_map/parts/ppermute | solution.py:226
  10.6 21.2 %copy-start = (f32[2048]{0:T(1024)S(1)}, f32[2048]{0:T(1024)}, u32[]{:S(2)}) copy-start(f32[2048]{0:T(1024)} %param.15) | copy-start | bytes 24580
  10.6 21.2 %copy-start.1 = (f32[4,4]{1,0:T(4,128)S(1)}, f32[4,4]{1,0:T(4,128)}, u32[]{:S(2)}) copy-start(f32[4,4]{1,0:T(4,128)} %cos_ref.1) | copy-start | bytes 196
  10.6 21.2 %copy-start.2 = (s32[512]{0:T(512)S(1)}, s32[512]{0:T(512)}, u32[]{:S(2)}) copy-start(s32[512]{0:T(512)} %param.19) | copy-start | bytes 6148
  10.6 21.2 %copy-start.3 = (f32[4]{0:T(128)S(1)}, f32[4]{0:T(128)}, u32[]{:S(2)}) copy-start(f32[4]{0:T(128)} %times_ref.1) | copy-start | bytes 52
  10.6 29.1 %all-to-all-start = ((bf16[8,528,128]{2,1,0:T(8,128)(2,1)}), bf16[8,528,128]{2,1,0:T(8,128)(2,1)S(1)}, u32[]{:S(2)}, u32[]{:S(2)}) async-start(bf16[8,528,128]{2,1,0:T(8,128)(2,1)} %after.1), calls=%async_computation | async-start | bytes 2162688 | tf_op jit(solution)/shard_map/parts/all_to_all | solution.py:228
  16.8 6.4 %collective-permute-start.3 = (bf16[512,128]{1,0:T(8,128)(2,1)S(1)}, bf16[512,128]{1,0:T(8,128)(2,1)S(1)}, u32[]{:S(2)}, u32[]{:S(2)}) collective-permute-start(bf16[512,128]{1,0:T(8,128)(2,1)S(1)} %collective-permute-done.other_ref.refs_0_), channel_id=1, source_target_pairs={{0,96},{32,0},{64,32},{96,64},{1,97},{33,1},{65,33},{97,65},{2,98}... | collective-permute-start | bytes 393224 | tf_op jit(solution)/shard_map/probes/ppermute | solution.py:230
  19.8 6.8 %collective-permute-start.2 = (bf16[512,128]{1,0:T(8,128)(2,1)S(1)}, bf16[512,128]{1,0:T(8,128)(2,1)S(1)}, u32[]{:S(2)}, u32[]{:S(2)}) collective-permute-start(bf16[512,128]{1,0:T(8,128)(2,1)S(1)} %collective-permute-done.other_ref.refs_0_), channel_id=1, source_target_pairs={{0,64},{32,96},{64,0},{96,32},{1,65},{33,97},{65,1},{97,33},{2,66}... | collective-permute-start | bytes 393224 | tf_op jit(solution)/shard_map/probes/ppermute | solution.py:230
  20.5 10.0 %collective-permute-start.1 = (bf16[512,128]{1,0:T(8,128)(2,1)S(1)}, bf16[512,128]{1,0:T(8,128)(2,1)S(1)}, u32[]{:S(2)}, u32[]{:S(2)}) collective-permute-start(bf16[512,128]{1,0:T(8,128)(2,1)S(1)} %collective-permute-done.other_ref.refs_0_), channel_id=1, source_target_pairs={{0,32},{32,64},{64,96},{96,0},{1,33},{33,65},{65,97},{97,1},{2,34}... | collective-permute-start | bytes 393224 | tf_op jit(solution)/shard_map/probes/ppermute | solution.py:230
  21.4 9.1 %collective-permute-start.4 = (bf16[512,128]{1,0:T(8,128)(2,1)S(1)}, bf16[512,128]{1,0:T(8,128)(2,1)S(1)}, u32[]{:S(2)}, u32[]{:S(2)}) collective-permute-start(bf16[512,128]{1,0:T(8,128)(2,1)S(1)} %collective-permute-done.other_ref.refs_0_), channel_id=1, source_target_pairs={{0,16},{16,0},{1,17},{17,1},{2,18},{18,2},{3,19},{19,3},{4,20},{20... | collective-permute-start | bytes 393224 | tf_op jit(solution)/shard_map/probes/ppermute | solution.py:231
  23.2 7.3 %collective-permute-start.7 = (bf16[512,128]{1,0:T(8,128)(2,1)S(1)}, bf16[512,128]{1,0:T(8,128)(2,1)S(1)}, u32[]{:S(2)}, u32[]{:S(2)}) collective-permute-start(bf16[512,128]{1,0:T(8,128)(2,1)S(1)} %collective-permute-done.3.refs_3_), channel_id=1, source_target_pairs={{0,16},{16,0},{1,17},{17,1},{2,18},{18,2},{3,19},{19,3},{4,20},{20... | collective-permute-start | bytes 393224 | tf_op jit(solution)/shard_map/probes/ppermute | solution.py:231
  26.7 3.9 %collective-permute-start.6 = (bf16[512,128]{1,0:T(8,128)(2,1)S(1)}, bf16[512,128]{1,0:T(8,128)(2,1)S(1)}, u32[]{:S(2)}, u32[]{:S(2)}) collective-permute-start(bf16[512,128]{1,0:T(8,128)(2,1)S(1)} %collective-permute-done.2.refs_2_), channel_id=1, source_target_pairs={{0,16},{16,0},{1,17},{17,1},{2,18},{18,2},{3,19},{19,3},{4,20},{20... | collective-permute-start | bytes 393224 | tf_op jit(solution)/shard_map/probes/ppermute | solution.py:231
  30.4 1.3 %collective-permute-start.5 = (bf16[512,128]{1,0:T(8,128)(2,1)S(1)}, bf16[512,128]{1,0:T(8,128)(2,1)S(1)}, u32[]{:S(2)}, u32[]{:S(2)}) collective-permute-start(bf16[512,128]{1,0:T(8,128)(2,1)S(1)} %collective-permute-done.1.refs_1_), channel_id=1, source_target_pairs={{0,16},{16,0},{1,17},{17,1},{2,18},{18,2},{3,19},{19,3},{4,20},{20... | collective-permute-start | bytes 393224 | tf_op jit(solution)/shard_map/probes/ppermute | solution.py:231
  59.4 1.3 %collective-permute-start.8 = (bf16[32,256]{1,0:T(8,128)(2,1)S(1)}, bf16[32,256]{1,0:T(8,128)(2,1)S(1)}, u32[]{:S(2)}, u32[]{:S(2)}) collective-permute-start(bf16[32,256]{1,0:T(8,128)(2,1)S(1)} %reduce_sum.12), channel_id=1, source_target_pairs={{0,16},{16,0},{1,17},{17,1},{2,18},{18,2},{3,19},{19,3},{4,20},{20... | collective-permute-start | bytes 49160 | tf_op jit(solution)/shard_map/spread/ppermute | solution.py:240

commit v12 on v10

--- a/solution.py
+++ b/solution.py
@@ -173,27 +173,24 @@
 def screened_response(parts, first, left_panel, weights):
     cut, rows = first.shape[0], left_panel.shape[0]
 
-    def kernel(parts_ref, first_ref, left_ref, weights_ref, out_ref, scaled, second, sem):
+    def kernel(*refs):
+        part_refs, (first_ref, left_ref, weights_ref, out_ref, scaled, second, sem) = refs[:4], refs[4:]
         fetch = pltpu.make_async_copy(left_ref.at[pl.ds(cut, rows - cut), :], second, sem)
         fetch.start()
         core = lax.axis_index("k")
         low = lax.broadcasted_iota(jnp.int32, (SET, LANES), 1) < PART
-        for y in range(4):
-            held = [
-                parts_ref[y, jnp.abs(core - k)].astype(F32) + parts_ref[4 + y, jnp.abs(core - k)].astype(F32)
-                for k in range(2)
-            ]
+        for n, part_ref in enumerate(part_refs):
+            y = (lax.axis_index("y") + 4 - n) % 4
+            held = [part_ref[jnp.abs(core - k)].astype(F32) for k in range(2)]
             for m in range(MB):
                 start = m // 2 * LANES
                 both = [held[k][:, start : start + LANES] for k in range(2)]
                 turned = 1 - m % 2
                 both[turned] = pltpu.roll(both[turned], PART, 1)
                 whole = jnp.where(low, both[0], both[1])
-                at = (m * 4 + y) * LANES
+                at = pl.ds(pl.multiple_of((m * 4 + y) * LANES, LANES), LANES)
                 for f in range(2):
-                    scaled[f * SET : (f + 1) * SET, at : at + LANES] = (
-                        whole * weights_ref[f : f + 1, at : at + LANES]
-                    ).astype(BF16)
+                    scaled[f * SET : (f + 1) * SET, at] = (whole * weights_ref[f : f + 1, at]).astype(BF16)
         for left, start, stop in ((first_ref, 0, cut), (second, cut, rows)):
             if start == cut:
                 fetch.wait()
@@ -206,7 +203,7 @@
     return pl.pallas_call(
         kernel,
         out_shape=jax.ShapeDtypeStruct((2, SET, rows), F32),
-        in_specs=[VMEM, VMEM, HBM, VMEM],
+        in_specs=[VMEM] * 5 + [HBM, VMEM],
         out_specs=VMEM,
         scratch_shapes=[
             pltpu.VMEM((2 * SET, NPAIR), BF16),
@@ -215,7 +212,7 @@
         ],
         compiler_params=pltpu.CompilerParams(vmem_limit_bytes=12 << 20),
         name="screened_response",
-    )(parts, first, left_panel, weights)
+    )(*parts, first, left_panel, weights)
 
 
 def shards(
@@ -240,8 +237,9 @@
         products = lax.all_to_all(products, ("u", "z"), 0, 0, tiled=True)
         product = jnp.sum(products.astype(F32), axis=0).astype(BF16)
     with jax.named_scope("spread"):
+        product = (product.astype(F32) + lax.ppermute(product, "f", swap).astype(F32)).astype(BF16)
         both = jnp.stack([product, lax.ppermute(product, "k", swap)])
-        both = lax.all_to_all(jnp.broadcast_to(both, (8,) + both.shape), ("f", "y"), 0, 0, tiled=True)
+        both = [both] + [lax.ppermute(both, "y", [(y, (y + n) % 4) for y in range(4)]) for n in (1, 2, 3)]
     with jax.named_scope("response"):
         turned = screened_response(both, first, left_panel, weights)
         return jnp.swapaxes(turned, 1, 2)

time: 77.4 us -> 77.2 us (level)
  blocking collectives: 30 us -> 18.1 us
  waiting for transfers between devices: 10.8 us -> 18.8 us
  starting transfers between devices: 22.2 us -> 26.8 us
    all_to_all x1 -> x0, blocking collectives: 11.9 us -> none  [shards(): lax.all_to_all(jnp.broadcast_to(both, (8,) + both.shape), ('f', 'y'), 0,...]
    ppermute x0 -> x4, waiting for transfers between devices: none -> 7.89 us  [the longest x3 4.17 us: shards(): lax.ppermute(both, 'y', [(y, (y + n) % 4) for y in range(4)])]
    ppermute x0 -> x4, starting transfers between devices: none -> 4.71 us  [the longest x3 4.62 us: shards(): lax.ppermute(both, 'y', [(y, (y + n) % 4) for y in range(4)])]
  transfers between devices with their start and end apart: 10 -> 14, of which waited for: 5 -> 9; matrix products, arithmetic and copies ran while one was open for 0% -> 0% of each run, Pallas kernels for 9% -> 9%
where the time goes in v12:
time: 77.2 us; the launch traced here: 76.9 us
  starting transfers between devices  26.8 us (35%)
  waiting for transfers between devices  18.8 us (24%)
  blocking collectives  18.1 us (23%)
  Pallas kernels  12.3 us (16%)
    all_to_all x1, blocking collectives, shards(): products = lax.all_to_all(products, ('u', 'z'), 0, 0, tiled=True)  18.1 us
    ppermute x4, starting transfers between devices, shards(): other = [lax.ppermute(columns, 'k', swap) for columns in own]  7.9 us
    all_to_all x1, starting transfers between devices, shards(): lax.all_to_all(after(parts, bank), ('k', 'u', 'z'), 0, 0, tiled=True, axi...  6.22 us
    all_to_all x1, waiting for transfers between devices, shards(): lax.all_to_all(after(parts, bank), ('k', 'u', 'z'), 0, 0, tiled=True, axi...  5.3 us
    pallas_call x1, Pallas kernels, outgoing_parts(): pl.pallas_call(kernel, out_shape=jax.ShapeDtypeStruct((GROUP, ROWS, LANES...  4.67 us
    ppermute x3, starting transfers between devices, shards(): lax.ppermute(both, 'y', [(y, (y + n) % 4) for y in range(4)])  4.62 us
    ppermute x3, starting transfers between devices, shards(): lax.ppermute(bank, 'y', [(y, (y + n) % 4) for y in range(4)])  4.61 us
    ppermute x3, waiting for transfers between devices, shards(): lax.ppermute(both, 'y', [(y, (y + n) % 4) for y in range(4)])  4.17 us
  transfers between devices with their start and end apart: 14, of which 9 were waited for; matrix products, arithmetic and copies ran while one was open for 0% of the time, Pallas kernels for 9%

profile of v12, /device:TPU:2, one launch (start us, length us, event | category | flops | bytes accessed | tf_op | source)
XLA Modules:
  0.0 76.9 jit_solution(18353663734160664144)
XLA Ops:
  0.0 3.3 %collective-permute-start = (bf16[512,128]{1,0:T(8,128)(2,1)}, bf16[512,128]{1,0:T(8,128)(2,1)S(1)}, u32[]{:S(2)}, u32[]{:S(2)}) collective-permute-start(bf16[512,128]{1,0:T(8,128)(2,1)} %param.18), channel_id=1, source_target_pairs={{0,6},{1,7},{2,0},{3,1},{4,2},{5,3},{6,4},{7,5},{128,130},{129,131... | collective-permute-start | bytes 393224 | tf_op jit(solution)/shard_map/parts/ppermute | solution.py:226
  3.9 4.7 %outgoing_parts.1.array_ref = bf16[8,528,128]{2,1,0:T(8,128)(2,1)} custom-call(s32[16]{0:T(128)} %bitcast.10, s32[16]{0:T(128)} %pairs_ref.1, s32[1]{0:T(128)S(6)} %copy.13.counts_ref, bf16[16,512,512]{2,1,0:T(8,128)(2,1)} %tiles_ref.1), custom_call_target="tpu_custom_call" | custom-call | tf_op jit(solution)/shard_map/parts/outgoing_parts/pallas_call | solution.py:76
  8.6 2.0 %collective-permute-done.other_ref.refs_0_ = bf16[512,128]{1,0:T(8,128)(2,1)S(1)} collective-permute-done((bf16[512,128]{1,0:T(8,128)(2,1)}, bf16[512,128]{1,0:T(8,128)(2,1)S(1)}, u32[]{:S(2)}, u32[]{:S(2)}) %collective-permute-start) | collective-permute-done | bytes 131104 | tf_op jit(solution)/shard_map/parts/ppermute | solution.py:226
  10.6 0.0 copy-start
  10.6 0.0 copy-start.1
  10.6 0.0 copy-start.2
  10.6 0.0 copy-start.3
  10.6 6.2 %all-to-all-start = ((bf16[8,528,128]{2,1,0:T(8,128)(2,1)}), bf16[8,528,128]{2,1,0:T(8,128)(2,1)S(1)}, u32[]{:S(2)}, u32[]{:S(2)}) async-start(bf16[8,528,128]{2,1,0:T(8,128)(2,1)} %after.1), calls=%async_computation | async-start | bytes 2162688 | tf_op jit(solution)/shard_map/parts/all_to_all | solution.py:228
  16.8 3.0 %collective-permute-start.3 = (bf16[512,128]{1,0:T(8,128)(2,1)S(1)}, bf16[512,128]{1,0:T(8,128)(2,1)S(1)}, u32[]{:S(2)}, u32[]{:S(2)}) collective-permute-start(bf16[512,128]{1,0:T(8,128)(2,1)S(1)} %collective-permute-done.other_ref.refs_0_), channel_id=1, source_target_pairs={{0,96},{32,0},{64,32},{96,64},{1,97},{33,1},{65,33},{97,65},{2,98}... | collective-permute-start | bytes 393224 | tf_op jit(solution)/shard_map/probes/ppermute | solution.py:230
  19.8 0.6 collective-permute-start.2
  20.5 1.0 %collective-permute-start.1 = (bf16[512,128]{1,0:T(8,128)(2,1)S(1)}, bf16[512,128]{1,0:T(8,128)(2,1)S(1)}, u32[]{:S(2)}, u32[]{:S(2)}) collective-permute-start(bf16[512,128]{1,0:T(8,128)(2,1)S(1)} %collective-permute-done.other_ref.refs_0_), channel_id=1, source_target_pairs={{0,32},{32,64},{64,96},{96,0},{1,33},{33,65},{65,97},{97,1},{2,34}... | collective-permute-start | bytes 393224 | tf_op jit(solution)/shard_map/probes/ppermute | solution.py:230
  21.4 1.8 %collective-permute-start.4 = (bf16[512,128]{1,0:T(8,128)(2,1)S(1)}, bf16[512,128]{1,0:T(8,128)(2,1)S(1)}, u32[]{:S(2)}, u32[]{:S(2)}) collective-permute-start(bf16[512,128]{1,0:T(8,128)(2,1)S(1)} %collective-permute-done.other_ref.refs_0_), channel_id=1, source_target_pairs={{0,16},{16,0},{1,17},{17,1},{2,18},{18,2},{3,19},{19,3},{4,20},{20... | collective-permute-start | bytes 393224 | tf_op jit(solution)/shard_map/probes/ppermute | solution.py:231
  23.2 0.0 collective-permute-done.3.refs_3_
  23.2 3.4 %collective-permute-start.7 = (bf16[512,128]{1,0:T(8,128)(2,1)S(1)}, bf16[512,128]{1,0:T(8,128)(2,1)S(1)}, u32[]{:S(2)}, u32[]{:S(2)}) collective-permute-start(bf16[512,128]{1,0:T(8,128)(2,1)S(1)} %collective-permute-done.3.refs_3_), channel_id=1, source_target_pairs={{0,16},{16,0},{1,17},{17,1},{2,18},{18,2},{3,19},{19,3},{4,20},{20... | collective-permute-start | bytes 393224 | tf_op jit(solution)/shard_map/probes/ppermute | solution.py:231
  26.7 0.0 collective-permute-done.2.refs_2_
  26.7 2.6 %collective-permute-start.6 = (bf16[512,128]{1,0:T(8,128)(2,1)S(1)}, bf16[512,128]{1,0:T(8,128)(2,1)S(1)}, u32[]{:S(2)}, u32[]{:S(2)}) collective-permute-start(bf16[512,128]{1,0:T(8,128)(2,1)S(1)} %collective-permute-done.2.refs_2_), channel_id=1, source_target_pairs={{0,16},{16,0},{1,17},{17,1},{2,18},{18,2},{3,19},{19,3},{4,20},{20... | collective-permute-start | bytes 393224 | tf_op jit(solution)/shard_map/probes/ppermute | solution.py:231
  29.2 1.2 %collective-permute-done.1.refs_1_ = bf16[512,128]{1,0:T(8,128)(2,1)S(1)} collective-permute-done((bf16[512,128]{1,0:T(8,128)(2,1)S(1)}, bf16[512,128]{1,0:T(8,128)(2,1)S(1)}, u32[]{:S(2)}, u32[]{:S(2)}) %collective-permute-start.1) | collective-permute-done | bytes 131104 | tf_op jit(solution)/shard_map/probes/ppermute | solution.py:230
  30.4 0.1 collective-permute-start.5
  30.5 0.0 collective-permute-done.4.refs_4_
  30.6 0.0 collective-permute-done.7.refs_7_
  30.6 0.0 collective-permute-done.6.refs_6_
  30.6 1.2 %collective-permute-done.5.refs_5_ = bf16[512,128]{1,0:T(8,128)(2,1)S(1)} collective-permute-done((bf16[512,128]{1,0:T(8,128)(2,1)S(1)}, bf16[512,128]{1,0:T(8,128)(2,1)S(1)}, u32[]{:S(2)}, u32[]{:S(2)}) %collective-permute-start.5) | collective-permute-done | bytes 131104 | tf_op jit(solution)/shard_map/probes/ppermute | solution.py:231
  31.8 0.0 copy-done
  31.8 0.0 copy-done.1
  31.8 0.0 copy-done.2
  31.8 0.0 copy-done.3
  31.8 2.6 %picked_probes.1 = (bf16[512,512]{1,0:T(8,128)(2,1)S(1)}, f32[2,2048]{1,0:T(2,128)S(1)}, bf16[384,2048]{1,0:T(8,128)(2,1)S(1)}) custom-call(f32[4]{0:T(128)S(1)} %copy-done.3, f32[4,4]{1,0:T(4,128)S(1)} %copy-done.1, bf16[512,128]{1,0:T(8,128)(2,1)S(1)} %collective-permute-done.other_ref.refs_0_, bf16[512,128]{1,0:T(8,128)(2,1)S(1)} %collective-permute-done.1.refs_1_, ...), custom_call_target="tpu_custom_call" | custom-call | tf_op jit(solution)/shard_map/probes/picked_probes/pallas_call | solution.py:129
  34.4 5.3 %all-to-all-done.parts_ref = bf16[8,528,128]{2,1,0:T(8,128)(2,1)S(1)} async-done(((bf16[8,528,128]{2,1,0:T(8,128)(2,1)}), bf16[8,528,128]{2,1,0:T(8,128)(2,1)S(1)}, u32[]{:S(2)}, u32[]{:S(2)}) %all-to-all-start) | async-done | bytes 1081376 | tf_op jit(solution)/shard_map/parts/all_to_all | solution.py:228
  39.7 1.5 %owner_products.1 = bf16[16,32,256]{2,1,0:T(8,128)(2,1)S(1)} custom-call(bf16[8,528,128]{2,1,0:T(8,128)(2,1)S(1)} %all-to-all-done.parts_ref, bf16[512,512]{1,0:T(8,128)(2,1)S(1)} %get-tuple-element.8.probes_ref), custom_call_target="tpu_custom_call" | custom-call | tf_op jit(solution)/shard_map/products/owner_products/pallas_call | solution.py:162
  41.2 18.1 %all_to_all.10 = bf16[16,32,256]{2,1,0:T(8,128)(2,1)S(1)} all-to-all(bf16[16,32,256]{2,1,0:T(8,128)(2,1)S(1)} %owner_products.1), channel_id=1, replica_groups=mesh['f'=2,'y'=4,'k'=2,'u'=2,'z'=8] {'u','z'}, dimensions={0} | all-to-all | bytes 524288 | tf_op jit(solution)/shard_map/products/all_to_all | solution.py:237
  59.4 0.1 collective-permute-start.8
  59.5 3.7 %collective-permute-done.8 = bf16[32,256]{1,0:T(8,128)(2,1)S(1)} collective-permute-done((bf16[32,256]{1,0:T(8,128)(2,1)S(1)}, bf16[32,256]{1,0:T(8,128)(2,1)S(1)}, u32[]{:S(2)}, u32[]{:S(2)}) %collective-permute-start.8) | collective-permute-done | bytes 16416 | tf_op jit(solution)/shard_map/spread/ppermute | solution.py:240
  63.2 0.1 collective-permute-start.9
  63.3 1.2 %collective-permute-done.9 = bf16[32,256]{1,0:T(8,128)(2,1)S(1)} collective-permute-done((bf16[32,256]{1,0:T(8,128)(2,1)S(1)}, bf16[32,256]{1,0:T(8,128)(2,1)S(1)}, u32[]{:S(2)}, u32[]{:S(2)}) %collective-permute-start.9) | collective-permute-done | bytes 16416 | tf_op jit(solution)/shard_map/spread/ppermute | solution.py:241
  64.5 3.0 %collective-permute-start.12 = (bf16[2,32,256]{2,1,0:T(8,128)(2,1)S(1)}, bf16[2,32,256]{2,1,0:T(8,128)(2,1)S(1)}, u32[]{:S(2)}, u32[]{:S(2)}) collective-permute-start(bf16[2,32,256]{2,1,0:T(8,128)(2,1)S(1)} %pad_maximum_fusion.refs_0_), channel_id=1, source_target_pairs={{0,96},{32,0},{64,32},{96,64},{1,97},{33,1},{65,33},{97,65},{2,98}... | collective-permute-start | bytes 98312 | tf_op jit(solution)/shard_map/spread/ppermute | solution.py:242
  67.5 0.6 collective-permute-start.11
  68.1 1.0 %collective-permute-start.10 = (bf16[2,32,256]{2,1,0:T(8,128)(2,1)S(1)}, bf16[2,32,256]{2,1,0:T(8,128)(2,1)S(1)}, u32[]{:S(2)}, u32[]{:S(2)}) collective-permute-start(bf16[2,32,256]{2,1,0:T(8,128)(2,1)S(1)} %pad_maximum_fusion.refs_0_), channel_id=1, source_target_pairs={{0,32},{32,64},{64,96},{96,0},{1,33},{33,65},{65,97},{97,1},{2,34}... | collective-permute-start | bytes 98312 | tf_op jit(solution)/shard_map/spread/ppermute | solution.py:242
  69.1 0.2 collective-permute-done.12.refs_3_
  69.3 3.6 %collective-permute-done.11.refs_2_ = bf16[2,32,256]{2,1,0:T(8,128)(2,1)S(1)} collective-permute-done((bf16[2,32,256]{2,1,0:T(8,128)(2,1)S(1)}, bf16[2,32,256]{2,1,0:T(8,128)(2,1)S(1)}, u32[]{:S(2)}, u32[]{:S(2)}) %collective-permute-start.11) | collective-permute-done | bytes 32800 | tf_op jit(solution)/shard_map/spread/ppermute | solution.py:242
  72.9 0.4 collective-permute-done.10.refs_1_
  73.3 3.6 %screened_response.1 = f32[2,32,1024]{2,1,0:T(8,128)} custom-call(bf16[2,32,256]{2,1,0:T(8,128)(2,1)S(1)} %pad_maximum_fusion.refs_0_, bf16[2,32,256]{2,1,0:T(8,128)(2,1)S(1)} %collective-permute-done.10.refs_1_, bf16[2,32,256]{2,1,0:T(8,128)(2,1)S(1)} %collective-permute-done.11.refs_2_, bf16[2,32,256]{2,1,0:T(8,128)(2,1)S(1)} %collective-permute-done.12.refs_3_, ...), custom_call_target="tpu_custom_call" | custom-call | tf_op jit(solution)/shard_map/response/screened_response/pallas_call | solution.py:203
  (4 shorter events, 0.1 us)
Async XLA Ops:
  0.0 10.6 %collective-permute-start = (bf16[512,128]{1,0:T(8,128)(2,1)}, bf16[512,128]{1,0:T(8,128)(2,1)S(1)}, u32[]{:S(2)}, u32[]{:S(2)}) collective-permute-start(bf16[512,128]{1,0:T(8,128)(2,1)} %param.18), channel_id=1, source_target_pairs={{0,6},{1,7},{2,0},{3,1},{4,2},{5,3},{6,4},{7,5},{128,130},{129,131... | collective-permute-start | bytes 393224 | tf_op jit(solution)/shard_map/parts/ppermute | solution.py:226
  10.6 21.2 %copy-start = (f32[2048]{0:T(1024)S(1)}, f32[2048]{0:T(1024)}, u32[]{:S(2)}) copy-start(f32[2048]{0:T(1024)} %param.15) | copy-start | bytes 24580
  10.6 21.2 %copy-start.1 = (f32[4,4]{1,0:T(4,128)S(1)}, f32[4,4]{1,0:T(4,128)}, u32[]{:S(2)}) copy-start(f32[4,4]{1,0:T(4,128)} %cos_ref.1) | copy-start | bytes 196
  10.6 21.2 %copy-start.2 = (s32[512]{0:T(512)S(1)}, s32[512]{0:T(512)}, u32[]{:S(2)}) copy-start(s32[512]{0:T(512)} %param.19) | copy-start | bytes 6148
  10.6 21.2 %copy-start.3 = (f32[4]{0:T(128)S(1)}, f32[4]{0:T(128)}, u32[]{:S(2)}) copy-start(f32[4]{0:T(128)} %times_ref.1) | copy-start | bytes 52
  10.6 29.1 %all-to-all-start = ((bf16[8,528,128]{2,1,0:T(8,128)(2,1)}), bf16[8,528,128]{2,1,0:T(8,128)(2,1)S(1)}, u32[]{:S(2)}, u32[]{:S(2)}) async-start(bf16[8,528,128]{2,1,0:T(8,128)(2,1)} %after.1), calls=%async_computation | async-start | bytes 2162688 | tf_op jit(solution)/shard_map/parts/all_to_all | solution.py:228
  16.8 6.4 %collective-permute-start.3 = (bf16[512,128]{1,0:T(8,128)(2,1)S(1)}, bf16[512,128]{1,0:T(8,128)(2,1)S(1)}, u32[]{:S(2)}, u32[]{:S(2)}) collective-permute-start(bf16[512,128]{1,0:T(8,128)(2,1)S(1)} %collective-permute-done.other_ref.refs_0_), channel_id=1, source_target_pairs={{0,96},{32,0},{64,32},{96,64},{1,97},{33,1},{65,33},{97,65},{2,98}... | collective-permute-start | bytes 393224 | tf_op jit(solution)/shard_map/probes/ppermute | solution.py:230
  19.8 6.8 %collective-permute-start.2 = (bf16[512,128]{1,0:T(8,128)(2,1)S(1)}, bf16[512,128]{1,0:T(8,128)(2,1)S(1)}, u32[]{:S(2)}, u32[]{:S(2)}) collective-permute-start(bf16[512,128]{1,0:T(8,128)(2,1)S(1)} %collective-permute-done.other_ref.refs_0_), channel_id=1, source_target_pairs={{0,64},{32,96},{64,0},{96,32},{1,65},{33,97},{65,1},{97,33},{2,66}... | collective-permute-start | bytes 393224 | tf_op jit(solution)/shard_map/probes/ppermute | solution.py:230
  20.5 10.0 %collective-permute-start.1 = (bf16[512,128]{1,0:T(8,128)(2,1)S(1)}, bf16[512,128]{1,0:T(8,128)(2,1)S(1)}, u32[]{:S(2)}, u32[]{:S(2)}) collective-permute-start(bf16[512,128]{1,0:T(8,128)(2,1)S(1)} %collective-permute-done.other_ref.refs_0_), channel_id=1, source_target_pairs={{0,32},{32,64},{64,96},{96,0},{1,33},{33,65},{65,97},{97,1},{2,34}... | collective-permute-start | bytes 393224 | tf_op jit(solution)/shard_map/probes/ppermute | solution.py:230
  21.4 9.1 %collective-permute-start.4 = (bf16[512,128]{1,0:T(8,128)(2,1)S(1)}, bf16[512,128]{1,0:T(8,128)(2,1)S(1)}, u32[]{:S(2)}, u32[]{:S(2)}) collective-permute-start(bf16[512,128]{1,0:T(8,128)(2,1)S(1)} %collective-permute-done.other_ref.refs_0_), channel_id=1, source_target_pairs={{0,16},{16,0},{1,17},{17,1},{2,18},{18,2},{3,19},{19,3},{4,20},{20... | collective-permute-start | bytes 393224 | tf_op jit(solution)/shard_map/probes/ppermute | solution.py:231
  23.2 7.3 %collective-permute-start.7 = (bf16[512,128]{1,0:T(8,128)(2,1)S(1)}, bf16[512,128]{1,0:T(8,128)(2,1)S(1)}, u32[]{:S(2)}, u32[]{:S(2)}) collective-permute-start(bf16[512,128]{1,0:T(8,128)(2,1)S(1)} %collective-permute-done.3.refs_3_), channel_id=1, source_target_pairs={{0,16},{16,0},{1,17},{17,1},{2,18},{18,2},{3,19},{19,3},{4,20},{20... | collective-permute-start | bytes 393224 | tf_op jit(solution)/shard_map/probes/ppermute | solution.py:231
  26.7 3.9 %collective-permute-start.6 = (bf16[512,128]{1,0:T(8,128)(2,1)S(1)}, bf16[512,128]{1,0:T(8,128)(2,1)S(1)}, u32[]{:S(2)}, u32[]{:S(2)}) collective-permute-start(bf16[512,128]{1,0:T(8,128)(2,1)S(1)} %collective-permute-done.2.refs_2_), channel_id=1, source_target_pairs={{0,16},{16,0},{1,17},{17,1},{2,18},{18,2},{3,19},{19,3},{4,20},{20... | collective-permute-start | bytes 393224 | tf_op jit(solution)/shard_map/probes/ppermute | solution.py:231
  30.4 1.3 %collective-permute-start.5 = (bf16[512,128]{1,0:T(8,128)(2,1)S(1)}, bf16[512,128]{1,0:T(8,128)(2,1)S(1)}, u32[]{:S(2)}, u32[]{:S(2)}) collective-permute-start(bf16[512,128]{1,0:T(8,128)(2,1)S(1)} %collective-permute-done.1.refs_1_), channel_id=1, source_target_pairs={{0,16},{16,0},{1,17},{17,1},{2,18},{18,2},{3,19},{19,3},{4,20},{20... | collective-permute-start | bytes 393224 | tf_op jit(solution)/shard_map/probes/ppermute | solution.py:231
  59.4 3.8 %collective-permute-start.8 = (bf16[32,256]{1,0:T(8,128)(2,1)S(1)}, bf16[32,256]{1,0:T(8,128)(2,1)S(1)}, u32[]{:S(2)}, u32[]{:S(2)}) collective-permute-start(bf16[32,256]{1,0:T(8,128)(2,1)S(1)} %reduce_sum.12), channel_id=1, source_target_pairs={{0,128},{128,0},{1,129},{129,1},{2,130},{130,2},{3,131},{131,3},{4... | collective-permute-start | bytes 49160 | tf_op jit(solution)/shard_map/spread/ppermute | solution.py:240
  63.2 1.3 %collective-permute-start.9 = (bf16[32,256]{1,0:T(8,128)(2,1)S(1)}, bf16[32,256]{1,0:T(8,128)(2,1)S(1)}, u32[]{:S(2)}, u32[]{:S(2)}) collective-permute-start(bf16[32,256]{1,0:T(8,128)(2,1)S(1)} %add_convert_fusion), channel_id=1, source_target_pairs={{0,16},{16,0},{1,17},{17,1},{2,18},{18,2},{3,19},{19,3},{4,20},{20... | collective-permute-start | bytes 49160 | tf_op jit(solution)/shard_map/spread/ppermute | solution.py:241
  64.5 4.8 %collective-permute-start.12 = (bf16[2,32,256]{2,1,0:T(8,128)(2,1)S(1)}, bf16[2,32,256]{2,1,0:T(8,128)(2,1)S(1)}, u32[]{:S(2)}, u32[]{:S(2)}) collective-permute-start(bf16[2,32,256]{2,1,0:T(8,128)(2,1)S(1)} %pad_maximum_fusion.refs_0_), channel_id=1, source_target_pairs={{0,96},{32,0},{64,32},{96,64},{1,97},{33,1},{65,33},{97,65},{2,98}... | collective-permute-start | bytes 98312 | tf_op jit(solution)/shard_map/spread/ppermute | solution.py:242
  67.5 5.4 %collective-permute-start.11 = (bf16[2,32,256]{2,1,0:T(8,128)(2,1)S(1)}, bf16[2,32,256]{2,1,0:T(8,128)(2,1)S(1)}, u32[]{:S(2)}, u32[]{:S(2)}) collective-permute-start(bf16[2,32,256]{2,1,0:T(8,128)(2,1)S(1)} %pad_maximum_fusion.refs_0_), channel_id=1, source_target_pairs={{0,64},{32,96},{64,0},{96,32},{1,65},{33,97},{65,1},{97,33},{2,66}... | collective-permute-start | bytes 98312 | tf_op jit(solution)/shard_map/spread/ppermute | solution.py:242
  68.1 5.1 %collective-permute-start.10 = (bf16[2,32,256]{2,1,0:T(8,128)(2,1)S(1)}, bf16[2,32,256]{2,1,0:T(8,128)(2,1)S(1)}, u32[]{:S(2)}, u32[]{:S(2)}) collective-permute-start(bf16[2,32,256]{2,1,0:T(8,128)(2,1)S(1)} %pad_maximum_fusion.refs_0_), channel_id=1, source_target_pairs={{0,32},{32,64},{64,96},{96,0},{1,33},{33,65},{65,97},{97,1},{2,34}... | collective-permute-start | bytes 98312 | tf_op jit(solution)/shard_map/spread/ppermute | solution.py:242

commit v13 on v10

--- a/solution.py
+++ b/solution.py
@@ -103,7 +103,7 @@
 
 
 def picked_probes(own, other, probe_idx, gaps, times, cos_weights, left_panel):
-    cut = left_panel.shape[0] // 8 * 3
+    cut = left_panel.shape[0] // 16 * 7
 
     def kernel(times_ref, cos_ref, *refs):
         bank_refs, (idx_ref, gaps_ref, left_ref, out_ref, weights_ref, first_ref, sem) = refs[:8], refs[8:]

time: 77.4 us -> 77.1 us (level)
  waiting for transfers between devices: 10.8 us -> 9.74 us
  local copies, waits for them, and re-layouts: 0.04 us -> 0.95 us
    all_to_all x1, waiting for transfers between devices: 5.3 us -> 4.3 us  [shards(): lax.all_to_all(after(parts, bank), ('k', 'u', 'z'), 0, 0, tiled=True, axi...]
    unnamed x8 -> x12, local copies, waits for them, and re-layouts: 0.01 us -> 0.93 us
  transfers between devices with their start and end apart: 10 -> 10, of which waited for: 5 -> 5; matrix products, arithmetic and copies ran while one was open for 0% -> 0% of each run, Pallas kernels for 9% -> 10%
where the time goes in v13:
time: 77.1 us; the launch traced here: 76.3 us
  blocking collectives  30 us (39%)
  starting transfers between devices  22.1 us (29%)
  Pallas kernels  12.7 us (16%)
  waiting for transfers between devices  9.74 us (13%)
  local copies, waits for them, and re-layouts  0.95 us (1%)
    all_to_all x1, blocking collectives, shards(): products = lax.all_to_all(products, ('u', 'z'), 0, 0, tiled=True)  18.1 us
    all_to_all x1, blocking collectives, shards(): lax.all_to_all(jnp.broadcast_to(both, (8,) + both.shape), ('f', 'y'), 0,...  11.9 us
    ppermute x4, starting transfers between devices, shards(): other = [lax.ppermute(columns, 'k', swap) for columns in own]  7.89 us
    all_to_all x1, starting transfers between devices, shards(): lax.all_to_all(after(parts, bank), ('k', 'u', 'z'), 0, 0, tiled=True, axi...  6.08 us
    pallas_call x1, Pallas kernels, outgoing_parts(): pl.pallas_call(kernel, out_shape=jax.ShapeDtypeStruct((GROUP, ROWS, LANES...  4.68 us
    ppermute x3, starting transfers between devices, shards(): lax.ppermute(bank, 'y', [(y, (y + n) % 4) for y in range(4)])  4.61 us
    all_to_all x1, waiting for transfers between devices, shards(): lax.all_to_all(after(parts, bank), ('k', 'u', 'z'), 0, 0, tiled=True, axi...  4.3 us
    pallas_call x1, Pallas kernels, screened_response(): pl.pallas_call(kernel, out_shape=jax.ShapeDtypeStruct((2, SET, rows), F32...  3.9 us
  transfers between devices with their start and end apart: 10, of which 5 were waited for; matrix products, arithmetic and copies ran while one was open for 0% of the time, Pallas kernels for 10%

profile of v13, /device:TPU:2, one launch (start us, length us, event | category | flops | bytes accessed | tf_op | source)
XLA Modules:
  0.0 76.3 jit_solution(4301629189043112021)
XLA Ops:
  0.0 3.3 %collective-permute-start = (bf16[512,128]{1,0:T(8,128)(2,1)}, bf16[512,128]{1,0:T(8,128)(2,1)S(1)}, u32[]{:S(2)}, u32[]{:S(2)}) collective-permute-start(bf16[512,128]{1,0:T(8,128)(2,1)} %param.18), channel_id=1, source_target_pairs={{0,6},{1,7},{2,0},{3,1},{4,2},{5,3},{6,4},{7,5},{128,130},{129,131... | collective-permute-start | bytes 393224 | tf_op jit(solution)/shard_map/parts/ppermute | solution.py:229
  3.9 4.7 %outgoing_parts.1.array_ref = bf16[8,528,128]{2,1,0:T(8,128)(2,1)} custom-call(s32[16]{0:T(128)} %bitcast.10, s32[16]{0:T(128)} %pairs_ref.1, s32[1]{0:T(128)S(6)} %copy.13.counts_ref, bf16[16,512,512]{2,1,0:T(8,128)(2,1)} %tiles_ref.1), custom_call_target="tpu_custom_call" | custom-call | tf_op jit(solution)/shard_map/parts/outgoing_parts/pallas_call | solution.py:76
  8.6 0.0 copy-start.2
  8.6 0.0 copy-start.3
  8.6 0.0 copy-start.4
  8.6 0.0 copy-start.5
  8.7 1.9 %collective-permute-done.other_ref.refs_0_ = bf16[512,128]{1,0:T(8,128)(2,1)S(1)} collective-permute-done((bf16[512,128]{1,0:T(8,128)(2,1)}, bf16[512,128]{1,0:T(8,128)(2,1)S(1)}, u32[]{:S(2)}, u32[]{:S(2)}) %collective-permute-start) | collective-permute-done | bytes 131104 | tf_op jit(solution)/shard_map/parts/ppermute | solution.py:229
  10.6 0.0 copy-start
  10.6 6.1 %all-to-all-start = ((bf16[8,528,128]{2,1,0:T(8,128)(2,1)}), bf16[8,528,128]{2,1,0:T(8,128)(2,1)S(1)}, u32[]{:S(2)}, u32[]{:S(2)}) async-start(bf16[8,528,128]{2,1,0:T(8,128)(2,1)} %after.1), calls=%async_computation | async-start | bytes 2162688 | tf_op jit(solution)/shard_map/parts/all_to_all | solution.py:231
  16.7 3.0 %collective-permute-start.3 = (bf16[512,128]{1,0:T(8,128)(2,1)S(1)}, bf16[512,128]{1,0:T(8,128)(2,1)S(1)}, u32[]{:S(2)}, u32[]{:S(2)}) collective-permute-start(bf16[512,128]{1,0:T(8,128)(2,1)S(1)} %collective-permute-done.other_ref.refs_0_), channel_id=1, source_target_pairs={{0,96},{32,0},{64,32},{96,64},{1,97},{33,1},{65,33},{97,65},{2,98}... | collective-permute-start | bytes 393224 | tf_op jit(solution)/shard_map/probes/ppermute | solution.py:233
  19.7 0.6 collective-permute-start.2
  20.3 1.0 %collective-permute-start.1 = (bf16[512,128]{1,0:T(8,128)(2,1)S(1)}, bf16[512,128]{1,0:T(8,128)(2,1)S(1)}, u32[]{:S(2)}, u32[]{:S(2)}) collective-permute-start(bf16[512,128]{1,0:T(8,128)(2,1)S(1)} %collective-permute-done.other_ref.refs_0_), channel_id=1, source_target_pairs={{0,32},{32,64},{64,96},{96,0},{1,33},{33,65},{65,97},{97,1},{2,34}... | collective-permute-start | bytes 393224 | tf_op jit(solution)/shard_map/probes/ppermute | solution.py:233
  21.3 0.0 copy-done
  21.3 1.8 %collective-permute-start.4 = (bf16[512,128]{1,0:T(8,128)(2,1)S(1)}, bf16[512,128]{1,0:T(8,128)(2,1)S(1)}, u32[]{:S(2)}, u32[]{:S(2)}) collective-permute-start(bf16[512,128]{1,0:T(8,128)(2,1)S(1)} %collective-permute-done.other_ref.refs_0_), channel_id=1, source_target_pairs={{0,16},{16,0},{1,17},{17,1},{2,18},{18,2},{3,19},{19,3},{4,20},{20... | collective-permute-start | bytes 393224 | tf_op jit(solution)/shard_map/probes/ppermute | solution.py:234
  23.1 0.0 collective-permute-done.3.refs_3_
  23.1 3.4 %collective-permute-start.7 = (bf16[512,128]{1,0:T(8,128)(2,1)S(1)}, bf16[512,128]{1,0:T(8,128)(2,1)S(1)}, u32[]{:S(2)}, u32[]{:S(2)}) collective-permute-start(bf16[512,128]{1,0:T(8,128)(2,1)S(1)} %collective-permute-done.3.refs_3_), channel_id=1, source_target_pairs={{0,16},{16,0},{1,17},{17,1},{2,18},{18,2},{3,19},{19,3},{4,20},{20... | collective-permute-start | bytes 393224 | tf_op jit(solution)/shard_map/probes/ppermute | solution.py:234
  26.5 0.0 collective-permute-done.2.refs_2_
  26.5 2.6 %collective-permute-start.6 = (bf16[512,128]{1,0:T(8,128)(2,1)S(1)}, bf16[512,128]{1,0:T(8,128)(2,1)S(1)}, u32[]{:S(2)}, u32[]{:S(2)}) collective-permute-start(bf16[512,128]{1,0:T(8,128)(2,1)S(1)} %collective-permute-done.2.refs_2_), channel_id=1, source_target_pairs={{0,16},{16,0},{1,17},{17,1},{2,18},{18,2},{3,19},{19,3},{4,20},{20... | collective-permute-start | bytes 393224 | tf_op jit(solution)/shard_map/probes/ppermute | solution.py:234
  29.1 1.2 %collective-permute-done.1.refs_1_ = bf16[512,128]{1,0:T(8,128)(2,1)S(1)} collective-permute-done((bf16[512,128]{1,0:T(8,128)(2,1)S(1)}, bf16[512,128]{1,0:T(8,128)(2,1)S(1)}, u32[]{:S(2)}, u32[]{:S(2)}) %collective-permute-start.1) | collective-permute-done | bytes 131104 | tf_op jit(solution)/shard_map/probes/ppermute | solution.py:233
  30.3 0.1 collective-permute-start.5
  30.4 0.0 collective-permute-done.4.refs_4_
  30.4 0.0 collective-permute-done.7.refs_7_
  30.4 0.0 collective-permute-done.6.refs_6_
  30.4 1.2 %collective-permute-done.5.refs_5_ = bf16[512,128]{1,0:T(8,128)(2,1)S(1)} collective-permute-done((bf16[512,128]{1,0:T(8,128)(2,1)S(1)}, bf16[512,128]{1,0:T(8,128)(2,1)S(1)}, u32[]{:S(2)}, u32[]{:S(2)}) %collective-permute-start.5) | collective-permute-done | bytes 131104 | tf_op jit(solution)/shard_map/probes/ppermute | solution.py:234
  31.6 0.0 copy-done.2
  31.6 0.0 copy-done.3
  31.6 0.0 copy-done.4
  31.6 0.0 copy-done.5
  31.6 0.0 copy-start.1
  31.7 0.9 %copy-done.1 = bf16[512,128]{1,0:T(8,128)(2,1)S(1)} copy-done((bf16[512,128]{1,0:T(8,128)(2,1)S(1)}, bf16[512,128]{1,0:T(8,128)(2,1)}, u32[]{:S(2)}) %copy-start.1) | copy-done | bytes 131096
  32.6 2.7 %picked_probes.1 = (bf16[512,512]{1,0:T(8,128)(2,1)S(1)}, f32[2,2048]{1,0:T(2,128)S(1)}, bf16[448,2048]{1,0:T(8,128)(2,1)S(1)}) custom-call(f32[4]{0:T(128)S(1)} %copy-done.5, f32[4,4]{1,0:T(4,128)S(1)} %copy-done.3, bf16[512,128]{1,0:T(8,128)(2,1)S(1)} %copy-done.1, bf16[512,128]{1,0:T(8,128)(2,1)S(1)} %collective-permute-done.1.refs_1_, ...), custom_call_target="tpu_custom_call" | custom-call | tf_op jit(solution)/shard_map/probes/picked_probes/pallas_call | solution.py:129
  35.2 4.3 %all-to-all-done.parts_ref = bf16[8,528,128]{2,1,0:T(8,128)(2,1)S(1)} async-done(((bf16[8,528,128]{2,1,0:T(8,128)(2,1)}), bf16[8,528,128]{2,1,0:T(8,128)(2,1)S(1)}, u32[]{:S(2)}, u32[]{:S(2)}) %all-to-all-start) | async-done | bytes 1081376 | tf_op jit(solution)/shard_map/parts/all_to_all | solution.py:231
  39.6 1.5 %owner_products.1 = bf16[16,32,256]{2,1,0:T(8,128)(2,1)S(1)} custom-call(bf16[8,528,128]{2,1,0:T(8,128)(2,1)S(1)} %all-to-all-done.parts_ref, bf16[512,512]{1,0:T(8,128)(2,1)S(1)} %get-tuple-element.8.probes_ref), custom_call_target="tpu_custom_call" | custom-call | tf_op jit(solution)/shard_map/products/owner_products/pallas_call | solution.py:162
  41.0 18.1 %all_to_all.15 = bf16[16,32,256]{2,1,0:T(8,128)(2,1)S(1)} all-to-all(bf16[16,32,256]{2,1,0:T(8,128)(2,1)S(1)} %owner_products.1), channel_id=1, replica_groups=mesh['f'=2,'y'=4,'k'=2,'u'=2,'z'=8] {'u','z'}, dimensions={0} | all-to-all | bytes 524288 | tf_op jit(solution)/shard_map/products/all_to_all | solution.py:240
  59.2 0.2 collective-permute-start.8
  59.4 1.1 %collective-permute-done.8 = bf16[32,256]{1,0:T(8,128)(2,1)S(1)} collective-permute-done((bf16[32,256]{1,0:T(8,128)(2,1)S(1)}, bf16[32,256]{1,0:T(8,128)(2,1)S(1)}, u32[]{:S(2)}, u32[]{:S(2)}) %collective-permute-start.8) | collective-permute-done | bytes 16416 | tf_op jit(solution)/shard_map/spread/ppermute | solution.py:243
  60.5 11.9 %all_to_all.16.parts_ref = bf16[8,2,32,256]{3,2,1,0:T(8,128)(2,1)S(1)} all-to-all(bf16[8,2,32,256]{3,2,1,0:T(8,128)(2,1)S(1)} %broadcast_in_dim.3), channel_id=1, replica_groups=mesh['f'=2,'y'=4,'k'=2,'u'=2,'z'=8] {'f','y'}, dimensions={0} | all-to-all | bytes 524288 | tf_op jit(solution)/shard_map/spread/all_to_all | solution.py:244
  72.4 3.9 %screened_response.1 = f32[2,32,1024]{2,1,0:T(8,128)} custom-call(bf16[8,2,32,256]{3,2,1,0:T(8,128)(2,1)S(1)} %all_to_all.16.parts_ref, bf16[448,2048]{1,0:T(8,128)(2,1)S(1)} %get-tuple-element.9.first_ref, bf16[1024,2048]{1,0:T(8,128)(2,1)} %left_ref.1, f32[2,2048]{1,0:T(2,128)S(1)} %get-tuple-element.10.weights_ref), custom_call_target="tpu_custom_call" | custom-call | tf_op jit(solution)/shard_map/response/screened_response/pallas_call | solution.py:206
  (4 shorter events, 0.1 us)
Async XLA Ops:
  0.0 10.6 %collective-permute-start = (bf16[512,128]{1,0:T(8,128)(2,1)}, bf16[512,128]{1,0:T(8,128)(2,1)S(1)}, u32[]{:S(2)}, u32[]{:S(2)}) collective-permute-start(bf16[512,128]{1,0:T(8,128)(2,1)} %param.18), channel_id=1, source_target_pairs={{0,6},{1,7},{2,0},{3,1},{4,2},{5,3},{6,4},{7,5},{128,130},{129,131... | collective-permute-start | bytes 393224 | tf_op jit(solution)/shard_map/parts/ppermute | solution.py:229
  8.6 23.0 %copy-start.2 = (f32[2048]{0:T(1024)S(1)}, f32[2048]{0:T(1024)}, u32[]{:S(2)}) copy-start(f32[2048]{0:T(1024)} %param.15) | copy-start | bytes 24580
  8.6 23.0 %copy-start.3 = (f32[4,4]{1,0:T(4,128)S(1)}, f32[4,4]{1,0:T(4,128)}, u32[]{:S(2)}) copy-start(f32[4,4]{1,0:T(4,128)} %cos_ref.1) | copy-start | bytes 196
  8.6 23.0 %copy-start.4 = (s32[512]{0:T(512)S(1)}, s32[512]{0:T(512)}, u32[]{:S(2)}) copy-start(s32[512]{0:T(512)} %param.19) | copy-start | bytes 6148
  8.6 23.0 %copy-start.5 = (f32[4]{0:T(128)S(1)}, f32[4]{0:T(128)}, u32[]{:S(2)}) copy-start(f32[4]{0:T(128)} %times_ref.1) | copy-start | bytes 52
  10.6 10.7 %copy-start = (bf16[512,128]{1,0:T(8,128)(2,1)}, bf16[512,128]{1,0:T(8,128)(2,1)S(1)}, u32[]{:S(2)}) copy-start(bf16[512,128]{1,0:T(8,128)(2,1)S(1)} %collective-permute-done.other_ref.refs_0_) | copy-start | bytes 393220
  10.6 29.0 %all-to-all-start = ((bf16[8,528,128]{2,1,0:T(8,128)(2,1)}), bf16[8,528,128]{2,1,0:T(8,128)(2,1)S(1)}, u32[]{:S(2)}, u32[]{:S(2)}) async-start(bf16[8,528,128]{2,1,0:T(8,128)(2,1)} %after.1), calls=%async_computation | async-start | bytes 2162688 | tf_op jit(solution)/shard_map/parts/all_to_all | solution.py:231
  16.7 6.4 %collective-permute-start.3 = (bf16[512,128]{1,0:T(8,128)(2,1)S(1)}, bf16[512,128]{1,0:T(8,128)(2,1)S(1)}, u32[]{:S(2)}, u32[]{:S(2)}) collective-permute-start(bf16[512,128]{1,0:T(8,128)(2,1)S(1)} %collective-permute-done.other_ref.refs_0_), channel_id=1, source_target_pairs={{0,96},{32,0},{64,32},{96,64},{1,97},{33,1},{65,33},{97,65},{2,98}... | collective-permute-start | bytes 393224 | tf_op jit(solution)/shard_map/probes/ppermute | solution.py:233
  19.7 6.8 %collective-permute-start.2 = (bf16[512,128]{1,0:T(8,128)(2,1)S(1)}, bf16[512,128]{1,0:T(8,128)(2,1)S(1)}, u32[]{:S(2)}, u32[]{:S(2)}) collective-permute-start(bf16[512,128]{1,0:T(8,128)(2,1)S(1)} %collective-permute-done.other_ref.refs_0_), channel_id=1, source_target_pairs={{0,64},{32,96},{64,0},{96,32},{1,65},{33,97},{65,1},{97,33},{2,66}... | collective-permute-start | bytes 393224 | tf_op jit(solution)/shard_map/probes/ppermute | solution.py:233
  20.3 10.0 %collective-permute-start.1 = (bf16[512,128]{1,0:T(8,128)(2,1)S(1)}, bf16[512,128]{1,0:T(8,128)(2,1)S(1)}, u32[]{:S(2)}, u32[]{:S(2)}) collective-permute-start(bf16[512,128]{1,0:T(8,128)(2,1)S(1)} %collective-permute-done.other_ref.refs_0_), channel_id=1, source_target_pairs={{0,32},{32,64},{64,96},{96,0},{1,33},{33,65},{65,97},{97,1},{2,34}... | collective-permute-start | bytes 393224 | tf_op jit(solution)/shard_map/probes/ppermute | solution.py:233
  21.3 9.1 %collective-permute-start.4 = (bf16[512,128]{1,0:T(8,128)(2,1)S(1)}, bf16[512,128]{1,0:T(8,128)(2,1)S(1)}, u32[]{:S(2)}, u32[]{:S(2)}) collective-permute-start(bf16[512,128]{1,0:T(8,128)(2,1)S(1)} %collective-permute-done.other_ref.refs_0_), channel_id=1, source_target_pairs={{0,16},{16,0},{1,17},{17,1},{2,18},{18,2},{3,19},{19,3},{4,20},{20... | collective-permute-start | bytes 393224 | tf_op jit(solution)/shard_map/probes/ppermute | solution.py:234
  23.1 7.3 %collective-permute-start.7 = (bf16[512,128]{1,0:T(8,128)(2,1)S(1)}, bf16[512,128]{1,0:T(8,128)(2,1)S(1)}, u32[]{:S(2)}, u32[]{:S(2)}) collective-permute-start(bf16[512,128]{1,0:T(8,128)(2,1)S(1)} %collective-permute-done.3.refs_3_), channel_id=1, source_target_pairs={{0,16},{16,0},{1,17},{17,1},{2,18},{18,2},{3,19},{19,3},{4,20},{20... | collective-permute-start | bytes 393224 | tf_op jit(solution)/shard_map/probes/ppermute | solution.py:234
  26.5 3.9 %collective-permute-start.6 = (bf16[512,128]{1,0:T(8,128)(2,1)S(1)}, bf16[512,128]{1,0:T(8,128)(2,1)S(1)}, u32[]{:S(2)}, u32[]{:S(2)}) collective-permute-start(bf16[512,128]{1,0:T(8,128)(2,1)S(1)} %collective-permute-done.2.refs_2_), channel_id=1, source_target_pairs={{0,16},{16,0},{1,17},{17,1},{2,18},{18,2},{3,19},{19,3},{4,20},{20... | collective-permute-start | bytes 393224 | tf_op jit(solution)/shard_map/probes/ppermute | solution.py:234
  30.3 1.3 %collective-permute-start.5 = (bf16[512,128]{1,0:T(8,128)(2,1)S(1)}, bf16[512,128]{1,0:T(8,128)(2,1)S(1)}, u32[]{:S(2)}, u32[]{:S(2)}) collective-permute-start(bf16[512,128]{1,0:T(8,128)(2,1)S(1)} %collective-permute-done.1.refs_1_), channel_id=1, source_target_pairs={{0,16},{16,0},{1,17},{17,1},{2,18},{18,2},{3,19},{19,3},{4,20},{20... | collective-permute-start | bytes 393224 | tf_op jit(solution)/shard_map/probes/ppermute | solution.py:234
  31.6 0.9 %copy-start.1 = (bf16[512,128]{1,0:T(8,128)(2,1)S(1)}, bf16[512,128]{1,0:T(8,128)(2,1)}, u32[]{:S(2)}) copy-start(bf16[512,128]{1,0:T(8,128)(2,1)} %copy-done) | copy-start | bytes 393220
  59.2 1.3 %collective-permute-start.8 = (bf16[32,256]{1,0:T(8,128)(2,1)S(1)}, bf16[32,256]{1,0:T(8,128)(2,1)S(1)}, u32[]{:S(2)}, u32[]{:S(2)}) collective-permute-start(bf16[32,256]{1,0:T(8,128)(2,1)S(1)} %reduce_sum.12), channel_id=1, source_target_pairs={{0,16},{16,0},{1,17},{17,1},{2,18},{18,2},{3,19},{19,3},{4,20},{20... | collective-permute-start | bytes 49160 | tf_op jit(solution)/shard_map/spread/ppermute | solution.py:243
